TPU v7x, 256 devices: a whole 4x4x8 slice. The times are simulated.
256 devices in a mesh: head: 8 (over z_hi, core), blk: 32 (over z_lo, x, y).
Axes of the slice: x: 4, y: 4, z: 8 (z_hi: 4, z_lo: 2; z = z_hi * 2 + z_lo), core: 2. Of those that a mesh axis runs over, the one named last changes fastest.
Arguments:
- queries: bfloat16 [32, 512, 2048], P('blk', 'head'), may hold values from -10 to 10
- keys: bfloat16 [32, 512, 512], P('blk', 'head'), may hold values from -10 to 10
- values: bfloat16 [32, 512, 512], P('blk', 'head'), may hold values from -6 to 6
- position: int32 [32, 512], replicated, may hold values from 0 to 16383, as said below
- segment: int32 [32, 512], replicated, may hold values from 0 to 3, as said below
Outputs:
- attended: bfloat16 [32, 512, 2048], P('blk', 'head')
Inputs may be any that keep to these rules, and one draw needn't show every extreme that they name: Each row b holds two runs of 256 consecutive positions in rising order, first c * 256 onward, then (63 - c) * 256 onward, with c a permutation of the rows; every position appears once. `segment`: documents are runs of consecutive positions; their numbers rise with position, start at 0 and may skip values.
All inputs are finite; a program needn't handle non-finite values.
Results may differ from a plain program's by a relative error of at most 0.007.
Values may be sent and summed in bfloat16 or wider, within the bound.
No kernel may reach another device: no remote copies, remote signals or barrier semaphores. Data moves between devices by JAX's collectives and lax.ppermute only.
A program may use at most 128 MiB of HBM per device.

v0:
```python
import functools

import jax
import jax.numpy as jnp
import numpy as np
from jax import lax
from jax.experimental import pallas as pl
from jax.experimental.pallas import tpu as pltpu
from jax.sharding import PartitionSpec as P

HEADS = 16
KV = 4
D = 128
AXES = ("head", "blk")
NEVER = 1 << 20
MASKED = -1e30
LOG2E_SCALE = float(np.log2(np.e) * D**-0.5)
VMEM_LIMIT = 40 * 1024 * 1024
SMALL_LIMIT = 8 * 1024 * 1024


def device_of(zl, x, y, zh, c):
    return ((zh % 4) * 2 + c % 2) * 32 + (zl % 2) * 16 + (x % 4) * 4 + y % 4


def place_of(device):
    h, b = device // 32, device % 32
    return b // 16, (b // 4) % 4, b % 4, h // 2, h % 2


def send(a, to):
    pairs = [(i, device_of(*to(*place_of(i)))) for i in range(256)]
    return lax.ppermute(a, AXES, pairs)


def along(first, step):
    def to(zl, x, y, zh, c):
        on_x = (c == 0) == first
        return (zl, x + step, y, zh, c) if on_x else (zl, x, y + step, zh, c)

    return to


def key_orders():
    table = np.zeros((256, 32), np.int32)
    for i in range(256):
        zl, x, y, zh, c = place_of(i)
        k = 0
        for s2 in (0, -1, 1, 2):
            for s1 in (0, -1, 1, 2):
                for f in (0, 1):
                    on_x, on_y = (s1, s2) if c == 0 else (s2, s1)
                    table[i, k] = ((zl + f) % 2) * 16 + ((x + on_x) % 4) * 4 + (y + on_y) % 4
                    k += 1
    return table


ORDERS = key_orders()


def pack_kernel(zh_ref, *refs):
    ins, outs = refs[:-4], refs[-4:]
    for s, out in enumerate(outs):
        head = lax.rem(zh_ref[0] + s, 4)
        at = 0
        for a in ins:
            width = a.shape[1] // 4
            cols = pl.ds(pl.multiple_of(head * width, width), width)
            out[:, pl.ds(at, width)] = a[:, cols]
            at += width


def pack(zh, *arrays):
    width = sum(a.shape[1] for a in arrays) // 4
    vmem = pl.BlockSpec(memory_space=pltpu.VMEM)
    return pl.pallas_call(
        pack_kernel,
        out_shape=[jax.ShapeDtypeStruct((64, width), jnp.bfloat16)] * 4,
        in_specs=[pl.BlockSpec(memory_space=pltpu.SMEM)] + [vmem] * len(arrays),
        out_specs=[vmem] * 4,
        compiler_params=pltpu.CompilerParams(vmem_limit_bytes=SMALL_LIMIT),
        name="pack",
    )(zh, *arrays)


def unpack_kernel(by_rows, zh_ref, *refs):
    out = refs[-1]
    for s in range(4):
        z = lax.rem(zh_ref[0] + 4 - s, 4)
        a = refs[s]
        if by_rows:
            out[pl.ds(pl.multiple_of(z * 64, 64), 64), :] = a[...]
        else:
            out[:, pl.ds(pl.multiple_of(z * 512, 512), 512)] = a[...]


def unpack(zh, arrays, by_rows):
    width = arrays[0].shape[1]
    shape = (256, width) if by_rows else (64, 4 * width)
    vmem = pl.BlockSpec(memory_space=pltpu.VMEM)
    return pl.pallas_call(
        functools.partial(unpack_kernel, by_rows),
        out_shape=jax.ShapeDtypeStruct(shape, jnp.bfloat16),
        in_specs=[pl.BlockSpec(memory_space=pltpu.SMEM)] + [vmem] * 4,
        out_specs=vmem,
        compiler_params=pltpu.CompilerParams(vmem_limit_bytes=SMALL_LIMIT),
        name="unpack",
    )(zh, *arrays)


def over_z(arrays):
    return [arrays[0]] + [
        send(arrays[s], lambda zl, x, y, z, c, s=s: (zl, x, y, z + s, c)) for s in (1, 2, 3)
    ]


PLAN = 72
Q_AT = 6 * PLAN
CHUNKS = ((0, 8), (8, 16), (24, 8))


def doc_start(meta, at):
    start = jnp.zeros_like(at)
    for s in range(3):
        edge = meta[Q_AT + 3 + s]
        start = jnp.maximum(start, jnp.where(edge <= at, edge, 0))
    return start


def plan_kernel(pos_ref, seg_ref, base_ref, order_ref, ids_ref, plan):
    pos, seg = pos_ref[...], seg_ref[...]
    for s in range(1, 4):
        plan[Q_AT + 2 + s] = jnp.min(jnp.where(seg >= s, pos, NEVER))
    plan[Q_AT + 2] = ids_ref[0]
    for hf in range(2):
        qb = base_ref[ids_ref[1] * 2 + hf]
        plan[Q_AT + hf] = qb
        lo_first, lo_last = doc_start(plan, qb), doc_start(plan, qb + 255)
        for chunk, (first, blocks) in enumerate(CHUNKS):
            off = (chunk * 2 + hf) * PLAN

            def classify(i, counts):
                n_full, n_part = counts
                source = order_ref[first + i]
                for t in range(2):
                    kb = base_ref[source * 2 + t]
                    seen = (kb <= qb) & (kb + 255 >= lo_first)
                    whole = seen & (kb < qb) & (kb >= lo_last)
                    entry = (i * 2 + t) + kb * 256
                    plan[off + 2 + n_full] = entry
                    plan[off + 36 + n_part] = entry
                    n_full = n_full + jnp.where(whole, 1, 0)
                    n_part = n_part + jnp.where(seen & jnp.logical_not(whole), 1, 0)
                return n_full, n_part

            n_full, n_part = lax.fori_loop(0, blocks, classify, (jnp.int32(0), jnp.int32(0)))
            odd = n_full % 2
            last = plan[off + 2 + jnp.maximum(n_full - 1, 0)]
            plan[off + 36 + n_part] = jnp.where(odd == 1, last, plan[off + 36 + n_part])
            plan[off] = n_full
            plan[off + 1] = n_part + odd


def make_plan(position, segment, bases, order, ids):
    smem, vmem = (pl.BlockSpec(memory_space=m) for m in (pltpu.SMEM, pltpu.VMEM))
    return pl.pallas_call(
        plan_kernel,
        out_shape=jax.ShapeDtypeStruct((Q_AT + 8,), jnp.int32),
        in_specs=[vmem, vmem, smem, smem, smem],
        out_specs=smem,
        compiler_params=pltpu.CompilerParams(vmem_limit_bytes=SMALL_LIMIT),
        name="plan",
    )(position, segment, bases, order, ids)


def flash_kernel(pieces, chunk, carry, final, *refs):
    meta = refs[0]
    q_own, q_oth = refs[1], refs[2]
    piece_refs = refs[3 : 3 + len(pieces)]
    rest = list(refs[3 + len(pieces) :])
    if carry:
        acc_in, ml_in = rest.pop(0), rest.pop(0)
    out_a, out_b = rest.pop(0), rest.pop(0)
    kv, kt, q_s, acc, m_s, l_s, sems = rest
    core = meta[Q_AT + 2]
    tiles = sum(pieces) // 128

    at = 0
    copies = []
    for i, rows in enumerate(pieces):
        copy = pltpu.make_async_copy(piece_refs[i], kv.at[pl.ds(at, rows), :], sems.at[i])
        copy.start()
        copies.append(copy)
        at += rows

    for hf in range(2):
        for h in range(4):
            rows, cols = pl.ds(hf * 128, 128), pl.ds(h * 128, 128)
            q_s[hf * 4 + h, pl.ds(0, 128), :] = q_own[rows, cols]
            q_s[hf * 4 + h, pl.ds(128, 128), :] = q_oth[rows, cols]
            if carry:
                acc[hf * 4 + h] = acc_in[hf * 4 + h]
                m_s[hf * 4 + h] = jnp.broadcast_to(ml_in[hf, :, h : h + 1], (256, 128))
                lane = lax.broadcasted_iota(jnp.int32, (256, 128), 1)
                l_s[hf * 4 + h] = jnp.where(lane == 0, ml_in[hf, :, 4 + h : 5 + h], 0.0)
            else:
                acc[hf * 4 + h] = jnp.zeros((256, 128), jnp.float32)
                m_s[hf * 4 + h] = jnp.full((256, 128), MASKED, jnp.float32)
                l_s[hf * 4 + h] = jnp.zeros((256, 128), jnp.float32)

    for copy in copies:
        copy.wait()
    for t in range(tiles):
        kt[t] = kv[pl.ds(t * 128, 128), pl.ds(0, D)].T

    row = lax.broadcasted_iota(jnp.int32, (256, 128), 0)
    lane = lax.broadcasted_iota(jnp.int32, (256, 128), 1)
    own_row = row < 128
    in_half = jnp.where(own_row, row, row - 128)
    q_core = jnp.where(own_row, core, 1 - core)
    q_off = jnp.where(in_half >= 64, in_half + 64, in_half) + q_core * 64
    k_off = jnp.where(lane >= 64, lane + 64, lane) + core * 64

    def step(hf, tile_a, tile_b, masks):
        k_a = kv[pl.ds(pl.multiple_of(tile_a * 128, 128), 128), :]
        k_b = kv[pl.ds(pl.multiple_of(tile_b * 128, 128), 128), :]
        k = jnp.concatenate([kt[tile_a], kt[tile_b]], 1)
        v = jnp.concatenate([k_a[:, D:], k_b[:, D:]], 0)
        ss = [
            lax.dot_general(
                q_s[hf * 4 + h], k, (((1,), (0,)), ((), ())), preferred_element_type=jnp.float32
            )
            for h in range(4)
        ]
        ps, fades = [], []
        for h in range(4):
            i = hf * 4 + h
            s_a, s_b = ss[h][:, :128], ss[h][:, 128:]
            if masks is not None:
                s_a = jnp.where(masks[0], s_a, MASKED)
                s_b = jnp.where(masks[1], s_b, MASKED)
            old = m_s[i]
            new = jnp.maximum(old, jnp.max(jnp.maximum(s_a, s_b), axis=1, keepdims=True))
            m_s[i] = new
            p_a = jnp.exp2((s_a - new) * LOG2E_SCALE)
            p_b = jnp.exp2((s_b - new) * LOG2E_SCALE)
            fades.append(jnp.exp2((old - new) * LOG2E_SCALE))
            l_s[i] = l_s[i] * fades[-1] + p_a + p_b
            ps.append(jnp.concatenate([p_a.astype(jnp.bfloat16), p_b.astype(jnp.bfloat16)], 1))
        for h in range(4):
            i = hf * 4 + h
            acc[i] = acc[i] * fades[h] + jnp.dot(ps[h], v, preferred_element_type=jnp.float32)

    def quad(hf, tiles4):
        kk = [kv[pl.ds(pl.multiple_of(t * 128, 128), 128), :] for t in tiles4]
        k = jnp.concatenate([kt[t] for t in tiles4], 1)
        v = jnp.concatenate([a[:, D:] for a in kk], 0)
        ss = [
            lax.dot_general(
                q_s[hf * 4 + h], k, (((1,), (0,)), ((), ())), preferred_element_type=jnp.float32
            )
            for h in range(4)
        ]
        ps, fades = [], []
        for h in range(4):
            i = hf * 4 + h
            st = [ss[h][:, t * 128 : t * 128 + 128] for t in range(4)]
            top = jnp.maximum(jnp.maximum(st[0], st[1]), jnp.maximum(st[2], st[3]))
            old = m_s[i]
            new = jnp.maximum(old, jnp.max(top, axis=1, keepdims=True))
            m_s[i] = new
            p = [jnp.exp2((a - new) * LOG2E_SCALE) for a in st]
            fades.append(jnp.exp2((old - new) * LOG2E_SCALE))
            l_s[i] = l_s[i] * fades[-1] + (p[0] + p[1]) + (p[2] + p[3])
            ps.append(jnp.concatenate([a.astype(jnp.bfloat16) for a in p], 1))
        for h in range(4):
            i = hf * 4 + h
            acc[i] = acc[i] * fades[h] + jnp.dot(ps[h], v, preferred_element_type=jnp.float32)

    for hf in range(2):
        qb = meta[Q_AT + hf]
        off = (chunk * 2 + hf) * PLAN
        n_full, n_part = meta[off], meta[off + 1]

        def whole(j):
            return meta[off + 2 + j] & 255

        def whole_quad(j, _):
            quad(hf, [whole(4 * j + t) for t in range(4)])
            return 0

        lax.fori_loop(0, n_full // 4, whole_quad, 0)

        def whole_pair(j, _):
            step(hf, whole(2 * j), whole(2 * j + 1), None)
            return 0

        lax.fori_loop(n_full // 4 * 2, n_full // 2, whole_pair, 0)

        q_pos = qb + q_off
        q_lo = doc_start(meta, q_pos)

        def part_pair(j, _):
            there = 2 * j + 1 < n_part
            e_a = meta[off + 36 + 2 * j]
            e_b = jnp.where(there, meta[off + 37 + 2 * j], e_a)
            tile_a, tile_b = e_a & 255, e_b & 255
            k_a = (e_a >> 8) + k_off
            k_b = jnp.where(there, e_b >> 8, NEVER) + k_off
            masks = ((k_a <= q_pos) & (k_a >= q_lo), (k_b <= q_pos) & (k_b >= q_lo))
            step(hf, tile_a, tile_b, masks)
            return 0

        lax.fori_loop(0, (n_part + 1) // 2, part_pair, 0)

        stats = jnp.zeros((256, 128), jnp.float32)
        for h in range(4):
            total = jnp.sum(l_s[hf * 4 + h], axis=1, keepdims=True)
            stats = jnp.where(lane == h, m_s[hf * 4 + h], stats)
            stats = jnp.where(lane == 4 + h, total, stats)
            if final:
                a = acc[hf * 4 + h]
                out_a[pl.ds(hf * 128, 128), pl.ds(h * 128, 128)] = a[:128]
                out_b[pl.ds(hf * 128, 128), pl.ds(h * 128, 128)] = a[128:]
            else:
                out_a[hf * 4 + h] = acc[hf * 4 + h]
        if final:
            out_a[pl.ds(hf * 128, 128), pl.ds(512, 128)] = stats[:128]
            out_b[pl.ds(hf * 128, 128), pl.ds(512, 128)] = stats[128:]
        else:
            out_b[hf] = stats


def flash(meta, q_own, q_oth, pieces, chunk, state, final):
    rows = tuple(p.shape[0] for p in pieces)
    carry = state is not None
    keys = sum(rows)
    if final:
        shapes = [jax.ShapeDtypeStruct((256, 640), jnp.float32)] * 2
    else:
        shapes = [
            jax.ShapeDtypeStruct((8, 256, 128), jnp.float32),
            jax.ShapeDtypeStruct((2, 256, 128), jnp.float32),
        ]
    vmem = pl.BlockSpec(memory_space=pltpu.VMEM)
    in_specs = [pl.BlockSpec(memory_space=pltpu.SMEM), vmem, vmem]
    in_specs += [pl.BlockSpec(memory_space=pl.ANY)] * len(pieces)
    in_specs += [vmem] * (2 if carry else 0)
    return pl.pallas_call(
        functools.partial(flash_kernel, rows, chunk, carry, final),
        out_shape=shapes,
        in_specs=in_specs,
        out_specs=[vmem, vmem],
        scratch_shapes=[
            pltpu.VMEM((keys, 256), jnp.bfloat16),
            pltpu.VMEM((keys // 128, 128, 128), jnp.bfloat16),
            pltpu.VMEM((8, 256, 128), jnp.bfloat16),
            pltpu.VMEM((8, 256, 128), jnp.float32),
            pltpu.VMEM((8, 256, 128), jnp.float32),
            pltpu.VMEM((8, 256, 128), jnp.float32),
            pltpu.SemaphoreType.DMA((len(pieces),)),
        ],
        compiler_params=pltpu.CompilerParams(vmem_limit_bytes=VMEM_LIMIT),
        cost_estimate=pl.CostEstimate(
            flops=2048 * keys * D * 24, bytes_accessed=keys * 512, transcendentals=1024 * keys
        ),
        name="flash",
    )(meta, q_own, q_oth, *pieces, *(state if carry else ()))


def merge_kernel(zh_ref, a_ref, b_ref, *outs):
    for s, out in enumerate(outs):
        z = lax.rem(zh_ref[0] + s, 4)
        rows = pl.ds(pl.multiple_of(z * 64, 64), 64)
        sa, sb = a_ref[rows, pl.ds(512, 128)], b_ref[rows, pl.ds(512, 128)]
        top = jnp.maximum(sa, sb)
        wa = jnp.exp2((sa - top) * LOG2E_SCALE)
        wb = jnp.exp2((sb - top) * LOG2E_SCALE)
        total = sa[:, 4:8] * wa[:, 0:4] + sb[:, 4:8] * wb[:, 0:4]
        wa, wb = wa[:, 0:4] / total, wb[:, 0:4] / total
        for h in range(4):
            cols = pl.ds(h * 128, 128)
            mixed = a_ref[rows, cols] * wa[:, h : h + 1] + b_ref[rows, cols] * wb[:, h : h + 1]
            out[:, cols] = mixed.astype(jnp.bfloat16)


def merge(zh, a, b):
    vmem = pl.BlockSpec(memory_space=pltpu.VMEM)
    return pl.pallas_call(
        merge_kernel,
        out_shape=[jax.ShapeDtypeStruct((64, 512), jnp.bfloat16)] * 4,
        in_specs=[pl.BlockSpec(memory_space=pltpu.SMEM), vmem, vmem],
        out_specs=[vmem] * 4,
        compiler_params=pltpu.CompilerParams(vmem_limit_bytes=SMALL_LIMIT),
        name="merge",
    )(zh, a, b)


def other_core(zl, x, y, zh, c):
    return (zl, x, y, zh, c + 1)


def other_lo(zl, x, y, zh, c):
    return (zl + 1, x, y, zh, c)


def after(first, *then):
    return lax.optimization_barrier((first, *then))[1:]


def local(queries, keys, values, position, segment):
    head, blk = lax.axis_index("head"), lax.axis_index("blk")
    zh, core = head // 2, head % 2
    zh = zh.astype(jnp.int32).reshape(1)

    with jax.named_scope("kv_heads"):
        kv = unpack(zh, over_z(pack(zh, keys.reshape(64, 512), values.reshape(64, 512))), True)
    with jax.named_scope("kv_z"):
        own = jnp.concatenate([kv, send(kv, other_lo)], 0)
    with jax.named_scope("kv_first"):
        line = [own, send(own, along(True, 1)), send(own, along(True, -1)), send(own, along(True, 2))]
        line = jnp.concatenate(line, 0)
    with jax.named_scope("q_heads"):
        queries, position, segment = after(own, queries, position, segment)
        q_own = unpack(zh, over_z(pack(zh, queries.reshape(64, 2048))), True)
        q_oth = send(q_own, other_core)
    with jax.named_scope("plan"):
        position, segment = after(line, position, segment)
        bases = position.reshape(32, 2, 256)[:, :, 0].reshape(64)
        order = lax.dynamic_slice(jnp.asarray(ORDERS), (head * 32 + blk, 0), (1, 32)).reshape(32)
        ids = jnp.stack([core, blk]).astype(jnp.int32)
        plan = make_plan(position, segment, bases, order, ids)
    with jax.named_scope("kv_second"):
        up, down = send(line, along(False, 1)), send(line, along(False, -1))
        half_a, half_b = send(up[:1024], along(False, 1)), send(down[1024:], along(False, -1))
    with jax.named_scope("attend"):
        state = flash(plan, q_own, q_oth, [line], 0, None, False)
        state = flash(plan, q_own, q_oth, [up, down], 1, state, False)
        mine, theirs = flash(plan, q_own, q_oth, [half_a, half_b], 2, state, True)
    with jax.named_scope("merge"):
        parts = merge(zh, mine, send(theirs, other_core))
    with jax.named_scope("out_heads"):
        out = unpack(zh, over_z(parts), False)
    return out.reshape(1, 64, HEADS * D)


def solution(mesh):
    spec = P("blk", "head", None)
    return jax.shard_map(
        local,
        mesh=mesh,
        in_specs=(spec, spec, spec, P(), P()),
        out_specs=spec,
        check_vma=False,
    )
```

profile of v0, /device:TPU:24, one launch (start us, length us, event | category | flops | bytes accessed | tf_op | source)
XLA Modules:
  0.0 87.3 jit_solution(15286274819765129256)
XLA Ops:
  0.0 0.8 copy-done.2
  0.8 0.8 copy-done.3
  1.7 3.3 %collective-permute-start = (bf16[64,256]{1,0:T(8,128)(2,1)S(1)}, bf16[64,256]{1,0:T(8,128)(2,1)S(1)}, u32[]{:S(2)}, u32[]{:S(2)}) collective-permute-start(bf16[64,256]{1,0:T(8,128)(2,1)S(1)} %get-tuple-element.29), channel_id=1, source_target_pairs={{0,64},{1,65},{2,66},{3,67},{4,68},{5,69},{6,70},{7,71},{8,72},{9,... | collective-permute-start | bytes 98312 | tf_op jit(solution)/shard_map/kv_heads/ppermute | solution.py:33
  5.1 5.4 %collective-permute-start.1 = (bf16[64,256]{1,0:T(8,128)(2,1)S(1)}, bf16[64,256]{1,0:T(8,128)(2,1)S(1)}, u32[]{:S(2)}, u32[]{:S(2)}) collective-permute-start(bf16[64,256]{1,0:T(8,128)(2,1)S(1)} %get-tuple-element.30), channel_id=1, source_target_pairs={{0,128},{1,129},{2,130},{3,131},{4,132},{5,133},{6,134},{7,135},{8... | collective-permute-start | bytes 98312 | tf_op jit(solution)/shard_map/kv_heads/ppermute | solution.py:33
  10.5 2.7 %collective-permute-start.2 = (bf16[64,256]{1,0:T(8,128)(2,1)S(1)}, bf16[64,256]{1,0:T(8,128)(2,1)S(1)}, u32[]{:S(2)}, u32[]{:S(2)}) collective-permute-start(bf16[64,256]{1,0:T(8,128)(2,1)S(1)} %get-tuple-element.31), channel_id=1, source_target_pairs={{0,192},{1,193},{2,194},{3,195},{4,196},{5,197},{6,198},{7,199},{8... | collective-permute-start | bytes 98312 | tf_op jit(solution)/shard_map/kv_heads/ppermute | solution.py:33
  13.1 0.0 collective-permute-done.refs_1_
  13.1 0.1 collective-permute-done.1.refs_2_
  13.2 2.1 %collective-permute-done.2.refs_3_ = bf16[64,256]{1,0:T(8,128)(2,1)S(1)} collective-permute-done((bf16[64,256]{1,0:T(8,128)(2,1)S(1)}, bf16[64,256]{1,0:T(8,128)(2,1)S(1)}, u32[]{:S(2)}, u32[]{:S(2)}) %collective-permute-start.2) | collective-permute-done | bytes 32800 | tf_op jit(solution)/shard_map/kv_heads/ppermute | solution.py:33
  15.3 1.1 %collective-permute-start.3 = (bf16[256,256]{1,0:T(8,128)(2,1)S(1)}, bf16[256,256]{1,0:T(8,128)(2,1)S(1)}, u32[]{:S(2)}, u32[]{:S(2)}) collective-permute-start(bf16[256,256]{1,0:T(8,128)(2,1)S(1)} %unpack.3), channel_id=1, source_target_pairs={{0,16},{1,17},{2,18},{3,19},{4,20},{5,21},{6,22},{7,23},{8,24},{9,... | collective-permute-start | bytes 393224 | tf_op jit(solution)/shard_map/kv_z/ppermute | solution.py:33
  16.4 0.1 pad_add_fusion.ids_ref
  16.5 3.9 %collective-permute-done.3 = bf16[256,256]{1,0:T(8,128)(2,1)S(1)} collective-permute-done((bf16[256,256]{1,0:T(8,128)(2,1)S(1)}, bf16[256,256]{1,0:T(8,128)(2,1)S(1)}, u32[]{:S(2)}, u32[]{:S(2)}) %collective-permute-start.3) | collective-permute-done | bytes 131104 | tf_op jit(solution)/shard_map/kv_z/ppermute | solution.py:33
  20.4 1.6 %collective-permute-start.4 = (bf16[512,256]{1,0:T(8,128)(2,1)S(1)}, bf16[512,256]{1,0:T(8,128)(2,1)S(1)}, u32[]{:S(2)}, u32[]{:S(2)}) collective-permute-start(bf16[512,256]{1,0:T(8,128)(2,1)S(1)} %pad_maximum_fusion), channel_id=1, source_target_pairs={{0,4},{1,5},{2,6},{3,7},{4,8},{5,9},{6,10},{7,11},{8,12},{9,13},{1... | collective-permute-start | bytes 786440 | tf_op jit(solution)/shard_map/kv_first/ppermute | solution.py:33
  21.9 0.7 dynamic-slice_bitcast_fusion.order_ref
  22.6 1.7 %collective-permute-start.5 = (bf16[512,256]{1,0:T(8,128)(2,1)S(1)}, bf16[512,256]{1,0:T(8,128)(2,1)S(1)}, u32[]{:S(2)}, u32[]{:S(2)}) collective-permute-start(bf16[512,256]{1,0:T(8,128)(2,1)S(1)} %pad_maximum_fusion), channel_id=1, source_target_pairs={{0,12},{1,13},{2,14},{3,15},{4,0},{5,1},{6,2},{7,3},{8,4},{9,5},{1... | collective-permute-start | bytes 786440 | tf_op jit(solution)/shard_map/kv_first/ppermute | solution.py:33
  24.4 2.2 %collective-permute-start.7 = (bf16[64,512]{1,0:T(8,128)(2,1)S(1)}, bf16[64,512]{1,0:T(8,128)(2,1)S(1)}, u32[]{:S(2)}, u32[]{:S(2)}) collective-permute-start(bf16[64,512]{1,0:T(8,128)(2,1)S(1)} %get-tuple-element.38), channel_id=1, source_target_pairs={{0,64},{1,65},{2,66},{3,67},{4,68},{5,69},{6,70},{7,71},{8,72},{9,... | collective-permute-start | bytes 196616 | tf_op jit(solution)/shard_map/q_heads/ppermute | solution.py:33
  26.6 1.9 %collective-permute-start.6 = (bf16[512,256]{1,0:T(8,128)(2,1)S(1)}, bf16[512,256]{1,0:T(8,128)(2,1)S(1)}, u32[]{:S(2)}, u32[]{:S(2)}) collective-permute-start(bf16[512,256]{1,0:T(8,128)(2,1)S(1)} %pad_maximum_fusion), channel_id=1, source_target_pairs={{0,8},{1,9},{2,10},{3,11},{4,12},{5,13},{6,14},{7,15},{8,0},{9,1},... | collective-permute-start | bytes 786440 | tf_op jit(solution)/shard_map/kv_first/ppermute | solution.py:33
  28.5 4.1 %collective-permute-start.8 = (bf16[64,512]{1,0:T(8,128)(2,1)S(1)}, bf16[64,512]{1,0:T(8,128)(2,1)S(1)}, u32[]{:S(2)}, u32[]{:S(2)}) collective-permute-start(bf16[64,512]{1,0:T(8,128)(2,1)S(1)} %get-tuple-element.39), channel_id=1, source_target_pairs={{0,128},{1,129},{2,130},{3,131},{4,132},{5,133},{6,134},{7,135},{8... | collective-permute-start | bytes 196616 | tf_op jit(solution)/shard_map/q_heads/ppermute | solution.py:33
  32.6 1.1 %collective-permute-start.9 = (bf16[64,512]{1,0:T(8,128)(2,1)S(1)}, bf16[64,512]{1,0:T(8,128)(2,1)S(1)}, u32[]{:S(2)}, u32[]{:S(2)}) collective-permute-start(bf16[64,512]{1,0:T(8,128)(2,1)S(1)} %get-tuple-element.40), channel_id=1, source_target_pairs={{0,192},{1,193},{2,194},{3,195},{4,196},{5,197},{6,198},{7,199},{8... | collective-permute-start | bytes 196616 | tf_op jit(solution)/shard_map/q_heads/ppermute | solution.py:33
  33.7 3.0 %collective-permute-done.8.refs_2_ = bf16[64,512]{1,0:T(8,128)(2,1)S(1)} collective-permute-done((bf16[64,512]{1,0:T(8,128)(2,1)S(1)}, bf16[64,512]{1,0:T(8,128)(2,1)S(1)}, u32[]{:S(2)}, u32[]{:S(2)}) %collective-permute-start.8) | collective-permute-done | bytes 65568 | tf_op jit(solution)/shard_map/q_heads/ppermute | solution.py:33
  36.7 2.0 %collective-permute-done.9.refs_3_ = bf16[64,512]{1,0:T(8,128)(2,1)S(1)} collective-permute-done((bf16[64,512]{1,0:T(8,128)(2,1)S(1)}, bf16[64,512]{1,0:T(8,128)(2,1)S(1)}, u32[]{:S(2)}, u32[]{:S(2)}) %collective-permute-start.9) | collective-permute-done | bytes 65568 | tf_op jit(solution)/shard_map/q_heads/ppermute | solution.py:33
  38.7 0.1 collective-permute-start.10
  38.8 0.0 collective-permute-done.4
  38.8 0.0 copy-start.1
  38.9 0.3 collective-permute-start.11
  39.2 1.8 %collective-permute-start.13 = (bf16[2048,256]{1,0:T(8,128)(2,1)S(1)}, bf16[2048,256]{1,0:T(8,128)(2,1)S(1)}, u32[]{:S(2)}, u32[]{:S(2)}) collective-permute-start(bf16[2048,256]{1,0:T(8,128)(2,1)S(1)} %constant_dynamic-update-slice_fusion.refs_3_), channel_id=1, source_target_pairs={{0,3},{1,0},{2,1},{3,2},{4,7},{5,4},{6,5},{7,6},{8,11},{9,8},{10,9... | collective-permute-start | bytes 3145736 | tf_op jit(solution)/shard_map/kv_second/ppermute | solution.py:33
  41.0 0.7 reshape.24
  41.7 2.0 %slice_reduce_fusion = s32[32,2]{1,0:T(8,128)} fusion(s32[32,2,256]{2,1,0:T(2,128)} %reshape.24), kind=kLoop, calls=%fused_computation.1 | loop fusion | bytes 512 | tf_op jit(solution)/shard_map/plan/slice | solution.py:429
  43.7 0.8 squeeze.3.base_ref
  44.5 2.9 %plan.1.refs_0_ = s32[440]{0:T(512)S(1)} custom-call(s32[32,512]{1,0:T(8,128)S(1)} %copy-done.1, s32[32,512]{1,0:T(8,128)S(1)} %copy-done.4, s32[64]{0:T(128)S(1)} %squeeze.3.base_ref, s32[32]{0:T(128)S(1)} %dynamic-slice_bitcast_fusion.order_ref, s32[2]{0:T(128)S(1)} %pad_add_fusion.ids_ref), custom_call_target="tpu_custom_call" | custom-call | tf_op jit(solution)/shard_map/plan/plan/pallas_call | solution.py:166
  47.4 0.0 collective-permute-done.10.refs_2_
  47.4 5.1 %flash.3 = (f32[8,256,128]{2,1,0:T(8,128)S(1)}, f32[2,256,128]{2,1,0:T(8,128)S(1)}) custom-call(s32[440]{0:T(512)S(1)} %plan.1.refs_0_, bf16[256,512]{1,0:T(8,128)(2,1)S(1)} %unpack.4.refs_1_, bf16[256,512]{1,0:T(8,128)(2,1)} %collective-permute-done.10.refs_2_, bf16[2048,256]{1,0:T(8,128)(2,1)S(1)} %constant_dynamic-update-slice_fusion.refs_3_), custom_call_target="tpu_custom_call" | custom-call | flops 12884901888 | bytes 1048576 | tf_op jit(solution)/shard_map/attend/flash/pallas_call | solution.py:349
  52.5 1.3 %collective-permute-done.11.refs_3_ = bf16[2048,256]{1,0:T(8,128)(2,1)S(1)} collective-permute-done((bf16[2048,256]{1,0:T(8,128)(2,1)S(1)}, bf16[2048,256]{1,0:T(8,128)(2,1)S(1)}, u32[]{:S(2)}, u32[]{:S(2)}) %collective-permute-start.11) | collective-permute-done | bytes 1048608 | tf_op jit(solution)/shard_map/kv_second/ppermute | solution.py:33
  53.8 1.5 %collective-permute-start.12 = (bf16[1024,256]{1,0:T(8,128)(2,1)S(1)}, bf16[1024,256]{1,0:T(8,128)(2,1)S(1)}, u32[]{:S(2)}, u32[]{:S(2)}) collective-permute-start(bf16[1024,256]{1,0:T(8,128)(2,1)S(1)} %slice.13), channel_id=1, source_target_pairs={{0,1},{1,2},{2,3},{3,0},{4,5},{5,6},{6,7},{7,4},{8,9},{9,10},{10,1... | collective-permute-start | bytes 1572872 | tf_op jit(solution)/shard_map/kv_second/ppermute | solution.py:33
  55.3 0.0 collective-permute-done.13.refs_4_
  55.4 0.7 collective-permute-start.14
  56.0 7.0 %flash.4 = (f32[8,256,128]{2,1,0:T(8,128)S(1)}, f32[2,256,128]{2,1,0:T(8,128)S(1)}) custom-call(s32[440]{0:T(512)S(1)} %plan.1.refs_0_, bf16[256,512]{1,0:T(8,128)(2,1)S(1)} %unpack.4.refs_1_, bf16[256,512]{1,0:T(8,128)(2,1)} %collective-permute-done.10.refs_2_, bf16[2048,256]{1,0:T(8,128)(2,1)S(1)} %collective-permute-done.11.refs_3_, ...), custom_call_target="tpu_custom_call" | custom-call | flops 25769803776 | bytes 2097152 | tf_op jit(solution)/shard_map/attend/flash/pallas_call | solution.py:349
  63.0 0.0 collective-permute-done.12.refs_3_
  63.1 2.8 %collective-permute-done.14.refs_4_ = bf16[1024,256]{1,0:T(8,128)(2,1)S(1)} collective-permute-done((bf16[1024,256]{1,0:T(8,128)(2,1)S(1)}, bf16[1024,256]{1,0:T(8,128)(2,1)S(1)}, u32[]{:S(2)}, u32[]{:S(2)}) %collective-permute-start.14) | collective-permute-done | bytes 524320 | tf_op jit(solution)/shard_map/kv_second/ppermute | solution.py:33
  65.8 4.9 %flash.5 = (f32[256,640]{1,0:T(8,128)S(1)}, f32[256,640]{1,0:T(8,128)S(1)}) custom-call(s32[440]{0:T(512)S(1)} %plan.1.refs_0_, bf16[256,512]{1,0:T(8,128)(2,1)S(1)} %unpack.4.refs_1_, bf16[256,512]{1,0:T(8,128)(2,1)} %collective-permute-done.10.refs_2_, bf16[1024,256]{1,0:T(8,128)(2,1)S(1)} %collective-permute-done.12.refs_3_, ...), custom_call_target="tpu_custom_call" | custom-call | flops 12884901888 | bytes 1048576 | tf_op jit(solution)/shard_map/attend/flash/pallas_call | solution.py:349
  70.7 0.1 collective-permute-start.15
  70.8 2.1 %collective-permute-done.15.b_ref = f32[256,640]{1,0:T(8,128)S(1)} collective-permute-done((f32[256,640]{1,0:T(8,128)S(1)}, f32[256,640]{1,0:T(8,128)S(1)}, u32[]{:S(2)}, u32[]{:S(2)}) %collective-permute-start.15) | collective-permute-done | bytes 655392 | tf_op jit(solution)/shard_map/merge/ppermute | solution.py:33
  72.9 1.0 %merge.1 = (bf16[64,512]{1,0:T(8,128)(2,1)S(1)}, bf16[64,512]{1,0:T(8,128)(2,1)S(1)}, bf16[64,512]{1,0:T(8,128)(2,1)S(1)}, bf16[64,512]{1,0:T(8,128)(2,1)S(1)}) custom-call(s32[1]{0:T(128)} %bitcast.zh_ref, f32[256,640]{1,0:T(8,128)S(1)} %get-tuple-element.45.a_ref, f32[256,640]{1,0:T(8,128)S(1)} %collective-permute-done.15.b_ref), custom_call_target="tpu_custom_call" | custom-call | tf_op jit(solution)/shard_map/merge/merge/pallas_call | solution.py:389
  73.9 1.5 %collective-permute-start.16 = (bf16[64,512]{1,0:T(8,128)(2,1)S(1)}, bf16[64,512]{1,0:T(8,128)(2,1)S(1)}, u32[]{:S(2)}, u32[]{:S(2)}) collective-permute-start(bf16[64,512]{1,0:T(8,128)(2,1)S(1)} %get-tuple-element.48), channel_id=1, source_target_pairs={{0,64},{1,65},{2,66},{3,67},{4,68},{5,69},{6,70},{7,71},{8,72},{9,... | collective-permute-start | bytes 196616 | tf_op jit(solution)/shard_map/out_heads/ppermute | solution.py:33
  75.3 3.3 %collective-permute-start.17 = (bf16[64,512]{1,0:T(8,128)(2,1)S(1)}, bf16[64,512]{1,0:T(8,128)(2,1)S(1)}, u32[]{:S(2)}, u32[]{:S(2)}) collective-permute-start(bf16[64,512]{1,0:T(8,128)(2,1)S(1)} %get-tuple-element.49), channel_id=1, source_target_pairs={{0,128},{1,129},{2,130},{3,131},{4,132},{5,133},{6,134},{7,135},{8... | collective-permute-start | bytes 196616 | tf_op jit(solution)/shard_map/out_heads/ppermute | solution.py:33
  78.6 2.3 %collective-permute-start.18 = (bf16[64,512]{1,0:T(8,128)(2,1)S(1)}, bf16[64,512]{1,0:T(8,128)(2,1)S(1)}, u32[]{:S(2)}, u32[]{:S(2)}) collective-permute-start(bf16[64,512]{1,0:T(8,128)(2,1)S(1)} %get-tuple-element.50), channel_id=1, source_target_pairs={{0,192},{1,193},{2,194},{3,195},{4,196},{5,197},{6,198},{7,199},{8... | collective-permute-start | bytes 196616 | tf_op jit(solution)/shard_map/out_heads/ppermute | solution.py:33
  80.9 4.2 %collective-permute-done.17.refs_2_ = bf16[64,512]{1,0:T(8,128)(2,1)S(1)} collective-permute-done((bf16[64,512]{1,0:T(8,128)(2,1)S(1)}, bf16[64,512]{1,0:T(8,128)(2,1)S(1)}, u32[]{:S(2)}, u32[]{:S(2)}) %collective-permute-start.17) | collective-permute-done | bytes 65568 | tf_op jit(solution)/shard_map/out_heads/ppermute | solution.py:33
  85.1 1.5 %collective-permute-done.18.refs_3_ = bf16[64,512]{1,0:T(8,128)(2,1)S(1)} collective-permute-done((bf16[64,512]{1,0:T(8,128)(2,1)S(1)}, bf16[64,512]{1,0:T(8,128)(2,1)S(1)}, u32[]{:S(2)}, u32[]{:S(2)}) %collective-permute-start.18) | collective-permute-done | bytes 65568 | tf_op jit(solution)/shard_map/out_heads/ppermute | solution.py:33
  86.6 0.7 unpack.5
  (23 shorter events, 0.3 us)
Async XLA Ops:
  0.0 0.8 copy-start.2
  0.8 0.8 copy-start.3
  1.7 11.4 %collective-permute-start = (bf16[64,256]{1,0:T(8,128)(2,1)S(1)}, bf16[64,256]{1,0:T(8,128)(2,1)S(1)}, u32[]{:S(2)}, u32[]{:S(2)}) collective-permute-start(bf16[64,256]{1,0:T(8,128)(2,1)S(1)} %get-tuple-element.29), channel_id=1, source_target_pairs={{0,64},{1,65},{2,66},{3,67},{4,68},{5,69},{6,70},{7,71},{8,72},{9,... | collective-permute-start | bytes 98312 | tf_op jit(solution)/shard_map/kv_heads/ppermute | solution.py:33
  5.1 8.2 %collective-permute-start.1 = (bf16[64,256]{1,0:T(8,128)(2,1)S(1)}, bf16[64,256]{1,0:T(8,128)(2,1)S(1)}, u32[]{:S(2)}, u32[]{:S(2)}) collective-permute-start(bf16[64,256]{1,0:T(8,128)(2,1)S(1)} %get-tuple-element.30), channel_id=1, source_target_pairs={{0,128},{1,129},{2,130},{3,131},{4,132},{5,133},{6,134},{7,135},{8... | collective-permute-start | bytes 98312 | tf_op jit(solution)/shard_map/kv_heads/ppermute | solution.py:33
  10.5 4.8 %collective-permute-start.2 = (bf16[64,256]{1,0:T(8,128)(2,1)S(1)}, bf16[64,256]{1,0:T(8,128)(2,1)S(1)}, u32[]{:S(2)}, u32[]{:S(2)}) collective-permute-start(bf16[64,256]{1,0:T(8,128)(2,1)S(1)} %get-tuple-element.31), channel_id=1, source_target_pairs={{0,192},{1,193},{2,194},{3,195},{4,196},{5,197},{6,198},{7,199},{8... | collective-permute-start | bytes 98312 | tf_op jit(solution)/shard_map/kv_heads/ppermute | solution.py:33
  15.3 5.1 %collective-permute-start.3 = (bf16[256,256]{1,0:T(8,128)(2,1)S(1)}, bf16[256,256]{1,0:T(8,128)(2,1)S(1)}, u32[]{:S(2)}, u32[]{:S(2)}) collective-permute-start(bf16[256,256]{1,0:T(8,128)(2,1)S(1)} %unpack.3), channel_id=1, source_target_pairs={{0,16},{1,17},{2,18},{3,19},{4,20},{5,21},{6,22},{7,23},{8,24},{9,... | collective-permute-start | bytes 393224 | tf_op jit(solution)/shard_map/kv_z/ppermute | solution.py:33
  16.5 7.9 %copy-start = (bf16[1,64,2048]{2,1,0:T(8,128)(2,1)S(1)}, bf16[1,64,2048]{2,1,0:T(8,128)(2,1)}, u32[]{:S(2)}) copy-start(bf16[1,64,2048]{2,1,0:T(8,128)(2,1)} %param.6) | copy-start | bytes 786436
  20.4 18.4 %collective-permute-start.4 = (bf16[512,256]{1,0:T(8,128)(2,1)S(1)}, bf16[512,256]{1,0:T(8,128)(2,1)S(1)}, u32[]{:S(2)}, u32[]{:S(2)}) collective-permute-start(bf16[512,256]{1,0:T(8,128)(2,1)S(1)} %pad_maximum_fusion), channel_id=1, source_target_pairs={{0,4},{1,5},{2,6},{3,7},{4,8},{5,9},{6,10},{7,11},{8,12},{9,13},{1... | collective-permute-start | bytes 786440 | tf_op jit(solution)/shard_map/kv_first/ppermute | solution.py:33
  22.6 16.2 %collective-permute-start.5 = (bf16[512,256]{1,0:T(8,128)(2,1)S(1)}, bf16[512,256]{1,0:T(8,128)(2,1)S(1)}, u32[]{:S(2)}, u32[]{:S(2)}) collective-permute-start(bf16[512,256]{1,0:T(8,128)(2,1)S(1)} %pad_maximum_fusion), channel_id=1, source_target_pairs={{0,12},{1,13},{2,14},{3,15},{4,0},{5,1},{6,2},{7,3},{8,4},{9,5},{1... | collective-permute-start | bytes 786440 | tf_op jit(solution)/shard_map/kv_first/ppermute | solution.py:33
  24.4 8.2 %collective-permute-start.7 = (bf16[64,512]{1,0:T(8,128)(2,1)S(1)}, bf16[64,512]{1,0:T(8,128)(2,1)S(1)}, u32[]{:S(2)}, u32[]{:S(2)}) collective-permute-start(bf16[64,512]{1,0:T(8,128)(2,1)S(1)} %get-tuple-element.38), channel_id=1, source_target_pairs={{0,64},{1,65},{2,66},{3,67},{4,68},{5,69},{6,70},{7,71},{8,72},{9,... | collective-permute-start | bytes 196616 | tf_op jit(solution)/shard_map/q_heads/ppermute | solution.py:33
  26.6 12.3 %collective-permute-start.6 = (bf16[512,256]{1,0:T(8,128)(2,1)S(1)}, bf16[512,256]{1,0:T(8,128)(2,1)S(1)}, u32[]{:S(2)}, u32[]{:S(2)}) collective-permute-start(bf16[512,256]{1,0:T(8,128)(2,1)S(1)} %pad_maximum_fusion), channel_id=1, source_target_pairs={{0,8},{1,9},{2,10},{3,11},{4,12},{5,13},{6,14},{7,15},{8,0},{9,1},... | collective-permute-start | bytes 786440 | tf_op jit(solution)/shard_map/kv_first/ppermute | solution.py:33
  28.5 8.2 %collective-permute-start.8 = (bf16[64,512]{1,0:T(8,128)(2,1)S(1)}, bf16[64,512]{1,0:T(8,128)(2,1)S(1)}, u32[]{:S(2)}, u32[]{:S(2)}) collective-permute-start(bf16[64,512]{1,0:T(8,128)(2,1)S(1)} %get-tuple-element.39), channel_id=1, source_target_pairs={{0,128},{1,129},{2,130},{3,131},{4,132},{5,133},{6,134},{7,135},{8... | collective-permute-start | bytes 196616 | tf_op jit(solution)/shard_map/q_heads/ppermute | solution.py:33
  32.6 6.0 %collective-permute-start.9 = (bf16[64,512]{1,0:T(8,128)(2,1)S(1)}, bf16[64,512]{1,0:T(8,128)(2,1)S(1)}, u32[]{:S(2)}, u32[]{:S(2)}) collective-permute-start(bf16[64,512]{1,0:T(8,128)(2,1)S(1)} %get-tuple-element.40), channel_id=1, source_target_pairs={{0,192},{1,193},{2,194},{3,195},{4,196},{5,197},{6,198},{7,199},{8... | collective-permute-start | bytes 196616 | tf_op jit(solution)/shard_map/q_heads/ppermute | solution.py:33
  38.7 8.8 %collective-permute-start.10 = (bf16[256,512]{1,0:T(8,128)(2,1)S(1)}, bf16[256,512]{1,0:T(8,128)(2,1)}, u32[]{:S(2)}, u32[]{:S(2)}) collective-permute-start(bf16[256,512]{1,0:T(8,128)(2,1)S(1)} %unpack.4.refs_1_), channel_id=1, source_target_pairs={{0,32},{1,33},{2,34},{3,35},{4,36},{5,37},{6,38},{7,39},{8,40},{9,... | collective-permute-start | bytes 786440 | tf_op jit(solution)/shard_map/q_heads/ppermute | solution.py:33
  38.8 2.2 %copy-start.1 = (s32[32,512]{1,0:T(8,128)S(1)}, s32[32,512]{1,0:T(8,128)}, u32[]{:S(2)}) copy-start(s32[32,512]{1,0:T(8,128)} %pos_ref) | copy-start | bytes 196612
  38.9 14.9 %collective-permute-start.11 = (bf16[2048,256]{1,0:T(8,128)(2,1)S(1)}, bf16[2048,256]{1,0:T(8,128)(2,1)S(1)}, u32[]{:S(2)}, u32[]{:S(2)}) collective-permute-start(bf16[2048,256]{1,0:T(8,128)(2,1)S(1)} %constant_dynamic-update-slice_fusion.refs_3_), channel_id=1, source_target_pairs={{0,1},{1,2},{2,3},{3,0},{4,5},{5,6},{6,7},{7,4},{8,9},{9,10},{10,1... | collective-permute-start | bytes 3145736 | tf_op jit(solution)/shard_map/kv_second/ppermute | solution.py:33
  39.2 16.1 %collective-permute-start.13 = (bf16[2048,256]{1,0:T(8,128)(2,1)S(1)}, bf16[2048,256]{1,0:T(8,128)(2,1)S(1)}, u32[]{:S(2)}, u32[]{:S(2)}) collective-permute-start(bf16[2048,256]{1,0:T(8,128)(2,1)S(1)} %constant_dynamic-update-slice_fusion.refs_3_), channel_id=1, source_target_pairs={{0,3},{1,0},{2,1},{3,2},{4,7},{5,4},{6,5},{7,6},{8,11},{9,8},{10,9... | collective-permute-start | bytes 3145736 | tf_op jit(solution)/shard_map/kv_second/ppermute | solution.py:33
  41.7 2.8 %copy-start.4 = (s32[32,512]{1,0:T(8,128)S(1)}, s32[32,512]{1,0:T(8,128)}, u32[]{:S(2)}) copy-start(s32[32,512]{1,0:T(8,128)} %seg_ref) | copy-start | bytes 196612
  53.8 9.3 %collective-permute-start.12 = (bf16[1024,256]{1,0:T(8,128)(2,1)S(1)}, bf16[1024,256]{1,0:T(8,128)(2,1)S(1)}, u32[]{:S(2)}, u32[]{:S(2)}) collective-permute-start(bf16[1024,256]{1,0:T(8,128)(2,1)S(1)} %slice.13), channel_id=1, source_target_pairs={{0,1},{1,2},{2,3},{3,0},{4,5},{5,6},{6,7},{7,4},{8,9},{9,10},{10,1... | collective-permute-start | bytes 1572872 | tf_op jit(solution)/shard_map/kv_second/ppermute | solution.py:33
  55.4 10.5 %collective-permute-start.14 = (bf16[1024,256]{1,0:T(8,128)(2,1)S(1)}, bf16[1024,256]{1,0:T(8,128)(2,1)S(1)}, u32[]{:S(2)}, u32[]{:S(2)}) collective-permute-start(bf16[1024,256]{1,0:T(8,128)(2,1)S(1)} %slice.14), channel_id=1, source_target_pairs={{0,3},{1,0},{2,1},{3,2},{4,7},{5,4},{6,5},{7,6},{8,11},{9,8},{10,9... | collective-permute-start | bytes 1572872 | tf_op jit(solution)/shard_map/kv_second/ppermute | solution.py:33
  70.7 2.2 %collective-permute-start.15 = (f32[256,640]{1,0:T(8,128)S(1)}, f32[256,640]{1,0:T(8,128)S(1)}, u32[]{:S(2)}, u32[]{:S(2)}) collective-permute-start(f32[256,640]{1,0:T(8,128)S(1)} %get-tuple-element.46), channel_id=1, source_target_pairs={{0,32},{1,33},{2,34},{3,35},{4,36},{5,37},{6,38},{7,39},{8,40},{9,... | collective-permute-start | bytes 1966088 | tf_op jit(solution)/shard_map/merge/ppermute | solution.py:33
  73.9 7.1 %collective-permute-start.16 = (bf16[64,512]{1,0:T(8,128)(2,1)S(1)}, bf16[64,512]{1,0:T(8,128)(2,1)S(1)}, u32[]{:S(2)}, u32[]{:S(2)}) collective-permute-start(bf16[64,512]{1,0:T(8,128)(2,1)S(1)} %get-tuple-element.48), channel_id=1, source_target_pairs={{0,64},{1,65},{2,66},{3,67},{4,68},{5,69},{6,70},{7,71},{8,72},{9,... | collective-permute-start | bytes 196616 | tf_op jit(solution)/shard_map/out_heads/ppermute | solution.py:33
  75.3 9.8 %collective-permute-start.17 = (bf16[64,512]{1,0:T(8,128)(2,1)S(1)}, bf16[64,512]{1,0:T(8,128)(2,1)S(1)}, u32[]{:S(2)}, u32[]{:S(2)}) collective-permute-start(bf16[64,512]{1,0:T(8,128)(2,1)S(1)} %get-tuple-element.49), channel_id=1, source_target_pairs={{0,128},{1,129},{2,130},{3,131},{4,132},{5,133},{6,134},{7,135},{8... | collective-permute-start | bytes 196616 | tf_op jit(solution)/shard_map/out_heads/ppermute | solution.py:33
  78.6 8.0 %collective-permute-start.18 = (bf16[64,512]{1,0:T(8,128)(2,1)S(1)}, bf16[64,512]{1,0:T(8,128)(2,1)S(1)}, u32[]{:S(2)}, u32[]{:S(2)}) collective-permute-start(bf16[64,512]{1,0:T(8,128)(2,1)S(1)} %get-tuple-element.50), channel_id=1, source_target_pairs={{0,192},{1,193},{2,194},{3,195},{4,196},{5,197},{6,198},{7,199},{8... | collective-permute-start | bytes 196616 | tf_op jit(solution)/shard_map/out_heads/ppermute | solution.py:33
where the time goes:
time: 87.8 us; the launch traced here: 87.3 us
  starting transfers between devices  36.6 us (42%)
  waiting for transfers between devices  22.8 us (26%)
  Pallas kernels  21.6 us (25%)
  local copies, waits for them, and re-layouts  6.02 us (7%)
    ppermute x19, starting transfers between devices, send(): return lax.ppermute(a, AXES, pairs)  36.6 us
    ppermute x19, waiting for transfers between devices, send(): return lax.ppermute(a, AXES, pairs)  22.8 us
    pallas_call x3, Pallas kernels, flash(): pl.pallas_call(functools.partial(flash_kernel, rows, chunk, carry, final)...  16.9 us
    pallas_call x1, Pallas kernels, make_plan(): pl.pallas_call(plan_kernel, out_shape=jax.ShapeDtypeStruct((Q_AT + 8,), j...  2.9 us
    slice x1, local copies, waits for them, and re-layouts, local(): bases = position.reshape(32, 2, 256)[:, :, 0].reshape(64)  2.01 us
  transfers between devices with their start and end apart: 19, of which 10 were waited for; matrix products, arithmetic and copies ran while one was open for 5% of the time, Pallas kernels for 17%

commit v1 on v0

v1 whole, which is shorter than its diff:
```python
import functools

import jax
import jax.numpy as jnp
import numpy as np
from jax import lax
from jax.experimental import pallas as pl
from jax.experimental.pallas import tpu as pltpu
from jax.sharding import PartitionSpec as P

HEADS = 16
KV = 4
D = 128
AXES = ("head", "blk")
NEVER = 1 << 20
MASKED = -1e30
LOG2E_SCALE = float(np.log2(np.e) * D**-0.5)
VMEM_LIMIT = 32 * 1024 * 1024
SMALL_LIMIT = 8 * 1024 * 1024


def device_of(zl, x, y, zh, c):
    return ((zh % 4) * 2 + c % 2) * 32 + (zl % 2) * 16 + (x % 4) * 4 + y % 4


def place_of(device):
    h, b = device // 32, device % 32
    return b // 16, (b // 4) % 4, b % 4, h // 2, h % 2


def send(a, to):
    pairs = [(i, device_of(*to(*place_of(i)))) for i in range(256)]
    return lax.ppermute(a, AXES, pairs)


def along(first, step):
    def to(zl, x, y, zh, c):
        on_x = (c == 0) == first
        return (zl, x + step, y, zh, c) if on_x else (zl, x, y + step, zh, c)

    return to


SHIFTS = (0, 3, 1, 2)


def my_z():
    return lax.axis_index("head") // 2


def pack_kernel(*refs):
    ins, outs, sems = refs[:-5], refs[-5:-1], refs[-1]
    copies = []
    for s, out in enumerate(outs):
        head = lax.rem(my_z() + s, 4)
        at = 0
        for i, a in enumerate(ins):
            width = a.shape[1] // 4
            cols = pl.ds(pl.multiple_of(head * width, width), width)
            copy = pltpu.make_async_copy(a.at[:, cols], out.at[:, pl.ds(at, width)], sems.at[s, i])
            copy.start()
            copies.append(copy)
            at += width
    for copy in copies:
        copy.wait()


def pack(*arrays):
    width = sum(a.shape[1] for a in arrays) // 4
    vmem = pl.BlockSpec(memory_space=pltpu.VMEM)
    return pl.pallas_call(
        pack_kernel,
        out_shape=[jax.ShapeDtypeStruct((64, width), jnp.bfloat16)] * 4,
        in_specs=[pl.BlockSpec(memory_space=pl.ANY)] * len(arrays),
        out_specs=[vmem] * 4,
        scratch_shapes=[pltpu.SemaphoreType.DMA((4, len(arrays)))],
        name="pack",
    )(*arrays)


def unpack_kernel(*refs):
    outs = refs[4:]
    for s in range(4):
        z = lax.rem(my_z() + 4 - s, 4)
        at = 0
        for out in outs:
            width = out.shape[1]
            out[pl.ds(pl.multiple_of(z * 64, 64), 64), :] = refs[s][:, pl.ds(at, width)]
            at += width


def unpack(arrays, widths):
    vmem = pl.BlockSpec(memory_space=pltpu.VMEM)
    return pl.pallas_call(
        unpack_kernel,
        out_shape=[jax.ShapeDtypeStruct((256, w), jnp.bfloat16) for w in widths],
        in_specs=[vmem] * 4,
        out_specs=[vmem] * len(widths),
        compiler_params=pltpu.CompilerParams(vmem_limit_bytes=SMALL_LIMIT),
        name="unpack",
    )(*arrays)


def finish_kernel(*refs):
    for s in range(4):
        z = lax.rem(my_z() + 4 - s, 4)
        refs[4][:, pl.ds(pl.multiple_of(z * 512, 512), 512)] = refs[s][...]


def finish(arrays):
    vmem = pl.BlockSpec(memory_space=pltpu.VMEM)
    return pl.pallas_call(
        finish_kernel,
        out_shape=jax.ShapeDtypeStruct((64, HEADS * D), jnp.bfloat16),
        in_specs=[vmem] * 4,
        out_specs=vmem,
        compiler_params=pltpu.CompilerParams(vmem_limit_bytes=SMALL_LIMIT),
        name="finish",
    )(*arrays)


def over_z(arrays):
    return [arrays[0]] + [
        send(arrays[s], lambda zl, x, y, z, c, s=s: (zl, x, y, z + s, c)) for s in (1, 2, 3)
    ]


CALLS = ((1, 0, 16, 1), (0, 0, 16, 24))
PLAN = 72
Q_AT = 2 * len(CALLS) * PLAN
CORE_AT = Q_AT + 4
EDGE_AT = Q_AT + 5


def doc_start(meta, at):
    start = jnp.zeros_like(at)
    for s in range(3):
        edge = meta[EDGE_AT + s]
        start = jnp.maximum(start, jnp.where(edge <= at, edge, 0))
    return start


def plan_kernel(pos_hbm, seg_hbm, behind, plan, first_ref, pos_ref, seg_ref, sems):
    core, block = lax.rem(lax.axis_index("head"), 2), lax.axis_index("blk")
    runs = [
        pltpu.make_async_copy(pos_hbm.at[:, pl.ds(h * 256, 128)], first_ref.at[h], sems.at[h])
        for h in range(2)
    ]
    whole = [
        pltpu.make_async_copy(pos_hbm, pos_ref, sems.at[2]),
        pltpu.make_async_copy(seg_hbm, seg_ref, sems.at[3]),
    ]
    for copy in whole + runs:
        copy.start()
    for copy in whole:
        copy.wait()
    zl, x, y = block // 16, (block // 4) % 4, block % 4
    pos, seg = pos_ref[...], seg_ref[...]
    for s in range(1, 4):
        plan[EDGE_AT + s - 1] = jnp.min(jnp.where(seg >= s, pos, NEVER))
    plan[CORE_AT] = core
    for copy in runs:
        copy.wait()
    queries = []
    for whose in range(2):
        for hf in range(2):
            qb = first_ref[hf, (block + 16 * whose) % 32, 0]
            plan[Q_AT + whose * 2 + hf] = qb
            queries.append((qb, doc_start(plan, qb), doc_start(plan, qb + 255)))
    for call, (whose, first, blocks, _) in enumerate(CALLS):
        counts = [[jnp.int32(0), jnp.int32(0)] for _ in range(2)]
        for k in range(first, first + blocks):
            s1, s2 = SHIFTS[k % 4], SHIFTS[k // 4]
            on_x, on_y = jnp.where(core == 0, s1, s2), jnp.where(core == 0, s2, s1)
            source = zl * 16 + (x + on_x) % 4 * 4 + (y + on_y) % 4
            for t in range(2):
                kb = first_ref[t, source, 0]
                entry = ((k - first) * 2 + t) + kb * 256
                for hf in range(2):
                    off = (call * 2 + hf) * PLAN
                    qb, lo_first, lo_last = queries[whose * 2 + hf]
                    n_full, n_part = counts[hf]
                    seen = (kb <= qb) & (kb + 255 >= lo_first)
                    whole = seen & (kb < qb) & (kb >= lo_last)
                    plan[off + 2 + n_full] = entry
                    plan[off + 36 + n_part] = entry
                    counts[hf][0] = n_full + jnp.where(whole, 1, 0)
                    counts[hf][1] = n_part + jnp.where(seen & jnp.logical_not(whole), 1, 0)
        for hf in range(2):
            off = (call * 2 + hf) * PLAN
            n_full, n_part = counts[hf]
            odd = n_full % 2
            last = plan[off + 2 + jnp.maximum(n_full - 1, 0)]
            plan[off + 36 + n_part] = jnp.where(odd == 1, last, plan[off + 36 + n_part])
            plan[off] = n_full
            plan[off + 1] = n_part + odd


def make_plan(position, segment, behind):
    return pl.pallas_call(
        plan_kernel,
        out_shape=jax.ShapeDtypeStruct((EDGE_AT + 3,), jnp.int32),
        in_specs=[pl.BlockSpec(memory_space=pl.ANY)] * 3,
        out_specs=pl.BlockSpec(memory_space=pltpu.SMEM),
        scratch_shapes=[
            pltpu.SMEM((2, 32, 128), jnp.int32),
            pltpu.VMEM((32, 512), jnp.int32),
            pltpu.VMEM((32, 512), jnp.int32),
            pltpu.SemaphoreType.DMA((4,)),
        ],
        name="plan",
    )(position, segment, behind)


def three_parts(log_sum):
    lane = lax.broadcasted_iota(jnp.int32, log_sum.shape, 1)
    high = log_sum.astype(jnp.bfloat16).astype(jnp.float32)
    rest = log_sum - high
    mid = rest.astype(jnp.bfloat16).astype(jnp.float32)
    return jnp.where(lane < 4, high, jnp.where(lane < 8, mid, rest - mid)).astype(jnp.bfloat16)


def flash_kernel(pieces, call, carry, final, *refs):
    meta = refs[0]
    q_own, q_oth = refs[1], refs[2]
    piece_refs = refs[3 : 3 + len(pieces)]
    rest = list(refs[3 + len(pieces) :])
    if carry:
        acc_in, ml_in = rest.pop(0), rest.pop(0)
    out_a, out_b = rest.pop(0), rest.pop(0)
    kt, v_s, q_s, acc, m_s, l_s = rest
    core = meta[CORE_AT]

    tile = 0
    for piece, keys in zip(piece_refs, pieces):
        for t in range(keys // 128):
            rows = pl.ds(t * 128, 128)
            kt[tile] = piece[rows, pl.ds(0, D)].T
            v_s[tile] = piece[rows, pl.ds(D, D)]
            tile += 1

    for hf in range(2):
        for h in range(4):
            rows, cols = pl.ds(hf * 128, 128), pl.ds(h * 128, 128)
            q_s[hf * 4 + h, pl.ds(0, 128), :] = q_own[rows, cols]
            q_s[hf * 4 + h, pl.ds(128, 128), :] = q_oth[rows, cols]
            if carry:
                acc[hf * 4 + h] = acc_in[hf * 4 + h]
                m_s[hf * 4 + h] = jnp.broadcast_to(ml_in[hf, :, h : h + 1], (256, 128))
                lane = lax.broadcasted_iota(jnp.int32, (256, 128), 1)
                l_s[hf * 4 + h] = jnp.where(lane == 0, ml_in[hf, :, 4 + h : 5 + h], 0.0)
            else:
                acc[hf * 4 + h] = jnp.zeros((256, 128), jnp.float32)
                m_s[hf * 4 + h] = jnp.full((256, 128), MASKED, jnp.float32)
                l_s[hf * 4 + h] = jnp.zeros((256, 128), jnp.float32)

    row = lax.broadcasted_iota(jnp.int32, (256, 128), 0)
    lane = lax.broadcasted_iota(jnp.int32, (256, 128), 1)
    own_row = row < 128
    in_half = jnp.where(own_row, row, row - 128)
    q_core = jnp.where(own_row, core, 1 - core)
    q_off = jnp.where(in_half >= 64, in_half + 64, in_half) + q_core * 64
    k_off = jnp.where(lane >= 64, lane + 64, lane) + core * 64

    def step(hf, tile_a, tile_b, masks):
        k = jnp.concatenate([kt[tile_a], kt[tile_b]], 1)
        v = jnp.concatenate([v_s[tile_a], v_s[tile_b]], 0)
        ss = [
            lax.dot_general(
                q_s[hf * 4 + h], k, (((1,), (0,)), ((), ())), preferred_element_type=jnp.float32
            )
            for h in range(4)
        ]
        ps, fades = [], []
        for h in range(4):
            i = hf * 4 + h
            s_a, s_b = ss[h][:, :128], ss[h][:, 128:]
            if masks is not None:
                s_a = jnp.where(masks[0], s_a, MASKED)
                s_b = jnp.where(masks[1], s_b, MASKED)
            old = m_s[i]
            new = jnp.maximum(old, jnp.max(jnp.maximum(s_a, s_b), axis=1, keepdims=True))
            m_s[i] = new
            p_a = jnp.exp2((s_a - new) * LOG2E_SCALE)
            p_b = jnp.exp2((s_b - new) * LOG2E_SCALE)
            fades.append(jnp.exp2((old - new) * LOG2E_SCALE))
            l_s[i] = l_s[i] * fades[-1] + p_a + p_b
            ps.append(jnp.concatenate([p_a.astype(jnp.bfloat16), p_b.astype(jnp.bfloat16)], 1))
        for h in range(4):
            i = hf * 4 + h
            acc[i] = acc[i] * fades[h] + jnp.dot(ps[h], v, preferred_element_type=jnp.float32)

    def quad(hf, tiles4):
        k = jnp.concatenate([kt[t] for t in tiles4], 1)
        v = jnp.concatenate([v_s[t] for t in tiles4], 0)
        ss = [
            lax.dot_general(
                q_s[hf * 4 + h], k, (((1,), (0,)), ((), ())), preferred_element_type=jnp.float32
            )
            for h in range(4)
        ]
        ps, fades = [], []
        for h in range(4):
            i = hf * 4 + h
            st = [ss[h][:, t * 128 : t * 128 + 128] for t in range(4)]
            top = jnp.maximum(jnp.maximum(st[0], st[1]), jnp.maximum(st[2], st[3]))
            old = m_s[i]
            new = jnp.maximum(old, jnp.max(top, axis=1, keepdims=True))
            m_s[i] = new
            p = [jnp.exp2((a - new) * LOG2E_SCALE) for a in st]
            fades.append(jnp.exp2((old - new) * LOG2E_SCALE))
            l_s[i] = l_s[i] * fades[-1] + (p[0] + p[1]) + (p[2] + p[3])
            ps.append(jnp.concatenate([a.astype(jnp.bfloat16) for a in p], 1))
        for h in range(4):
            i = hf * 4 + h
            acc[i] = acc[i] * fades[h] + jnp.dot(ps[h], v, preferred_element_type=jnp.float32)

    for hf in range(2):
        qb = meta[Q_AT + CALLS[call][0] * 2 + hf]
        off = (call * 2 + hf) * PLAN
        n_full, n_part = meta[off], meta[off + 1]

        def whole(j):
            return meta[off + 2 + j] & 255

        def whole_quad(j, _):
            quad(hf, [whole(4 * j + t) for t in range(4)])
            return 0

        lax.fori_loop(0, n_full // 4, whole_quad, 0)

        def whole_pair(j, _):
            step(hf, whole(2 * j), whole(2 * j + 1), None)
            return 0

        lax.fori_loop(n_full // 4 * 2, n_full // 2, whole_pair, 0)

        q_pos = qb + q_off
        q_lo = doc_start(meta, q_pos)

        def part_pair(j, _):
            there = 2 * j + 1 < n_part
            e_a = meta[off + 36 + 2 * j]
            e_b = jnp.where(there, meta[off + 37 + 2 * j], e_a)
            tile_a, tile_b = e_a & 255, e_b & 255
            k_a = (e_a >> 8) + k_off
            k_b = jnp.where(there, e_b >> 8, NEVER) + k_off
            masks = ((k_a <= q_pos) & (k_a >= q_lo), (k_b <= q_pos) & (k_b >= q_lo))
            step(hf, tile_a, tile_b, masks)
            return 0

        lax.fori_loop(0, (n_part + 1) // 2, part_pair, 0)

        stats = jnp.zeros((256, 128), jnp.float32)
        rows = pl.ds(hf * 128, 128)
        for h in range(4):
            i, cols = hf * 4 + h, pl.ds(h * 128, 128)
            total = jnp.sum(l_s[i], axis=1, keepdims=True)
            if final:
                total = jnp.maximum(total, 1e-30)
                log_sum = m_s[i] * LOG2E_SCALE + jnp.log2(total)
                stats = jnp.where((lane % 4 == h) & (lane < 12), log_sum, stats)
                mean = acc[i] / total
                out_a[rows, cols] = mean[:128]
                out_b[rows, cols] = mean[128:].astype(jnp.bfloat16)
            else:
                stats = jnp.where(lane == h, m_s[i], stats)
                stats = jnp.where(lane == 4 + h, total, stats)
                out_a[i] = acc[i]
        if final:
            out_a[rows, pl.ds(512, 128)] = stats[:128]
            out_b[rows, pl.ds(512, 128)] = three_parts(stats[128:])
        else:
            out_b[hf] = stats


def flash(meta, q_own, q_oth, pieces, call, state, final):
    rows = tuple(p.shape[0] for p in pieces)
    carry = state is not None
    keys = sum(rows)
    if final:
        shapes = [jax.ShapeDtypeStruct((256, 640), t) for t in (jnp.float32, jnp.bfloat16)]
    else:
        shapes = [
            jax.ShapeDtypeStruct((8, 256, 128), jnp.float32),
            jax.ShapeDtypeStruct((2, 256, 128), jnp.float32),
        ]
    vmem = pl.BlockSpec(memory_space=pltpu.VMEM)
    in_specs = [pl.BlockSpec(memory_space=pltpu.SMEM), vmem, vmem]
    in_specs += [vmem] * (len(pieces) + (2 if carry else 0))
    return pl.pallas_call(
        functools.partial(flash_kernel, rows, call, carry, final),
        out_shape=shapes,
        in_specs=in_specs,
        out_specs=[vmem, vmem],
        scratch_shapes=[
            pltpu.VMEM((keys // 128, 128, 128), jnp.bfloat16),
            pltpu.VMEM((keys // 128, 128, 128), jnp.bfloat16),
            pltpu.VMEM((8, 256, 128), jnp.bfloat16),
            pltpu.VMEM((8, 256, 128), jnp.float32),
            pltpu.VMEM((8, 256, 128), jnp.float32),
            pltpu.VMEM((8, 256, 128), jnp.float32),
        ],
        compiler_params=pltpu.CompilerParams(vmem_limit_bytes=VMEM_LIMIT),
        cost_estimate=pl.CostEstimate(
            flops=CALLS[call][3] * 2048 * keys * D, bytes_accessed=keys * 512, transcendentals=0
        ),
        name="flash",
    )(meta, q_own, q_oth, *pieces, *(state if carry else ()))


def merge_kernel(count, *refs):
    ins, outs = refs[:count], refs[count:]
    step = 256 // len(outs)
    for s, out in enumerate(outs):
        at = lax.rem(my_z() + s, 4) * 64 if len(outs) == 4 else 0
        rows = pl.ds(pl.multiple_of(at, 64), step)
        logs = []
        for a in ins:
            log_sum = a[rows, pl.ds(512, 128)].astype(jnp.float32)
            if a.dtype == jnp.bfloat16:
                log_sum = log_sum[:, 0:4] + log_sum[:, 4:8] + log_sum[:, 8:12]
            logs.append(log_sum[:, 0:4])
        top = functools.reduce(jnp.maximum, logs)
        weights = [jnp.exp2(log_sum - top) for log_sum in logs]
        total = sum(weights)
        weights = [w / total for w in weights]
        for h in range(4):
            cols = pl.ds(h * 128, 128)
            mixed = sum(
                a[rows, cols].astype(jnp.float32) * w[:, h : h + 1] for a, w in zip(ins, weights)
            )
            out[:, cols] = mixed.astype(jnp.bfloat16)
        if len(outs) == 1:
            log_sum = top + jnp.log2(total)
            lane = lax.broadcasted_iota(jnp.int32, (step, 128), 1)
            spread = jnp.zeros((step, 128), jnp.float32)
            for h in range(4):
                spread = jnp.where((lane % 4 == h) & (lane < 12), log_sum[:, h : h + 1], spread)
            out[:, pl.ds(512, 128)] = three_parts(spread)


def merge(partials, last):
    vmem = pl.BlockSpec(memory_space=pltpu.VMEM)
    shape, count = ((64, 512), 4) if last else ((256, 640), 1)
    return pl.pallas_call(
        functools.partial(merge_kernel, len(partials)),
        out_shape=[jax.ShapeDtypeStruct(shape, jnp.bfloat16)] * count,
        in_specs=[vmem] * len(partials),
        out_specs=[vmem] * count,
        compiler_params=pltpu.CompilerParams(vmem_limit_bytes=SMALL_LIMIT),
        name="merge",
    )(*partials)


def other_core(zl, x, y, zh, c):
    return (zl, x, y, zh, c + 1)


def other_lo(zl, x, y, zh, c):
    return (zl + 1, x, y, zh, c)


def after(first, *then):
    return lax.optimization_barrier((first, *then))[1:]


def local(queries, keys, values, position, segment):
    with jax.named_scope("heads"):
        parts = pack(keys.reshape(64, 512), values.reshape(64, 512), queries.reshape(64, 2048))
        kv, q_own = unpack(over_z(parts), (256, 512))
    with jax.named_scope("plan"):
        plan = make_plan(position, segment, kv[:16, :128])
    with jax.named_scope("kv_first"):
        line = [kv] + [send(kv, along(True, step)) for step in (1, -1, 2)]
        line = after(plan, *line)
        line = jnp.concatenate(line, 0)
    with jax.named_scope("q_other"):
        far_own = send(q_own, other_lo)
        q_oth = send(*after(line, q_own), other_core)
    with jax.named_scope("kv_second"):
        up, down = send(line, along(False, 1)), send(line, along(False, -1))
        half_a, half_b = send(up[:512], along(False, 1)), send(down[512:], along(False, -1))
    with jax.named_scope("attend_far"):
        (far_own,) = after(up, far_own)
        far_oth = send(far_own, other_core)
        keys = [line, up, down, half_a, half_b]
        mine, theirs = flash(plan, far_own, far_oth, keys, 0, None, True)
    with jax.named_scope("merge_far"):
        (far,) = merge([mine, send(theirs, other_core)], False)
        far_got = send(far, other_lo)
    with jax.named_scope("attend_own"):
        q_own, q_oth = after(far, q_own, q_oth)
        mine, theirs = flash(plan, q_own, q_oth, keys, 1, None, True)
    with jax.named_scope("merge_own"):
        (theirs,) = after(far_got, theirs)
        parts = merge([mine, send(theirs, other_core), far_got], True)
    with jax.named_scope("out_heads"):
        out = finish(over_z(parts))
    return out.reshape(1, 64, HEADS * D)


def solution(mesh):
    spec = P("blk", "head", None)
    return jax.shard_map(
        local,
        mesh=mesh,
        in_specs=(spec, spec, spec, P(), P()),
        out_specs=spec,
        check_vma=False,
    )
```

time: 87.8 us -> 85.2 us (0.970)
  the two profiles are of different devices: /device:TPU:24 before, /device:TPU:1 now
where the time goes in v1:
time: 85.2 us; the launch traced here: 84.1 us
  starting transfers between devices  34.1 us (40%)
  waiting for transfers between devices  28 us (33%)
  Pallas kernels  20.3 us (24%)
  local copies, waits for them, and re-layouts  1.57 us (2%)
    ppermute x19, starting transfers between devices, send(): return lax.ppermute(a, AXES, pairs)  34.1 us
    ppermute x19, waiting for transfers between devices, send(): return lax.ppermute(a, AXES, pairs)  28 us
    pallas_call x2, Pallas kernels, flash(): pl.pallas_call(functools.partial(flash_kernel, rows, call, carry, final),...  12.9 us
    pallas_call x1, Pallas kernels, make_plan(): pl.pallas_call(plan_kernel, out_shape=jax.ShapeDtypeStruct((EDGE_AT + 3,)...  2.94 us
    pallas_call x1, Pallas kernels, pack(): pl.pallas_call(pack_kernel, out_shape=[jax.ShapeDtypeStruct((64, width),...  1.88 us
    pallas_call x2, Pallas kernels, merge(): pl.pallas_call(functools.partial(merge_kernel, len(partials)), out_shape=...  1.74 us
  transfers between devices with their start and end apart: 19, of which 11 were waited for; matrix products, arithmetic and copies ran while one was open for 1% of the time, Pallas kernels for 13%

profile of v1, /device:TPU:1, one launch (start us, length us, event | category | flops | bytes accessed | tf_op | source)
XLA Modules:
  0.0 84.1 jit_solution(5246492804329400413)
XLA Ops:
  0.0 1.9 %pack.1 = (bf16[64,768]{1,0:T(8,128)(2,1)}, bf16[64,768]{1,0:T(8,128)(2,1)}, bf16[64,768]{1,0:T(8,128)(2,1)}, bf16[64,768]{1,0:T(8,128)(2,1)}) custom-call(bf16[64,512]{1,0:T(8,128)(2,1)} %bitcast.5, bf16[64,512]{1,0:T(8,128)(2,1)} %bitcast.6, bf16[64,2048]{1,0:T(8,128)(2,1)} %bitcast.4), custom_call_target="tpu_custom_call" | custom-call | tf_op jit(solution)/shard_map/heads/pack/pallas_call | solution.py:71
  1.9 3.9 %collective-permute-start = (bf16[64,768]{1,0:T(8,128)(2,1)}, bf16[64,768]{1,0:T(8,128)(2,1)S(1)}, u32[]{:S(2)}, u32[]{:S(2)}) collective-permute-start(bf16[64,768]{1,0:T(8,128)(2,1)} %get-tuple-element.29), channel_id=1, source_target_pairs={{0,64},{1,65},{2,66},{3,67},{4,68},{5,69},{6,70},{7,71},{8,72},{9,... | collective-permute-start | bytes 294920 | tf_op jit(solution)/shard_map/heads/ppermute | solution.py:33
  5.8 5.1 %collective-permute-start.1 = (bf16[64,768]{1,0:T(8,128)(2,1)}, bf16[64,768]{1,0:T(8,128)(2,1)S(1)}, u32[]{:S(2)}, u32[]{:S(2)}) collective-permute-start(bf16[64,768]{1,0:T(8,128)(2,1)} %get-tuple-element.30), channel_id=1, source_target_pairs={{0,128},{1,129},{2,130},{3,131},{4,132},{5,133},{6,134},{7,135},{8... | collective-permute-start | bytes 294920 | tf_op jit(solution)/shard_map/heads/ppermute | solution.py:33
  10.9 2.4 %collective-permute-start.2 = (bf16[64,768]{1,0:T(8,128)(2,1)}, bf16[64,768]{1,0:T(8,128)(2,1)S(1)}, u32[]{:S(2)}, u32[]{:S(2)}) collective-permute-start(bf16[64,768]{1,0:T(8,128)(2,1)} %get-tuple-element.31), channel_id=1, source_target_pairs={{0,192},{1,193},{2,194},{3,195},{4,196},{5,197},{6,198},{7,199},{8... | collective-permute-start | bytes 294920 | tf_op jit(solution)/shard_map/heads/ppermute | solution.py:33
  13.3 0.0 collective-permute-done.refs_1_
  13.3 4.0 %collective-permute-done.1.refs_2_ = bf16[64,768]{1,0:T(8,128)(2,1)S(1)} collective-permute-done((bf16[64,768]{1,0:T(8,128)(2,1)}, bf16[64,768]{1,0:T(8,128)(2,1)S(1)}, u32[]{:S(2)}, u32[]{:S(2)}) %collective-permute-start.1) | collective-permute-done | bytes 98336 | tf_op jit(solution)/shard_map/heads/ppermute | solution.py:33
  17.3 3.9 %collective-permute-done.2.refs_3_ = bf16[64,768]{1,0:T(8,128)(2,1)S(1)} collective-permute-done((bf16[64,768]{1,0:T(8,128)(2,1)}, bf16[64,768]{1,0:T(8,128)(2,1)S(1)}, u32[]{:S(2)}, u32[]{:S(2)}) %collective-permute-start.2) | collective-permute-done | bytes 98336 | tf_op jit(solution)/shard_map/heads/ppermute | solution.py:33
  21.2 0.9 %copy-done = bf16[64,768]{1,0:T(8,128)(2,1)S(1)} copy-done((bf16[64,768]{1,0:T(8,128)(2,1)S(1)}, bf16[64,768]{1,0:T(8,128)(2,1)}, u32[]{:S(2)}) %copy-start) | copy-done | bytes 98328
  22.2 1.4 %collective-permute-start.3 = (bf16[256,256]{1,0:T(8,128)(2,1)S(1)}, bf16[256,256]{1,0:T(8,128)(2,1)S(1)}, u32[]{:S(2)}, u32[]{:S(2)}) collective-permute-start(bf16[256,256]{1,0:T(8,128)(2,1)S(1)} %get-tuple-element.33), channel_id=1, source_target_pairs={{0,4},{1,5},{2,6},{3,7},{4,8},{5,9},{6,10},{7,11},{8,12},{9,13},{1... | collective-permute-start | bytes 393224 | tf_op jit(solution)/shard_map/kv_first/ppermute | solution.py:33
  23.6 1.5 %collective-permute-start.4 = (bf16[256,256]{1,0:T(8,128)(2,1)S(1)}, bf16[256,256]{1,0:T(8,128)(2,1)S(1)}, u32[]{:S(2)}, u32[]{:S(2)}) collective-permute-start(bf16[256,256]{1,0:T(8,128)(2,1)S(1)} %get-tuple-element.33), channel_id=1, source_target_pairs={{0,12},{1,13},{2,14},{3,15},{4,0},{5,1},{6,2},{7,3},{8,4},{9,5},{1... | collective-permute-start | bytes 393224 | tf_op jit(solution)/shard_map/kv_first/ppermute | solution.py:33
  25.1 1.6 %collective-permute-start.5 = (bf16[256,256]{1,0:T(8,128)(2,1)S(1)}, bf16[256,256]{1,0:T(8,128)(2,1)S(1)}, u32[]{:S(2)}, u32[]{:S(2)}) collective-permute-start(bf16[256,256]{1,0:T(8,128)(2,1)S(1)} %get-tuple-element.33), channel_id=1, source_target_pairs={{0,8},{1,9},{2,10},{3,11},{4,12},{5,13},{6,14},{7,15},{8,0},{9,1},... | collective-permute-start | bytes 393224 | tf_op jit(solution)/shard_map/kv_first/ppermute | solution.py:33
  26.6 0.6 slice.9.behind
  27.2 2.9 %plan.1.refs_0_ = s32[296]{0:T(512)} custom-call(s32[32,512]{1,0:T(8,128)} %pos_hbm.1, s32[32,512]{1,0:T(8,128)} %seg_hbm.1, bf16[16,128]{1,0:T(8,128)(2,1)} %slice.9.behind), custom_call_target="tpu_custom_call" | custom-call | tf_op jit(solution)/shard_map/plan/plan/pallas_call | solution.py:200
  30.2 0.0 collective-permute-done.3
  30.2 0.0 collective-permute-done.4
  30.2 0.5 collective-permute-done.5
  30.8 1.0 %collective-permute-start.6 = (bf16[1024,256]{1,0:T(8,128)(2,1)S(1)}, bf16[1024,256]{1,0:T(8,128)(2,1)S(1)}, u32[]{:S(2)}, u32[]{:S(2)}) collective-permute-start(bf16[1024,256]{1,0:T(8,128)(2,1)S(1)} %constant_dynamic-update-slice_fusion.refs_3_), channel_id=1, source_target_pairs={{0,1},{1,2},{2,3},{3,0},{4,5},{5,6},{6,7},{7,4},{8,9},{9,10},{10,1... | collective-permute-start | bytes 1572872 | tf_op jit(solution)/shard_map/kv_second/ppermute | solution.py:33
  31.8 1.8 %collective-permute-start.9 = (bf16[1024,256]{1,0:T(8,128)(2,1)S(1)}, bf16[1024,256]{1,0:T(8,128)(2,1)S(1)}, u32[]{:S(2)}, u32[]{:S(2)}) collective-permute-start(bf16[1024,256]{1,0:T(8,128)(2,1)S(1)} %constant_dynamic-update-slice_fusion.refs_3_), channel_id=1, source_target_pairs={{0,3},{1,0},{2,1},{3,2},{4,7},{5,4},{6,5},{7,6},{8,11},{9,8},{10,9... | collective-permute-start | bytes 1572872 | tf_op jit(solution)/shard_map/kv_second/ppermute | solution.py:33
  33.5 0.0 collective-permute-start.7
  33.5 5.5 %collective-permute-done.7.refs_1_ = bf16[256,512]{1,0:T(8,128)(2,1)S(1)} collective-permute-done((bf16[256,512]{1,0:T(8,128)(2,1)S(1)}, bf16[256,512]{1,0:T(8,128)(2,1)S(1)}, u32[]{:S(2)}, u32[]{:S(2)}) %collective-permute-start.7) | collective-permute-done | bytes 262176 | tf_op jit(solution)/shard_map/q_other/ppermute | solution.py:33
  39.0 1.3 %collective-permute-done.6.refs_4_ = bf16[1024,256]{1,0:T(8,128)(2,1)S(1)} collective-permute-done((bf16[1024,256]{1,0:T(8,128)(2,1)S(1)}, bf16[1024,256]{1,0:T(8,128)(2,1)S(1)}, u32[]{:S(2)}, u32[]{:S(2)}) %collective-permute-start.6) | collective-permute-done | bytes 524320 | tf_op jit(solution)/shard_map/kv_second/ppermute | solution.py:33
  40.4 2.6 %collective-permute-start.8 = (bf16[256,512]{1,0:T(8,128)(2,1)S(1)}, bf16[256,512]{1,0:T(8,128)(2,1)S(1)}, u32[]{:S(2)}, u32[]{:S(2)}) collective-permute-start(bf16[256,512]{1,0:T(8,128)(2,1)S(1)} %collective-permute-done.7.refs_1_), channel_id=1, source_target_pairs={{0,32},{1,33},{2,34},{3,35},{4,36},{5,37},{6,38},{7,39},{8,40},{9,... | collective-permute-start | bytes 786440 | tf_op jit(solution)/shard_map/attend_far/ppermute | solution.py:33
  43.0 0.1 collective-permute-start.10
  43.1 0.0 collective-permute-done.9.refs_5_
  43.2 2.7 %collective-permute-start.11 = (bf16[512,256]{1,0:T(8,128)(2,1)S(1)}, bf16[512,256]{1,0:T(8,128)(2,1)S(1)}, u32[]{:S(2)}, u32[]{:S(2)}) collective-permute-start(bf16[512,256]{1,0:T(8,128)(2,1)S(1)} %slice.13), channel_id=1, source_target_pairs={{0,3},{1,0},{2,1},{3,2},{4,7},{5,4},{6,5},{7,6},{8,11},{9,8},{10,9... | collective-permute-start | bytes 786440 | tf_op jit(solution)/shard_map/kv_second/ppermute | solution.py:33
  45.9 0.0 collective-permute-done.8.refs_2_
  45.9 3.9 %collective-permute-done.10.refs_6_ = bf16[512,256]{1,0:T(8,128)(2,1)S(1)} collective-permute-done((bf16[512,256]{1,0:T(8,128)(2,1)S(1)}, bf16[512,256]{1,0:T(8,128)(2,1)S(1)}, u32[]{:S(2)}, u32[]{:S(2)}) %collective-permute-start.10) | collective-permute-done | bytes 262176 | tf_op jit(solution)/shard_map/kv_second/ppermute | solution.py:33
  49.8 0.0 collective-permute-done.11.refs_7_
  49.8 0.0 copy-done.1
  49.8 5.8 %flash.2 = (f32[256,640]{1,0:T(8,128)S(1)}, bf16[256,640]{1,0:T(8,128)(2,1)S(1)}) custom-call(s32[296]{0:T(512)S(1)} %copy-done.1, bf16[256,512]{1,0:T(8,128)(2,1)S(1)} %collective-permute-done.7.refs_1_, bf16[256,512]{1,0:T(8,128)(2,1)S(1)} %collective-permute-done.8.refs_2_, bf16[1024,256]{1,0:T(8,128)(2,1)S(1)} %constant_dynamic-update-slice_fusion.refs_3_, ...), custom_call_target="tpu_custom_call" | custom-call | flops 1073741824 | bytes 2097152 | tf_op jit(solution)/shard_map/attend_far/flash/pallas_call | solution.py:391
  55.6 0.9 %collective-permute-start.12 = (bf16[256,640]{1,0:T(8,128)(2,1)S(1)}, bf16[256,640]{1,0:T(8,128)(2,1)S(1)}, u32[]{:S(2)}, u32[]{:S(2)}) collective-permute-start(bf16[256,640]{1,0:T(8,128)(2,1)S(1)} %get-tuple-element.40), channel_id=1, source_target_pairs={{0,32},{1,33},{2,34},{3,35},{4,36},{5,37},{6,38},{7,39},{8,40},{9,... | collective-permute-start | bytes 983048 | tf_op jit(solution)/shard_map/merge_far/ppermute | solution.py:33
  56.6 0.1 collective-permute-start.13
  56.7 1.2 %collective-permute-done.12.refs_1_ = bf16[256,640]{1,0:T(8,128)(2,1)S(1)} collective-permute-done((bf16[256,640]{1,0:T(8,128)(2,1)S(1)}, bf16[256,640]{1,0:T(8,128)(2,1)S(1)}, u32[]{:S(2)}, u32[]{:S(2)}) %collective-permute-start.12) | collective-permute-done | bytes 327712 | tf_op jit(solution)/shard_map/merge_far/ppermute | solution.py:33
  57.8 0.6 merge.2
  58.5 0.2 collective-permute-start.14
  58.7 0.0 collective-permute-done.13.refs_2_
  58.7 7.2 %flash.3 = (f32[256,640]{1,0:T(8,128)S(1)}, bf16[256,640]{1,0:T(8,128)(2,1)S(1)}) custom-call(s32[296]{0:T(512)S(1)} %copy-done.1, bf16[256,512]{1,0:T(8,128)(2,1)S(1)} %get-tuple-element.42.refs_1_, bf16[256,512]{1,0:T(8,128)(2,1)S(1)} %collective-permute-done.13.refs_2_, bf16[1024,256]{1,0:T(8,128)(2,1)S(1)} %constant_dynamic-update-slice_fusion.refs_3_, ...), custom_call_target="tpu_custom_call" | custom-call | flops 25769803776 | bytes 2097152 | tf_op jit(solution)/shard_map/attend_own/flash/pallas_call | solution.py:391
  65.9 1.6 %collective-permute-done.14.refs_2_ = bf16[256,640]{1,0:T(8,128)(2,1)S(1)} collective-permute-done((bf16[256,640]{1,0:T(8,128)(2,1)S(1)}, bf16[256,640]{1,0:T(8,128)(2,1)S(1)}, u32[]{:S(2)}, u32[]{:S(2)}) %collective-permute-start.14) | collective-permute-done | bytes 327712 | tf_op jit(solution)/shard_map/merge_far/ppermute | solution.py:33
  67.5 1.2 %collective-permute-start.15 = (bf16[256,640]{1,0:T(8,128)(2,1)S(1)}, bf16[256,640]{1,0:T(8,128)(2,1)S(1)}, u32[]{:S(2)}, u32[]{:S(2)}) collective-permute-start(bf16[256,640]{1,0:T(8,128)(2,1)S(1)} %get-tuple-element.46), channel_id=1, source_target_pairs={{0,32},{1,33},{2,34},{3,35},{4,36},{5,37},{6,38},{7,39},{8,40},{9,... | collective-permute-start | bytes 983048 | tf_op jit(solution)/shard_map/merge_own/ppermute | solution.py:33
  68.7 1.3 %collective-permute-done.15.refs_1_ = bf16[256,640]{1,0:T(8,128)(2,1)S(1)} collective-permute-done((bf16[256,640]{1,0:T(8,128)(2,1)S(1)}, bf16[256,640]{1,0:T(8,128)(2,1)S(1)}, u32[]{:S(2)}, u32[]{:S(2)}) %collective-permute-start.15) | collective-permute-done | bytes 327712 | tf_op jit(solution)/shard_map/merge_own/ppermute | solution.py:33
  70.0 1.1 %merge.3 = (bf16[64,512]{1,0:T(8,128)(2,1)S(1)}, bf16[64,512]{1,0:T(8,128)(2,1)S(1)}, bf16[64,512]{1,0:T(8,128)(2,1)S(1)}, bf16[64,512]{1,0:T(8,128)(2,1)S(1)}) custom-call(f32[256,640]{1,0:T(8,128)S(1)} %get-tuple-element.44.refs_0_, bf16[256,640]{1,0:T(8,128)(2,1)S(1)} %collective-permute-done.15.refs_1_, bf16[256,640]{1,0:T(8,128)(2,1)S(1)} %collective-permute-done.14.refs_2_), custom_call_target="tpu_custom_call" | custom-call | tf_op jit(solution)/shard_map/merge_own/merge/pallas_call | solution.py:446
  71.1 2.0 %collective-permute-start.16 = (bf16[64,512]{1,0:T(8,128)(2,1)S(1)}, bf16[64,512]{1,0:T(8,128)(2,1)S(1)}, u32[]{:S(2)}, u32[]{:S(2)}) collective-permute-start(bf16[64,512]{1,0:T(8,128)(2,1)S(1)} %get-tuple-element.48), channel_id=1, source_target_pairs={{0,64},{1,65},{2,66},{3,67},{4,68},{5,69},{6,70},{7,71},{8,72},{9,... | collective-permute-start | bytes 196616 | tf_op jit(solution)/shard_map/out_heads/ppermute | solution.py:33
  73.1 3.5 %collective-permute-start.17 = (bf16[64,512]{1,0:T(8,128)(2,1)S(1)}, bf16[64,512]{1,0:T(8,128)(2,1)S(1)}, u32[]{:S(2)}, u32[]{:S(2)}) collective-permute-start(bf16[64,512]{1,0:T(8,128)(2,1)S(1)} %get-tuple-element.49), channel_id=1, source_target_pairs={{0,128},{1,129},{2,130},{3,131},{4,132},{5,133},{6,134},{7,135},{8... | collective-permute-start | bytes 196616 | tf_op jit(solution)/shard_map/out_heads/ppermute | solution.py:33
  76.5 2.1 %collective-permute-start.18 = (bf16[64,512]{1,0:T(8,128)(2,1)S(1)}, bf16[64,512]{1,0:T(8,128)(2,1)S(1)}, u32[]{:S(2)}, u32[]{:S(2)}) collective-permute-start(bf16[64,512]{1,0:T(8,128)(2,1)S(1)} %get-tuple-element.50), channel_id=1, source_target_pairs={{0,192},{1,193},{2,194},{3,195},{4,196},{5,197},{6,198},{7,199},{8... | collective-permute-start | bytes 196616 | tf_op jit(solution)/shard_map/out_heads/ppermute | solution.py:33
  78.7 0.0 collective-permute-done.16.refs_1_
  78.7 2.8 %collective-permute-done.17.refs_2_ = bf16[64,512]{1,0:T(8,128)(2,1)S(1)} collective-permute-done((bf16[64,512]{1,0:T(8,128)(2,1)S(1)}, bf16[64,512]{1,0:T(8,128)(2,1)S(1)}, u32[]{:S(2)}, u32[]{:S(2)}) %collective-permute-start.17) | collective-permute-done | bytes 65568 | tf_op jit(solution)/shard_map/out_heads/ppermute | solution.py:33
  81.5 1.9 %collective-permute-done.18.refs_3_ = bf16[64,512]{1,0:T(8,128)(2,1)S(1)} collective-permute-done((bf16[64,512]{1,0:T(8,128)(2,1)S(1)}, bf16[64,512]{1,0:T(8,128)(2,1)S(1)}, u32[]{:S(2)}, u32[]{:S(2)}) %collective-permute-start.18) | collective-permute-done | bytes 65568 | tf_op jit(solution)/shard_map/out_heads/ppermute | solution.py:33
  83.4 0.7 finish.1
  (9 shorter events, 0.1 us)
Async XLA Ops:
  1.9 11.4 %collective-permute-start = (bf16[64,768]{1,0:T(8,128)(2,1)}, bf16[64,768]{1,0:T(8,128)(2,1)S(1)}, u32[]{:S(2)}, u32[]{:S(2)}) collective-permute-start(bf16[64,768]{1,0:T(8,128)(2,1)} %get-tuple-element.29), channel_id=1, source_target_pairs={{0,64},{1,65},{2,66},{3,67},{4,68},{5,69},{6,70},{7,71},{8,72},{9,... | collective-permute-start | bytes 294920 | tf_op jit(solution)/shard_map/heads/ppermute | solution.py:33
  5.8 11.5 %collective-permute-start.1 = (bf16[64,768]{1,0:T(8,128)(2,1)}, bf16[64,768]{1,0:T(8,128)(2,1)S(1)}, u32[]{:S(2)}, u32[]{:S(2)}) collective-permute-start(bf16[64,768]{1,0:T(8,128)(2,1)} %get-tuple-element.30), channel_id=1, source_target_pairs={{0,128},{1,129},{2,130},{3,131},{4,132},{5,133},{6,134},{7,135},{8... | collective-permute-start | bytes 294920 | tf_op jit(solution)/shard_map/heads/ppermute | solution.py:33
  10.9 10.3 %collective-permute-start.2 = (bf16[64,768]{1,0:T(8,128)(2,1)}, bf16[64,768]{1,0:T(8,128)(2,1)S(1)}, u32[]{:S(2)}, u32[]{:S(2)}) collective-permute-start(bf16[64,768]{1,0:T(8,128)(2,1)} %get-tuple-element.31), channel_id=1, source_target_pairs={{0,192},{1,193},{2,194},{3,195},{4,196},{5,197},{6,198},{7,199},{8... | collective-permute-start | bytes 294920 | tf_op jit(solution)/shard_map/heads/ppermute | solution.py:33
  21.2 0.9 %copy-start = (bf16[64,768]{1,0:T(8,128)(2,1)S(1)}, bf16[64,768]{1,0:T(8,128)(2,1)}, u32[]{:S(2)}) copy-start(bf16[64,768]{1,0:T(8,128)(2,1)} %get-tuple-element.28.refs_0_) | copy-start | bytes 294916
  22.2 8.0 %collective-permute-start.3 = (bf16[256,256]{1,0:T(8,128)(2,1)S(1)}, bf16[256,256]{1,0:T(8,128)(2,1)S(1)}, u32[]{:S(2)}, u32[]{:S(2)}) collective-permute-start(bf16[256,256]{1,0:T(8,128)(2,1)S(1)} %get-tuple-element.33), channel_id=1, source_target_pairs={{0,4},{1,5},{2,6},{3,7},{4,8},{5,9},{6,10},{7,11},{8,12},{9,13},{1... | collective-permute-start | bytes 393224 | tf_op jit(solution)/shard_map/kv_first/ppermute | solution.py:33
  23.6 6.6 %collective-permute-start.4 = (bf16[256,256]{1,0:T(8,128)(2,1)S(1)}, bf16[256,256]{1,0:T(8,128)(2,1)S(1)}, u32[]{:S(2)}, u32[]{:S(2)}) collective-permute-start(bf16[256,256]{1,0:T(8,128)(2,1)S(1)} %get-tuple-element.33), channel_id=1, source_target_pairs={{0,12},{1,13},{2,14},{3,15},{4,0},{5,1},{6,2},{7,3},{8,4},{9,5},{1... | collective-permute-start | bytes 393224 | tf_op jit(solution)/shard_map/kv_first/ppermute | solution.py:33
  25.1 5.6 %collective-permute-start.5 = (bf16[256,256]{1,0:T(8,128)(2,1)S(1)}, bf16[256,256]{1,0:T(8,128)(2,1)S(1)}, u32[]{:S(2)}, u32[]{:S(2)}) collective-permute-start(bf16[256,256]{1,0:T(8,128)(2,1)S(1)} %get-tuple-element.33), channel_id=1, source_target_pairs={{0,8},{1,9},{2,10},{3,11},{4,12},{5,13},{6,14},{7,15},{8,0},{9,1},... | collective-permute-start | bytes 393224 | tf_op jit(solution)/shard_map/kv_first/ppermute | solution.py:33
  30.8 9.6 %collective-permute-start.6 = (bf16[1024,256]{1,0:T(8,128)(2,1)S(1)}, bf16[1024,256]{1,0:T(8,128)(2,1)S(1)}, u32[]{:S(2)}, u32[]{:S(2)}) collective-permute-start(bf16[1024,256]{1,0:T(8,128)(2,1)S(1)} %constant_dynamic-update-slice_fusion.refs_3_), channel_id=1, source_target_pairs={{0,1},{1,2},{2,3},{3,0},{4,5},{5,6},{6,7},{7,4},{8,9},{9,10},{10,1... | collective-permute-start | bytes 1572872 | tf_op jit(solution)/shard_map/kv_second/ppermute | solution.py:33
  31.8 11.4 %collective-permute-start.9 = (bf16[1024,256]{1,0:T(8,128)(2,1)S(1)}, bf16[1024,256]{1,0:T(8,128)(2,1)S(1)}, u32[]{:S(2)}, u32[]{:S(2)}) collective-permute-start(bf16[1024,256]{1,0:T(8,128)(2,1)S(1)} %constant_dynamic-update-slice_fusion.refs_3_), channel_id=1, source_target_pairs={{0,3},{1,0},{2,1},{3,2},{4,7},{5,4},{6,5},{7,6},{8,11},{9,8},{10,9... | collective-permute-start | bytes 1572872 | tf_op jit(solution)/shard_map/kv_second/ppermute | solution.py:33
  33.5 5.5 %collective-permute-start.7 = (bf16[256,512]{1,0:T(8,128)(2,1)S(1)}, bf16[256,512]{1,0:T(8,128)(2,1)S(1)}, u32[]{:S(2)}, u32[]{:S(2)}) collective-permute-start(bf16[256,512]{1,0:T(8,128)(2,1)S(1)} %get-tuple-element.42.refs_1_), channel_id=1, source_target_pairs={{0,16},{1,17},{2,18},{3,19},{4,20},{5,21},{6,22},{7,23},{8,24},{9,... | collective-permute-start | bytes 786440 | tf_op jit(solution)/shard_map/q_other/ppermute | solution.py:33
  40.4 5.5 %collective-permute-start.8 = (bf16[256,512]{1,0:T(8,128)(2,1)S(1)}, bf16[256,512]{1,0:T(8,128)(2,1)S(1)}, u32[]{:S(2)}, u32[]{:S(2)}) collective-permute-start(bf16[256,512]{1,0:T(8,128)(2,1)S(1)} %collective-permute-done.7.refs_1_), channel_id=1, source_target_pairs={{0,32},{1,33},{2,34},{3,35},{4,36},{5,37},{6,38},{7,39},{8,40},{9,... | collective-permute-start | bytes 786440 | tf_op jit(solution)/shard_map/attend_far/ppermute | solution.py:33
  43.0 6.8 %copy-start.1 = (s32[296]{0:T(512)S(1)}, s32[296]{0:T(512)}, u32[]{:S(2)}) copy-start(s32[296]{0:T(512)} %plan.1.refs_0_) | copy-start | bytes 3556
  43.0 6.8 %collective-permute-start.10 = (bf16[512,256]{1,0:T(8,128)(2,1)S(1)}, bf16[512,256]{1,0:T(8,128)(2,1)S(1)}, u32[]{:S(2)}, u32[]{:S(2)}) collective-permute-start(bf16[512,256]{1,0:T(8,128)(2,1)S(1)} %slice.12), channel_id=1, source_target_pairs={{0,1},{1,2},{2,3},{3,0},{4,5},{5,6},{6,7},{7,4},{8,9},{9,10},{10,1... | collective-permute-start | bytes 786440 | tf_op jit(solution)/shard_map/kv_second/ppermute | solution.py:33
  43.2 6.7 %collective-permute-start.11 = (bf16[512,256]{1,0:T(8,128)(2,1)S(1)}, bf16[512,256]{1,0:T(8,128)(2,1)S(1)}, u32[]{:S(2)}, u32[]{:S(2)}) collective-permute-start(bf16[512,256]{1,0:T(8,128)(2,1)S(1)} %slice.13), channel_id=1, source_target_pairs={{0,3},{1,0},{2,1},{3,2},{4,7},{5,4},{6,5},{7,6},{8,11},{9,8},{10,9... | collective-permute-start | bytes 786440 | tf_op jit(solution)/shard_map/kv_second/ppermute | solution.py:33
  55.6 2.2 %collective-permute-start.12 = (bf16[256,640]{1,0:T(8,128)(2,1)S(1)}, bf16[256,640]{1,0:T(8,128)(2,1)S(1)}, u32[]{:S(2)}, u32[]{:S(2)}) collective-permute-start(bf16[256,640]{1,0:T(8,128)(2,1)S(1)} %get-tuple-element.40), channel_id=1, source_target_pairs={{0,32},{1,33},{2,34},{3,35},{4,36},{5,37},{6,38},{7,39},{8,40},{9,... | collective-permute-start | bytes 983048 | tf_op jit(solution)/shard_map/merge_far/ppermute | solution.py:33
  56.6 2.1 %collective-permute-start.13 = (bf16[256,512]{1,0:T(8,128)(2,1)S(1)}, bf16[256,512]{1,0:T(8,128)(2,1)S(1)}, u32[]{:S(2)}, u32[]{:S(2)}) collective-permute-start(bf16[256,512]{1,0:T(8,128)(2,1)S(1)} %get-tuple-element.42.refs_1_), channel_id=1, source_target_pairs={{0,32},{1,33},{2,34},{3,35},{4,36},{5,37},{6,38},{7,39},{8,40},{9,... | collective-permute-start | bytes 786440 | tf_op jit(solution)/shard_map/q_other/ppermute | solution.py:33
  58.5 9.0 %collective-permute-start.14 = (bf16[256,640]{1,0:T(8,128)(2,1)S(1)}, bf16[256,640]{1,0:T(8,128)(2,1)S(1)}, u32[]{:S(2)}, u32[]{:S(2)}) collective-permute-start(bf16[256,640]{1,0:T(8,128)(2,1)S(1)} %merge.2), channel_id=1, source_target_pairs={{0,16},{1,17},{2,18},{3,19},{4,20},{5,21},{6,22},{7,23},{8,24},{9,... | collective-permute-start | bytes 983048 | tf_op jit(solution)/shard_map/merge_far/ppermute | solution.py:33
  67.5 2.5 %collective-permute-start.15 = (bf16[256,640]{1,0:T(8,128)(2,1)S(1)}, bf16[256,640]{1,0:T(8,128)(2,1)S(1)}, u32[]{:S(2)}, u32[]{:S(2)}) collective-permute-start(bf16[256,640]{1,0:T(8,128)(2,1)S(1)} %get-tuple-element.46), channel_id=1, source_target_pairs={{0,32},{1,33},{2,34},{3,35},{4,36},{5,37},{6,38},{7,39},{8,40},{9,... | collective-permute-start | bytes 983048 | tf_op jit(solution)/shard_map/merge_own/ppermute | solution.py:33
  71.1 7.6 %collective-permute-start.16 = (bf16[64,512]{1,0:T(8,128)(2,1)S(1)}, bf16[64,512]{1,0:T(8,128)(2,1)S(1)}, u32[]{:S(2)}, u32[]{:S(2)}) collective-permute-start(bf16[64,512]{1,0:T(8,128)(2,1)S(1)} %get-tuple-element.48), channel_id=1, source_target_pairs={{0,64},{1,65},{2,66},{3,67},{4,68},{5,69},{6,70},{7,71},{8,72},{9,... | collective-permute-start | bytes 196616 | tf_op jit(solution)/shard_map/out_heads/ppermute | solution.py:33
  73.1 8.4 %collective-permute-start.17 = (bf16[64,512]{1,0:T(8,128)(2,1)S(1)}, bf16[64,512]{1,0:T(8,128)(2,1)S(1)}, u32[]{:S(2)}, u32[]{:S(2)}) collective-permute-start(bf16[64,512]{1,0:T(8,128)(2,1)S(1)} %get-tuple-element.49), channel_id=1, source_target_pairs={{0,128},{1,129},{2,130},{3,131},{4,132},{5,133},{6,134},{7,135},{8... | collective-permute-start | bytes 196616 | tf_op jit(solution)/shard_map/out_heads/ppermute | solution.py:33
  76.5 6.9 %collective-permute-start.18 = (bf16[64,512]{1,0:T(8,128)(2,1)S(1)}, bf16[64,512]{1,0:T(8,128)(2,1)S(1)}, u32[]{:S(2)}, u32[]{:S(2)}) collective-permute-start(bf16[64,512]{1,0:T(8,128)(2,1)S(1)} %get-tuple-element.50), channel_id=1, source_target_pairs={{0,192},{1,193},{2,194},{3,195},{4,196},{5,197},{6,198},{7,199},{8... | collective-permute-start | bytes 196616 | tf_op jit(solution)/shard_map/out_heads/ppermute | solution.py:33

commit v2 on v1

--- a/solution.py
+++ b/solution.py
@@ -48,19 +48,23 @@
     return lax.axis_index("head") // 2
 
 
+def cut(arrays, s):
+    head, at = lax.rem(my_z() + s, 4), 0
+    for a in arrays:
+        width = a.shape[1] // 4
+        yield a, pl.ds(pl.multiple_of(head * width, width), width), at
+        at += width
+
+
 def pack_kernel(*refs):
-    ins, outs, sems = refs[:-5], refs[-5:-1], refs[-1]
+    ins, outs, sems = refs[:3], refs[3:6], refs[6]
     copies = []
     for s, out in enumerate(outs):
-        head = lax.rem(my_z() + s, 4)
-        at = 0
-        for i, a in enumerate(ins):
+        for i, (a, cols, at) in enumerate(cut(ins, s + 1)):
             width = a.shape[1] // 4
-            cols = pl.ds(pl.multiple_of(head * width, width), width)
             copy = pltpu.make_async_copy(a.at[:, cols], out.at[:, pl.ds(at, width)], sems.at[s, i])
             copy.start()
             copies.append(copy)
-            at += width
     for copy in copies:
         copy.wait()
 
@@ -70,35 +74,39 @@
     vmem = pl.BlockSpec(memory_space=pltpu.VMEM)
     return pl.pallas_call(
         pack_kernel,
-        out_shape=[jax.ShapeDtypeStruct((64, width), jnp.bfloat16)] * 4,
-        in_specs=[pl.BlockSpec(memory_space=pl.ANY)] * len(arrays),
-        out_specs=[vmem] * 4,
-        scratch_shapes=[pltpu.SemaphoreType.DMA((4, len(arrays)))],
+        out_shape=[jax.ShapeDtypeStruct((64, width), jnp.bfloat16)] * 3,
+        in_specs=[pl.BlockSpec(memory_space=pl.ANY)] * 3,
+        out_specs=[vmem] * 3,
+        scratch_shapes=[pltpu.SemaphoreType.DMA((3, 3))],
         name="pack",
     )(*arrays)
 
 
 def unpack_kernel(*refs):
-    outs = refs[4:]
-    for s in range(4):
-        z = lax.rem(my_z() + 4 - s, 4)
-        at = 0
-        for out in outs:
-            width = out.shape[1]
-            out[pl.ds(pl.multiple_of(z * 64, 64), 64), :] = refs[s][:, pl.ds(at, width)]
-            at += width
-
-
-def unpack(arrays, widths):
+    ins, outs = refs[:3], refs[6:]
+    own = pl.ds(pl.multiple_of(my_z() * 64, 64), 64)
+    for a, cols, at in cut(ins, 0):
+        width = a.shape[1] // 4
+        if at < 256:
+            outs[0][own, pl.ds(at, width)] = a[:, cols]
+        else:
+            outs[1][own, :] = a[:, cols]
+    for s in range(1, 4):
+        rows = pl.ds(pl.multiple_of(lax.rem(my_z() + 4 - s, 4) * 64, 64), 64)
+        outs[0][rows, :] = refs[2 + s][:, pl.ds(0, 256)]
+        outs[1][rows, :] = refs[2 + s][:, pl.ds(256, 512)]
+
+
+def unpack(arrays, got):
     vmem = pl.BlockSpec(memory_space=pltpu.VMEM)
     return pl.pallas_call(
         unpack_kernel,
-        out_shape=[jax.ShapeDtypeStruct((256, w), jnp.bfloat16) for w in widths],
-        in_specs=[vmem] * 4,
-        out_specs=[vmem] * len(widths),
+        out_shape=[jax.ShapeDtypeStruct((256, w), jnp.bfloat16) for w in (256, 512)],
+        in_specs=[vmem] * 6,
+        out_specs=[vmem] * 2,
         compiler_params=pltpu.CompilerParams(vmem_limit_bytes=SMALL_LIMIT),
         name="unpack",
-    )(*arrays)
+    )(*arrays, *got)
 
 
 def finish_kernel(*refs):
@@ -120,12 +128,12 @@
 
 
 def over_z(arrays):
-    return [arrays[0]] + [
-        send(arrays[s], lambda zl, x, y, z, c, s=s: (zl, x, y, z + s, c)) for s in (1, 2, 3)
+    return [
+        send(a, lambda zl, x, y, z, c, s=s: (zl, x, y, z + s, c)) for s, a in enumerate(arrays, 1)
     ]
 
 
-CALLS = ((1, 0, 16, 1), (0, 0, 16, 24))
+CALLS = ((1, 0, 12, 1), (1, 12, 4, 1), (0, 0, 16, 24))
 PLAN = 72
 Q_AT = 2 * len(CALLS) * PLAN
 CORE_AT = Q_AT + 4
@@ -140,7 +148,7 @@
     return start
 
 
-def plan_kernel(pos_hbm, seg_hbm, behind, plan, first_ref, pos_ref, seg_ref, sems):
+def plan_kernel(pos_hbm, seg_hbm, plan, first_ref, pos_ref, seg_ref, sems):
     core, block = lax.rem(lax.axis_index("head"), 2), lax.axis_index("blk")
     runs = [
         pltpu.make_async_copy(pos_hbm.at[:, pl.ds(h * 256, 128)], first_ref.at[h], sems.at[h])
@@ -196,11 +204,11 @@
             plan[off + 1] = n_part + odd
 
 
-def make_plan(position, segment, behind):
+def make_plan(position, segment):
     return pl.pallas_call(
         plan_kernel,
         out_shape=jax.ShapeDtypeStruct((EDGE_AT + 3,), jnp.int32),
-        in_specs=[pl.BlockSpec(memory_space=pl.ANY)] * 3,
+        in_specs=[pl.BlockSpec(memory_space=pl.ANY)] * 2,
         out_specs=pl.BlockSpec(memory_space=pltpu.SMEM),
         scratch_shapes=[
             pltpu.SMEM((2, 32, 128), jnp.int32),
@@ -208,8 +216,9 @@
             pltpu.VMEM((32, 512), jnp.int32),
             pltpu.SemaphoreType.DMA((4,)),
         ],
+        compiler_params=pltpu.CompilerParams(vmem_limit_bytes=SMALL_LIMIT),
         name="plan",
-    )(position, segment, behind)
+    )(position, segment)
 
 
 def three_parts(log_sum):
@@ -360,7 +369,7 @@
                 total = jnp.maximum(total, 1e-30)
                 log_sum = m_s[i] * LOG2E_SCALE + jnp.log2(total)
                 stats = jnp.where((lane % 4 == h) & (lane < 12), log_sum, stats)
-                mean = acc[i] / total
+                mean = acc[i] * (1 / total)
                 out_a[rows, cols] = mean[:128]
                 out_b[rows, cols] = mean[128:].astype(jnp.bfloat16)
             else:
@@ -467,36 +476,36 @@
 
 def local(queries, keys, values, position, segment):
     with jax.named_scope("heads"):
-        parts = pack(keys.reshape(64, 512), values.reshape(64, 512), queries.reshape(64, 2048))
-        kv, q_own = unpack(over_z(parts), (256, 512))
-    with jax.named_scope("plan"):
-        plan = make_plan(position, segment, kv[:16, :128])
+        held = keys.reshape(64, 512), values.reshape(64, 512), queries.reshape(64, 2048)
+        plan = make_plan(position, segment)
+        kv, q_own = unpack(held, after(plan, *over_z(pack(*held))))
     with jax.named_scope("kv_first"):
         line = [kv] + [send(kv, along(True, step)) for step in (1, -1, 2)]
-        line = after(plan, *line)
-        line = jnp.concatenate(line, 0)
+        line_a, line_b = jnp.concatenate(line[:2], 0), jnp.concatenate(line[2:], 0)
+    with jax.named_scope("kv_second"):
+        up_a, down_b = send(line_a, along(False, 1)), send(line_b, along(False, -1))
+        up_b, down_a = send(line_b, along(False, 1)), send(line_a, along(False, -1))
+        far_a, far_b = send(up_a, along(False, 1)), send(down_b, along(False, -1))
     with jax.named_scope("q_other"):
+        q_oth = send(*after(line_a, q_own), other_core)
         far_own = send(q_own, other_lo)
-        q_oth = send(*after(line, q_own), other_core)
-    with jax.named_scope("kv_second"):
-        up, down = send(line, along(False, 1)), send(line, along(False, -1))
-        half_a, half_b = send(up[:512], along(False, 1)), send(down[512:], along(False, -1))
+        (far_own,) = after(up_b, far_own)
+        far_oth = send(far_own, other_core)
     with jax.named_scope("attend_far"):
-        (far_own,) = after(up, far_own)
-        far_oth = send(far_own, other_core)
-        keys = [line, up, down, half_a, half_b]
-        mine, theirs = flash(plan, far_own, far_oth, keys, 0, None, True)
+        keys = [line_a, line_b, up_a, up_b, down_a, down_b, far_a, far_b]
+        state = flash(plan, far_own, far_oth, keys[:6], 0, None, False)
+        mine, theirs = flash(plan, far_own, far_oth, keys[6:], 1, state, True)
     with jax.named_scope("merge_far"):
         (far,) = merge([mine, send(theirs, other_core)], False)
         far_got = send(far, other_lo)
     with jax.named_scope("attend_own"):
         q_own, q_oth = after(far, q_own, q_oth)
-        mine, theirs = flash(plan, q_own, q_oth, keys, 1, None, True)
+        mine, theirs = flash(plan, q_own, q_oth, keys, 2, None, True)
     with jax.named_scope("merge_own"):
         (theirs,) = after(far_got, theirs)
         parts = merge([mine, send(theirs, other_core), far_got], True)
     with jax.named_scope("out_heads"):
-        out = finish(over_z(parts))
+        out = finish([parts[0]] + over_z(parts[1:]))
     return out.reshape(1, 64, HEADS * D)
 
 

time: 85.2 us -> 81.3 us (0.954); the launches traced: 84.1 us -> 82 us
  waiting for transfers between devices: 28 us -> 21.8 us
  starting transfers between devices: 34.1 us -> 37.4 us
  Pallas kernels: 20.3 us -> 22.7 us
  local copies, waits for them, and re-layouts: 1.57 us -> 0.06 us
    ppermute x19 -> x21, waiting for transfers between devices: 28 us -> 21.8 us  [send(): return lax.ppermute(a, AXES, pairs)]
    ppermute x19 -> x21, starting transfers between devices: 34.1 us -> 37.4 us  [send(): return lax.ppermute(a, AXES, pairs)]
    pallas_call x2 -> x3, Pallas kernels: 12.9 us -> 15.4 us  [flash(): pl.pallas_call(functools.partial(flash_kernel, rows, call, carry, final),...]
    unnamed x7 -> x12, local copies, waits for them, and re-layouts: 0.93 us -> 0.04 us
  transfers between devices with their start and end apart: 19 -> 21, of which waited for: 11 -> 12; matrix products, arithmetic and copies ran while one was open for 1% -> 0% of each run, Pallas kernels for 13% -> 19%
where the time goes in v2:
time: 81.3 us; the launch traced here: 82 us
  starting transfers between devices  37.4 us (46%)
  Pallas kernels  22.7 us (28%)
  waiting for transfers between devices  21.8 us (27%)
    ppermute x21, starting transfers between devices, send(): return lax.ppermute(a, AXES, pairs)  37.4 us
    ppermute x21, waiting for transfers between devices, send(): return lax.ppermute(a, AXES, pairs)  21.8 us
    pallas_call x3, Pallas kernels, flash(): pl.pallas_call(functools.partial(flash_kernel, rows, call, carry, final),...  15.4 us
    pallas_call x1, Pallas kernels, make_plan(): pl.pallas_call(plan_kernel, out_shape=jax.ShapeDtypeStruct((EDGE_AT + 3,)...  2.89 us
    pallas_call x1, Pallas kernels, pack(): pl.pallas_call(pack_kernel, out_shape=[jax.ShapeDtypeStruct((64, width),...  1.83 us
    pallas_call x2, Pallas kernels, merge(): pl.pallas_call(functools.partial(merge_kernel, len(partials)), out_shape=...  1.74 us
  transfers between devices with their start and end apart: 21, of which 12 were waited for; matrix products, arithmetic and copies ran while one was open for 0% of the time, Pallas kernels for 19%

profile of v2, /device:TPU:1, one launch (start us, length us, event | category | flops | bytes accessed | tf_op | source)
XLA Modules:
  0.0 82.0 jit_solution(16684249278018200937)
XLA Ops:
  0.0 1.8 %pack.1 = (bf16[64,768]{1,0:T(8,128)(2,1)}, bf16[64,768]{1,0:T(8,128)(2,1)}, bf16[64,768]{1,0:T(8,128)(2,1)}) custom-call(bf16[64,512]{1,0:T(8,128)(2,1)} %bitcast.6, bf16[64,512]{1,0:T(8,128)(2,1)} %bitcast.8, bf16[64,2048]{1,0:T(8,128)(2,1)} %bitcast.4), custom_call_target="tpu_custom_call" | custom-call | tf_op jit(solution)/shard_map/heads/pack/pallas_call | solution.py:75
  1.9 3.9 %collective-permute-start = (bf16[64,768]{1,0:T(8,128)(2,1)}, bf16[64,768]{1,0:T(8,128)(2,1)S(1)}, u32[]{:S(2)}, u32[]{:S(2)}) collective-permute-start(bf16[64,768]{1,0:T(8,128)(2,1)} %get-tuple-element.28), channel_id=1, source_target_pairs={{0,64},{1,65},{2,66},{3,67},{4,68},{5,69},{6,70},{7,71},{8,72},{9,... | collective-permute-start | bytes 294920 | tf_op jit(solution)/shard_map/heads/ppermute | solution.py:33
  5.8 5.1 %collective-permute-start.1 = (bf16[64,768]{1,0:T(8,128)(2,1)}, bf16[64,768]{1,0:T(8,128)(2,1)S(1)}, u32[]{:S(2)}, u32[]{:S(2)}) collective-permute-start(bf16[64,768]{1,0:T(8,128)(2,1)} %get-tuple-element.29), channel_id=1, source_target_pairs={{0,128},{1,129},{2,130},{3,131},{4,132},{5,133},{6,134},{7,135},{8... | collective-permute-start | bytes 294920 | tf_op jit(solution)/shard_map/heads/ppermute | solution.py:33
  10.9 2.4 %collective-permute-start.2 = (bf16[64,768]{1,0:T(8,128)(2,1)}, bf16[64,768]{1,0:T(8,128)(2,1)S(1)}, u32[]{:S(2)}, u32[]{:S(2)}) collective-permute-start(bf16[64,768]{1,0:T(8,128)(2,1)} %get-tuple-element.30), channel_id=1, source_target_pairs={{0,192},{1,193},{2,194},{3,195},{4,196},{5,197},{6,198},{7,199},{8... | collective-permute-start | bytes 294920 | tf_op jit(solution)/shard_map/heads/ppermute | solution.py:33
  13.3 2.9 %plan.1.refs_0_ = s32[440]{0:T(512)S(1)} custom-call(s32[32,512]{1,0:T(8,128)S(1)} %copy-done.3, s32[32,512]{1,0:T(8,128)S(1)} %copy-done.4), custom_call_target="tpu_custom_call" | custom-call | tf_op jit(solution)/shard_map/heads/plan/pallas_call | solution.py:208
  16.2 0.0 collective-permute-done.refs_3_
  16.2 1.1 %collective-permute-done.1.refs_4_ = bf16[64,768]{1,0:T(8,128)(2,1)S(1)} collective-permute-done((bf16[64,768]{1,0:T(8,128)(2,1)}, bf16[64,768]{1,0:T(8,128)(2,1)S(1)}, u32[]{:S(2)}, u32[]{:S(2)}) %collective-permute-start.1) | collective-permute-done | bytes 98336 | tf_op jit(solution)/shard_map/heads/ppermute | solution.py:33
  17.3 3.9 %collective-permute-done.2.refs_5_ = bf16[64,768]{1,0:T(8,128)(2,1)S(1)} collective-permute-done((bf16[64,768]{1,0:T(8,128)(2,1)}, bf16[64,768]{1,0:T(8,128)(2,1)S(1)}, u32[]{:S(2)}, u32[]{:S(2)}) %collective-permute-start.2) | collective-permute-done | bytes 98336 | tf_op jit(solution)/shard_map/heads/ppermute | solution.py:33
  21.2 0.1 unpack.1
  21.3 2.8 %collective-permute-start.3 = (bf16[256,256]{1,0:T(8,128)(2,1)S(1)}, bf16[256,256]{1,0:T(8,128)(2,1)S(1)}, u32[]{:S(2)}, u32[]{:S(2)}) collective-permute-start(bf16[256,256]{1,0:T(8,128)(2,1)S(1)} %get-tuple-element.34), channel_id=1, source_target_pairs={{0,12},{1,13},{2,14},{3,15},{4,0},{5,1},{6,2},{7,3},{8,4},{9,5},{1... | collective-permute-start | bytes 393224 | tf_op jit(solution)/shard_map/kv_first/ppermute | solution.py:33
  24.1 0.3 collective-permute-start.4
  24.5 0.8 collective-permute-start.8
  25.2 0.0 collective-permute-start.6
  25.2 2.2 %collective-permute-done.3 = bf16[256,256]{1,0:T(8,128)(2,1)S(1)} collective-permute-done((bf16[256,256]{1,0:T(8,128)(2,1)S(1)}, bf16[256,256]{1,0:T(8,128)(2,1)S(1)}, u32[]{:S(2)}, u32[]{:S(2)}) %collective-permute-start.3) | collective-permute-done | bytes 131104 | tf_op jit(solution)/shard_map/kv_first/ppermute | solution.py:33
  27.4 2.3 %collective-permute-done.4 = bf16[256,256]{1,0:T(8,128)(2,1)S(1)} collective-permute-done((bf16[256,256]{1,0:T(8,128)(2,1)S(1)}, bf16[256,256]{1,0:T(8,128)(2,1)S(1)}, u32[]{:S(2)}, u32[]{:S(2)}) %collective-permute-start.4) | collective-permute-done | bytes 131104 | tf_op jit(solution)/shard_map/kv_first/ppermute | solution.py:33
  29.7 1.1 %collective-permute-start.5 = (bf16[512,256]{1,0:T(8,128)(2,1)S(1)}, bf16[512,256]{1,0:T(8,128)(2,1)S(1)}, u32[]{:S(2)}, u32[]{:S(2)}) collective-permute-start(bf16[512,256]{1,0:T(8,128)(2,1)S(1)} %constant_dynamic-update-slice_fusion.refs_4_), channel_id=1, source_target_pairs={{0,1},{1,2},{2,3},{3,0},{4,5},{5,6},{6,7},{7,4},{8,9},{9,10},{10,1... | collective-permute-start | bytes 786440 | tf_op jit(solution)/shard_map/kv_second/ppermute | solution.py:33
  30.8 0.3 collective-permute-done.8
  31.1 1.0 %collective-permute-start.9 = (bf16[512,256]{1,0:T(8,128)(2,1)S(1)}, bf16[512,256]{1,0:T(8,128)(2,1)S(1)}, u32[]{:S(2)}, u32[]{:S(2)}) collective-permute-start(bf16[512,256]{1,0:T(8,128)(2,1)S(1)} %constant_dynamic-update-slice_fusion.2.refs_3_), channel_id=1, source_target_pairs={{0,1},{1,2},{2,3},{3,0},{4,5},{5,6},{6,7},{7,4},{8,9},{9,10},{10,1... | collective-permute-start | bytes 786440 | tf_op jit(solution)/shard_map/kv_second/ppermute | solution.py:33
  32.1 1.8 %collective-permute-start.11 = (bf16[512,256]{1,0:T(8,128)(2,1)S(1)}, bf16[512,256]{1,0:T(8,128)(2,1)S(1)}, u32[]{:S(2)}, u32[]{:S(2)}) collective-permute-start(bf16[512,256]{1,0:T(8,128)(2,1)S(1)} %constant_dynamic-update-slice_fusion.refs_4_), channel_id=1, source_target_pairs={{0,3},{1,0},{2,1},{3,2},{4,7},{5,4},{6,5},{7,6},{8,11},{9,8},{10,9... | collective-permute-start | bytes 786440 | tf_op jit(solution)/shard_map/kv_second/ppermute | solution.py:33
  33.9 1.0 %collective-permute-start.13 = (bf16[512,256]{1,0:T(8,128)(2,1)S(1)}, bf16[512,256]{1,0:T(8,128)(2,1)S(1)}, u32[]{:S(2)}, u32[]{:S(2)}) collective-permute-start(bf16[512,256]{1,0:T(8,128)(2,1)S(1)} %constant_dynamic-update-slice_fusion.2.refs_3_), channel_id=1, source_target_pairs={{0,3},{1,0},{2,1},{3,2},{4,7},{5,4},{6,5},{7,6},{8,11},{9,8},{10,9... | collective-permute-start | bytes 786440 | tf_op jit(solution)/shard_map/kv_second/ppermute | solution.py:33
  34.9 0.0 collective-permute-done.6.refs_1_
  34.9 1.7 %collective-permute-done.5.refs_6_ = bf16[512,256]{1,0:T(8,128)(2,1)S(1)} collective-permute-done((bf16[512,256]{1,0:T(8,128)(2,1)S(1)}, bf16[512,256]{1,0:T(8,128)(2,1)S(1)}, u32[]{:S(2)}, u32[]{:S(2)}) %collective-permute-start.5) | collective-permute-done | bytes 262176 | tf_op jit(solution)/shard_map/kv_second/ppermute | solution.py:33
  36.5 2.3 %collective-permute-start.7 = (bf16[256,512]{1,0:T(8,128)(2,1)S(1)}, bf16[256,512]{1,0:T(8,128)(2,1)S(1)}, u32[]{:S(2)}, u32[]{:S(2)}) collective-permute-start(bf16[256,512]{1,0:T(8,128)(2,1)S(1)} %collective-permute-done.6.refs_1_), channel_id=1, source_target_pairs={{0,32},{1,33},{2,34},{3,35},{4,36},{5,37},{6,38},{7,39},{8,40},{9,... | collective-permute-start | bytes 786440 | tf_op jit(solution)/shard_map/q_other/ppermute | solution.py:33
  38.8 0.5 collective-permute-done.9.refs_5_
  39.3 0.0 collective-permute-start.10
  39.3 2.7 %collective-permute-start.12 = (bf16[512,256]{1,0:T(8,128)(2,1)S(1)}, bf16[512,256]{1,0:T(8,128)(2,1)S(1)}, u32[]{:S(2)}, u32[]{:S(2)}) collective-permute-start(bf16[512,256]{1,0:T(8,128)(2,1)S(1)} %collective-permute-done.11.refs_8_), channel_id=1, source_target_pairs={{0,3},{1,0},{2,1},{3,2},{4,7},{5,4},{6,5},{7,6},{8,11},{9,8},{10,9... | collective-permute-start | bytes 786440 | tf_op jit(solution)/shard_map/kv_second/ppermute | solution.py:33
  42.0 0.0 collective-permute-done.13.refs_7_
  42.0 0.0 collective-permute-done.7.refs_2_
  42.0 5.6 %flash.3 = (f32[8,256,128]{2,1,0:T(8,128)S(1)}, f32[2,256,128]{2,1,0:T(8,128)S(1)}) custom-call(s32[440]{0:T(512)S(1)} %plan.1.refs_0_, bf16[256,512]{1,0:T(8,128)(2,1)S(1)} %collective-permute-done.6.refs_1_, bf16[256,512]{1,0:T(8,128)(2,1)S(1)} %collective-permute-done.7.refs_2_, bf16[512,256]{1,0:T(8,128)(2,1)S(1)} %constant_dynamic-update-slice_fusion.2.refs_3_, ...), custom_call_target="tpu_custom_call" | custom-call | flops 805306368 | bytes 1572864 | tf_op jit(solution)/shard_map/attend_far/flash/pallas_call | solution.py:400
  47.7 0.0 collective-permute-done.10.refs_3_.refs_9_
  47.7 3.2 %flash.4 = (f32[256,640]{1,0:T(8,128)S(1)}, bf16[256,640]{1,0:T(8,128)(2,1)S(1)}) custom-call(s32[440]{0:T(512)S(1)} %plan.1.refs_0_, bf16[256,512]{1,0:T(8,128)(2,1)S(1)} %collective-permute-done.6.refs_1_, bf16[256,512]{1,0:T(8,128)(2,1)S(1)} %collective-permute-done.7.refs_2_, bf16[512,256]{1,0:T(8,128)(2,1)S(1)} %collective-permute-done.10.refs_3_.refs_9_, ...), custom_call_target="tpu_custom_call" | custom-call | flops 268435456 | bytes 524288 | tf_op jit(solution)/shard_map/attend_far/flash/pallas_call | solution.py:400
  50.9 3.0 %collective-permute-start.14 = (bf16[256,640]{1,0:T(8,128)(2,1)S(1)}, bf16[256,640]{1,0:T(8,128)(2,1)S(1)}, u32[]{:S(2)}, u32[]{:S(2)}) collective-permute-start(bf16[256,640]{1,0:T(8,128)(2,1)S(1)} %get-tuple-element.40), channel_id=1, source_target_pairs={{0,32},{1,33},{2,34},{3,35},{4,36},{5,37},{6,38},{7,39},{8,40},{9,... | collective-permute-start | bytes 983048 | tf_op jit(solution)/shard_map/merge_far/ppermute | solution.py:33
  53.9 0.1 collective-permute-start.15
  54.0 1.2 %collective-permute-done.14.refs_1_ = bf16[256,640]{1,0:T(8,128)(2,1)S(1)} collective-permute-done((bf16[256,640]{1,0:T(8,128)(2,1)S(1)}, bf16[256,640]{1,0:T(8,128)(2,1)S(1)}, u32[]{:S(2)}, u32[]{:S(2)}) %collective-permute-start.14) | collective-permute-done | bytes 327712 | tf_op jit(solution)/shard_map/merge_far/ppermute | solution.py:33
  55.2 0.6 merge.2
  55.8 0.3 collective-permute-start.16
  56.2 0.0 collective-permute-done.15.refs_2_
  56.2 6.5 %flash.5 = (f32[256,640]{1,0:T(8,128)S(1)}, bf16[256,640]{1,0:T(8,128)(2,1)S(1)}) custom-call(s32[440]{0:T(512)S(1)} %plan.1.refs_0_, bf16[256,512]{1,0:T(8,128)(2,1)S(1)} %get-tuple-element.42.refs_1_, bf16[256,512]{1,0:T(8,128)(2,1)S(1)} %collective-permute-done.15.refs_2_, bf16[512,256]{1,0:T(8,128)(2,1)S(1)} %constant_dynamic-update-slice_fusion.2.refs_3_, ...), custom_call_target="tpu_custom_call" | custom-call | flops 25769803776 | bytes 2097152 | tf_op jit(solution)/shard_map/attend_own/flash/pallas_call | solution.py:400
  62.7 2.3 %collective-permute-done.16.refs_2_ = bf16[256,640]{1,0:T(8,128)(2,1)S(1)} collective-permute-done((bf16[256,640]{1,0:T(8,128)(2,1)S(1)}, bf16[256,640]{1,0:T(8,128)(2,1)S(1)}, u32[]{:S(2)}, u32[]{:S(2)}) %collective-permute-start.16) | collective-permute-done | bytes 327712 | tf_op jit(solution)/shard_map/merge_far/ppermute | solution.py:33
  65.1 1.2 %collective-permute-start.17 = (bf16[256,640]{1,0:T(8,128)(2,1)S(1)}, bf16[256,640]{1,0:T(8,128)(2,1)S(1)}, u32[]{:S(2)}, u32[]{:S(2)}) collective-permute-start(bf16[256,640]{1,0:T(8,128)(2,1)S(1)} %get-tuple-element.46), channel_id=1, source_target_pairs={{0,32},{1,33},{2,34},{3,35},{4,36},{5,37},{6,38},{7,39},{8,40},{9,... | collective-permute-start | bytes 983048 | tf_op jit(solution)/shard_map/merge_own/ppermute | solution.py:33
  66.3 1.3 %collective-permute-done.17.refs_1_ = bf16[256,640]{1,0:T(8,128)(2,1)S(1)} collective-permute-done((bf16[256,640]{1,0:T(8,128)(2,1)S(1)}, bf16[256,640]{1,0:T(8,128)(2,1)S(1)}, u32[]{:S(2)}, u32[]{:S(2)}) %collective-permute-start.17) | collective-permute-done | bytes 327712 | tf_op jit(solution)/shard_map/merge_own/ppermute | solution.py:33
  67.5 1.1 %merge.3 = (bf16[64,512]{1,0:T(8,128)(2,1)S(1)}, bf16[64,512]{1,0:T(8,128)(2,1)S(1)}, bf16[64,512]{1,0:T(8,128)(2,1)S(1)}, bf16[64,512]{1,0:T(8,128)(2,1)S(1)}) custom-call(f32[256,640]{1,0:T(8,128)S(1)} %get-tuple-element.44.refs_0_, bf16[256,640]{1,0:T(8,128)(2,1)S(1)} %collective-permute-done.17.refs_1_, bf16[256,640]{1,0:T(8,128)(2,1)S(1)} %collective-permute-done.16.refs_2_), custom_call_target="tpu_custom_call" | custom-call | tf_op jit(solution)/shard_map/merge_own/merge/pallas_call | solution.py:455
  68.6 1.4 %collective-permute-start.18 = (bf16[64,512]{1,0:T(8,128)(2,1)S(1)}, bf16[64,512]{1,0:T(8,128)(2,1)S(1)}, u32[]{:S(2)}, u32[]{:S(2)}) collective-permute-start(bf16[64,512]{1,0:T(8,128)(2,1)S(1)} %get-tuple-element.48), channel_id=1, source_target_pairs={{0,64},{1,65},{2,66},{3,67},{4,68},{5,69},{6,70},{7,71},{8,72},{9,... | collective-permute-start | bytes 196616 | tf_op jit(solution)/shard_map/out_heads/ppermute | solution.py:33
  70.1 4.1 %collective-permute-start.19 = (bf16[64,512]{1,0:T(8,128)(2,1)S(1)}, bf16[64,512]{1,0:T(8,128)(2,1)S(1)}, u32[]{:S(2)}, u32[]{:S(2)}) collective-permute-start(bf16[64,512]{1,0:T(8,128)(2,1)S(1)} %get-tuple-element.49), channel_id=1, source_target_pairs={{0,128},{1,129},{2,130},{3,131},{4,132},{5,133},{6,134},{7,135},{8... | collective-permute-start | bytes 196616 | tf_op jit(solution)/shard_map/out_heads/ppermute | solution.py:33
  74.1 2.1 %collective-permute-start.20 = (bf16[64,512]{1,0:T(8,128)(2,1)S(1)}, bf16[64,512]{1,0:T(8,128)(2,1)S(1)}, u32[]{:S(2)}, u32[]{:S(2)}) collective-permute-start(bf16[64,512]{1,0:T(8,128)(2,1)S(1)} %get-tuple-element.50), channel_id=1, source_target_pairs={{0,192},{1,193},{2,194},{3,195},{4,196},{5,197},{6,198},{7,199},{8... | collective-permute-start | bytes 196616 | tf_op jit(solution)/shard_map/out_heads/ppermute | solution.py:33
  76.3 2.7 %collective-permute-done.19.refs_2_ = bf16[64,512]{1,0:T(8,128)(2,1)S(1)} collective-permute-done((bf16[64,512]{1,0:T(8,128)(2,1)S(1)}, bf16[64,512]{1,0:T(8,128)(2,1)S(1)}, u32[]{:S(2)}, u32[]{:S(2)}) %collective-permute-start.19) | collective-permute-done | bytes 65568 | tf_op jit(solution)/shard_map/out_heads/ppermute | solution.py:33
  78.9 2.4 %collective-permute-done.20.refs_3_ = bf16[64,512]{1,0:T(8,128)(2,1)S(1)} collective-permute-done((bf16[64,512]{1,0:T(8,128)(2,1)S(1)}, bf16[64,512]{1,0:T(8,128)(2,1)S(1)}, u32[]{:S(2)}, u32[]{:S(2)}) %collective-permute-start.20) | collective-permute-done | bytes 65568 | tf_op jit(solution)/shard_map/out_heads/ppermute | solution.py:33
  81.3 0.7 finish.1
  (17 shorter events, 0.1 us)
Async XLA Ops:
  0.0 13.3 %copy-start.3 = (s32[32,512]{1,0:T(8,128)S(1)}, s32[32,512]{1,0:T(8,128)}, u32[]{:S(2)}) copy-start(s32[32,512]{1,0:T(8,128)} %pos_hbm.1) | copy-start | bytes 196612
  0.0 13.3 %copy-start.4 = (s32[32,512]{1,0:T(8,128)S(1)}, s32[32,512]{1,0:T(8,128)}, u32[]{:S(2)}) copy-start(s32[32,512]{1,0:T(8,128)} %seg_hbm.1) | copy-start | bytes 196612
  0.0 21.2 %copy-start = (bf16[1,64,2048]{2,1,0:T(8,128)(2,1)S(1)}, bf16[1,64,2048]{2,1,0:T(8,128)(2,1)}, u32[]{:S(2)}) copy-start(bf16[1,64,2048]{2,1,0:T(8,128)(2,1)} %param.5) | copy-start | bytes 786436
  1.9 14.3 %collective-permute-start = (bf16[64,768]{1,0:T(8,128)(2,1)}, bf16[64,768]{1,0:T(8,128)(2,1)S(1)}, u32[]{:S(2)}, u32[]{:S(2)}) collective-permute-start(bf16[64,768]{1,0:T(8,128)(2,1)} %get-tuple-element.28), channel_id=1, source_target_pairs={{0,64},{1,65},{2,66},{3,67},{4,68},{5,69},{6,70},{7,71},{8,72},{9,... | collective-permute-start | bytes 294920 | tf_op jit(solution)/shard_map/heads/ppermute | solution.py:33
  5.8 11.5 %collective-permute-start.1 = (bf16[64,768]{1,0:T(8,128)(2,1)}, bf16[64,768]{1,0:T(8,128)(2,1)S(1)}, u32[]{:S(2)}, u32[]{:S(2)}) collective-permute-start(bf16[64,768]{1,0:T(8,128)(2,1)} %get-tuple-element.29), channel_id=1, source_target_pairs={{0,128},{1,129},{2,130},{3,131},{4,132},{5,133},{6,134},{7,135},{8... | collective-permute-start | bytes 294920 | tf_op jit(solution)/shard_map/heads/ppermute | solution.py:33
  10.9 10.3 %copy-start.1 = (bf16[1,64,512]{2,1,0:T(8,128)(2,1)S(1)}, bf16[1,64,512]{2,1,0:T(8,128)(2,1)}, u32[]{:S(2)}) copy-start(bf16[1,64,512]{2,1,0:T(8,128)(2,1)} %param.6) | copy-start | bytes 196612
  10.9 10.3 %copy-start.2 = (bf16[1,64,512]{2,1,0:T(8,128)(2,1)S(1)}, bf16[1,64,512]{2,1,0:T(8,128)(2,1)}, u32[]{:S(2)}) copy-start(bf16[1,64,512]{2,1,0:T(8,128)(2,1)} %param.7) | copy-start | bytes 196612
  10.9 10.3 %collective-permute-start.2 = (bf16[64,768]{1,0:T(8,128)(2,1)}, bf16[64,768]{1,0:T(8,128)(2,1)S(1)}, u32[]{:S(2)}, u32[]{:S(2)}) collective-permute-start(bf16[64,768]{1,0:T(8,128)(2,1)} %get-tuple-element.30), channel_id=1, source_target_pairs={{0,192},{1,193},{2,194},{3,195},{4,196},{5,197},{6,198},{7,199},{8... | collective-permute-start | bytes 294920 | tf_op jit(solution)/shard_map/heads/ppermute | solution.py:33
  21.3 6.1 %collective-permute-start.3 = (bf16[256,256]{1,0:T(8,128)(2,1)S(1)}, bf16[256,256]{1,0:T(8,128)(2,1)S(1)}, u32[]{:S(2)}, u32[]{:S(2)}) collective-permute-start(bf16[256,256]{1,0:T(8,128)(2,1)S(1)} %get-tuple-element.34), channel_id=1, source_target_pairs={{0,12},{1,13},{2,14},{3,15},{4,0},{5,1},{6,2},{7,3},{8,4},{9,5},{1... | collective-permute-start | bytes 393224 | tf_op jit(solution)/shard_map/kv_first/ppermute | solution.py:33
  24.1 5.6 %collective-permute-start.4 = (bf16[256,256]{1,0:T(8,128)(2,1)S(1)}, bf16[256,256]{1,0:T(8,128)(2,1)S(1)}, u32[]{:S(2)}, u32[]{:S(2)}) collective-permute-start(bf16[256,256]{1,0:T(8,128)(2,1)S(1)} %get-tuple-element.34), channel_id=1, source_target_pairs={{0,8},{1,9},{2,10},{3,11},{4,12},{5,13},{6,14},{7,15},{8,0},{9,1},... | collective-permute-start | bytes 393224 | tf_op jit(solution)/shard_map/kv_first/ppermute | solution.py:33
  24.5 6.7 %collective-permute-start.8 = (bf16[256,256]{1,0:T(8,128)(2,1)S(1)}, bf16[256,256]{1,0:T(8,128)(2,1)S(1)}, u32[]{:S(2)}, u32[]{:S(2)}) collective-permute-start(bf16[256,256]{1,0:T(8,128)(2,1)S(1)} %get-tuple-element.34), channel_id=1, source_target_pairs={{0,4},{1,5},{2,6},{3,7},{4,8},{5,9},{6,10},{7,11},{8,12},{9,13},{1... | collective-permute-start | bytes 393224 | tf_op jit(solution)/shard_map/kv_first/ppermute | solution.py:33
  25.2 9.6 %collective-permute-start.6 = (bf16[256,512]{1,0:T(8,128)(2,1)S(1)}, bf16[256,512]{1,0:T(8,128)(2,1)S(1)}, u32[]{:S(2)}, u32[]{:S(2)}) collective-permute-start(bf16[256,512]{1,0:T(8,128)(2,1)S(1)} %get-tuple-element.42.refs_1_), channel_id=1, source_target_pairs={{0,16},{1,17},{2,18},{3,19},{4,20},{5,21},{6,22},{7,23},{8,24},{9,... | collective-permute-start | bytes 786440 | tf_op jit(solution)/shard_map/q_other/ppermute | solution.py:33
  29.7 6.8 %collective-permute-start.5 = (bf16[512,256]{1,0:T(8,128)(2,1)S(1)}, bf16[512,256]{1,0:T(8,128)(2,1)S(1)}, u32[]{:S(2)}, u32[]{:S(2)}) collective-permute-start(bf16[512,256]{1,0:T(8,128)(2,1)S(1)} %constant_dynamic-update-slice_fusion.refs_4_), channel_id=1, source_target_pairs={{0,1},{1,2},{2,3},{3,0},{4,5},{5,6},{6,7},{7,4},{8,9},{9,10},{10,1... | collective-permute-start | bytes 786440 | tf_op jit(solution)/shard_map/kv_second/ppermute | solution.py:33
  31.1 8.2 %collective-permute-start.9 = (bf16[512,256]{1,0:T(8,128)(2,1)S(1)}, bf16[512,256]{1,0:T(8,128)(2,1)S(1)}, u32[]{:S(2)}, u32[]{:S(2)}) collective-permute-start(bf16[512,256]{1,0:T(8,128)(2,1)S(1)} %constant_dynamic-update-slice_fusion.2.refs_3_), channel_id=1, source_target_pairs={{0,1},{1,2},{2,3},{3,0},{4,5},{5,6},{6,7},{7,4},{8,9},{9,10},{10,1... | collective-permute-start | bytes 786440 | tf_op jit(solution)/shard_map/kv_second/ppermute | solution.py:33
  32.1 7.2 %collective-permute-start.11 = (bf16[512,256]{1,0:T(8,128)(2,1)S(1)}, bf16[512,256]{1,0:T(8,128)(2,1)S(1)}, u32[]{:S(2)}, u32[]{:S(2)}) collective-permute-start(bf16[512,256]{1,0:T(8,128)(2,1)S(1)} %constant_dynamic-update-slice_fusion.refs_4_), channel_id=1, source_target_pairs={{0,3},{1,0},{2,1},{3,2},{4,7},{5,4},{6,5},{7,6},{8,11},{9,8},{10,9... | collective-permute-start | bytes 786440 | tf_op jit(solution)/shard_map/kv_second/ppermute | solution.py:33
  33.9 8.1 %collective-permute-start.13 = (bf16[512,256]{1,0:T(8,128)(2,1)S(1)}, bf16[512,256]{1,0:T(8,128)(2,1)S(1)}, u32[]{:S(2)}, u32[]{:S(2)}) collective-permute-start(bf16[512,256]{1,0:T(8,128)(2,1)S(1)} %constant_dynamic-update-slice_fusion.2.refs_3_), channel_id=1, source_target_pairs={{0,3},{1,0},{2,1},{3,2},{4,7},{5,4},{6,5},{7,6},{8,11},{9,8},{10,9... | collective-permute-start | bytes 786440 | tf_op jit(solution)/shard_map/kv_second/ppermute | solution.py:33
  36.5 5.5 %collective-permute-start.7 = (bf16[256,512]{1,0:T(8,128)(2,1)S(1)}, bf16[256,512]{1,0:T(8,128)(2,1)S(1)}, u32[]{:S(2)}, u32[]{:S(2)}) collective-permute-start(bf16[256,512]{1,0:T(8,128)(2,1)S(1)} %collective-permute-done.6.refs_1_), channel_id=1, source_target_pairs={{0,32},{1,33},{2,34},{3,35},{4,36},{5,37},{6,38},{7,39},{8,40},{9,... | collective-permute-start | bytes 786440 | tf_op jit(solution)/shard_map/q_other/ppermute | solution.py:33
  39.3 8.3 %collective-permute-start.10 = (bf16[512,256]{1,0:T(8,128)(2,1)S(1)}, bf16[512,256]{1,0:T(8,128)(2,1)S(1)}, u32[]{:S(2)}, u32[]{:S(2)}) collective-permute-start(bf16[512,256]{1,0:T(8,128)(2,1)S(1)} %collective-permute-done.9.refs_5_), channel_id=1, source_target_pairs={{0,1},{1,2},{2,3},{3,0},{4,5},{5,6},{6,7},{7,4},{8,9},{9,10},{10,1... | collective-permute-start | bytes 786440 | tf_op jit(solution)/shard_map/kv_second/ppermute | solution.py:33
  39.3 8.3 %collective-permute-start.12 = (bf16[512,256]{1,0:T(8,128)(2,1)S(1)}, bf16[512,256]{1,0:T(8,128)(2,1)S(1)}, u32[]{:S(2)}, u32[]{:S(2)}) collective-permute-start(bf16[512,256]{1,0:T(8,128)(2,1)S(1)} %collective-permute-done.11.refs_8_), channel_id=1, source_target_pairs={{0,3},{1,0},{2,1},{3,2},{4,7},{5,4},{6,5},{7,6},{8,11},{9,8},{10,9... | collective-permute-start | bytes 786440 | tf_op jit(solution)/shard_map/kv_second/ppermute | solution.py:33
  50.9 4.3 %collective-permute-start.14 = (bf16[256,640]{1,0:T(8,128)(2,1)S(1)}, bf16[256,640]{1,0:T(8,128)(2,1)S(1)}, u32[]{:S(2)}, u32[]{:S(2)}) collective-permute-start(bf16[256,640]{1,0:T(8,128)(2,1)S(1)} %get-tuple-element.40), channel_id=1, source_target_pairs={{0,32},{1,33},{2,34},{3,35},{4,36},{5,37},{6,38},{7,39},{8,40},{9,... | collective-permute-start | bytes 983048 | tf_op jit(solution)/shard_map/merge_far/ppermute | solution.py:33
  53.9 2.2 %collective-permute-start.15 = (bf16[256,512]{1,0:T(8,128)(2,1)S(1)}, bf16[256,512]{1,0:T(8,128)(2,1)S(1)}, u32[]{:S(2)}, u32[]{:S(2)}) collective-permute-start(bf16[256,512]{1,0:T(8,128)(2,1)S(1)} %get-tuple-element.42.refs_1_), channel_id=1, source_target_pairs={{0,32},{1,33},{2,34},{3,35},{4,36},{5,37},{6,38},{7,39},{8,40},{9,... | collective-permute-start | bytes 786440 | tf_op jit(solution)/shard_map/q_other/ppermute | solution.py:33
  55.8 9.2 %collective-permute-start.16 = (bf16[256,640]{1,0:T(8,128)(2,1)S(1)}, bf16[256,640]{1,0:T(8,128)(2,1)S(1)}, u32[]{:S(2)}, u32[]{:S(2)}) collective-permute-start(bf16[256,640]{1,0:T(8,128)(2,1)S(1)} %merge.2), channel_id=1, source_target_pairs={{0,16},{1,17},{2,18},{3,19},{4,20},{5,21},{6,22},{7,23},{8,24},{9,... | collective-permute-start | bytes 983048 | tf_op jit(solution)/shard_map/merge_far/ppermute | solution.py:33
  65.1 2.5 %collective-permute-start.17 = (bf16[256,640]{1,0:T(8,128)(2,1)S(1)}, bf16[256,640]{1,0:T(8,128)(2,1)S(1)}, u32[]{:S(2)}, u32[]{:S(2)}) collective-permute-start(bf16[256,640]{1,0:T(8,128)(2,1)S(1)} %get-tuple-element.46), channel_id=1, source_target_pairs={{0,32},{1,33},{2,34},{3,35},{4,36},{5,37},{6,38},{7,39},{8,40},{9,... | collective-permute-start | bytes 983048 | tf_op jit(solution)/shard_map/merge_own/ppermute | solution.py:33
  68.6 7.6 %collective-permute-start.18 = (bf16[64,512]{1,0:T(8,128)(2,1)S(1)}, bf16[64,512]{1,0:T(8,128)(2,1)S(1)}, u32[]{:S(2)}, u32[]{:S(2)}) collective-permute-start(bf16[64,512]{1,0:T(8,128)(2,1)S(1)} %get-tuple-element.48), channel_id=1, source_target_pairs={{0,64},{1,65},{2,66},{3,67},{4,68},{5,69},{6,70},{7,71},{8,72},{9,... | collective-permute-start | bytes 196616 | tf_op jit(solution)/shard_map/out_heads/ppermute | solution.py:33
  70.1 8.8 %collective-permute-start.19 = (bf16[64,512]{1,0:T(8,128)(2,1)S(1)}, bf16[64,512]{1,0:T(8,128)(2,1)S(1)}, u32[]{:S(2)}, u32[]{:S(2)}) collective-permute-start(bf16[64,512]{1,0:T(8,128)(2,1)S(1)} %get-tuple-element.49), channel_id=1, source_target_pairs={{0,128},{1,129},{2,130},{3,131},{4,132},{5,133},{6,134},{7,135},{8... | collective-permute-start | bytes 196616 | tf_op jit(solution)/shard_map/out_heads/ppermute | solution.py:33
  74.1 7.2 %collective-permute-start.20 = (bf16[64,512]{1,0:T(8,128)(2,1)S(1)}, bf16[64,512]{1,0:T(8,128)(2,1)S(1)}, u32[]{:S(2)}, u32[]{:S(2)}) collective-permute-start(bf16[64,512]{1,0:T(8,128)(2,1)S(1)} %get-tuple-element.50), channel_id=1, source_target_pairs={{0,192},{1,193},{2,194},{3,195},{4,196},{5,197},{6,198},{7,199},{8... | collective-permute-start | bytes 196616 | tf_op jit(solution)/shard_map/out_heads/ppermute | solution.py:33

commit v3 on v2

--- a/solution.py
+++ b/solution.py
@@ -133,7 +133,7 @@
     ]
 
 
-CALLS = ((1, 0, 12, 1), (1, 12, 4, 1), (0, 0, 16, 24))
+CALLS = ((1, 0, 12, 1, False), (1, 12, 4, 1, True), (0, 0, 16, 24, False))
 PLAN = 72
 Q_AT = 2 * len(CALLS) * PLAN
 CORE_AT = Q_AT + 4
@@ -175,7 +175,7 @@
             qb = first_ref[hf, (block + 16 * whose) % 32, 0]
             plan[Q_AT + whose * 2 + hf] = qb
             queries.append((qb, doc_start(plan, qb), doc_start(plan, qb + 255)))
-    for call, (whose, first, blocks, _) in enumerate(CALLS):
+    for call, (whose, first, blocks, _, carry) in enumerate(CALLS):
         counts = [[jnp.int32(0), jnp.int32(0)] for _ in range(2)]
         for k in range(first, first + blocks):
             s1, s2 = SHIFTS[k % 4], SHIFTS[k // 4]
@@ -189,7 +189,7 @@
                     qb, lo_first, lo_last = queries[whose * 2 + hf]
                     n_full, n_part = counts[hf]
                     seen = (kb <= qb) & (kb + 255 >= lo_first)
-                    whole = seen & (kb < qb) & (kb >= lo_last)
+                    whole = seen & (kb < qb) & (kb >= (lo_last if carry else lo_first))
                     plan[off + 2 + n_full] = entry
                     plan[off + 36 + n_part] = entry
                     counts[hf][0] = n_full + jnp.where(whole, 1, 0)
@@ -346,6 +346,16 @@
 
         q_pos = qb + q_off
         q_lo = doc_start(meta, q_pos)
+        if not carry:
+
+            @pl.when(doc_start(meta, qb + 255) > doc_start(meta, qb))
+            def forget():
+                keep = q_lo <= qb
+                for h in range(4):
+                    i = hf * 4 + h
+                    m_s[i] = jnp.where(keep, m_s[i], MASKED)
+                    l_s[i] = jnp.where(keep, l_s[i], 0.0)
+                    acc[i] = jnp.where(keep, acc[i], 0.0)
 
         def part_pair(j, _):
             there = 2 * j + 1 < n_part

time: 81.3 us -> 83.9 us (1.032)
  the two profiles are of different devices: /device:TPU:1 before, /device:TPU:8 now
where the time goes in v3:
time: 83.9 us; the launch traced here: 84.3 us
  starting transfers between devices  38.1 us (45%)
  Pallas kernels  25.1 us (30%)
  waiting for transfers between devices  20.9 us (25%)
    ppermute x21, starting transfers between devices, send(): return lax.ppermute(a, AXES, pairs)  38.1 us
    ppermute x21, waiting for transfers between devices, send(): return lax.ppermute(a, AXES, pairs)  20.9 us
    pallas_call x3, Pallas kernels, flash(): pl.pallas_call(functools.partial(flash_kernel, rows, call, carry, final),...  17.8 us
    pallas_call x1, Pallas kernels, make_plan(): pl.pallas_call(plan_kernel, out_shape=jax.ShapeDtypeStruct((EDGE_AT + 3,)...  2.88 us
    pallas_call x1, Pallas kernels, pack(): pl.pallas_call(pack_kernel, out_shape=[jax.ShapeDtypeStruct((64, width),...  1.83 us
    pallas_call x2, Pallas kernels, merge(): pl.pallas_call(functools.partial(merge_kernel, len(partials)), out_shape=...  1.74 us
  transfers between devices with their start and end apart: 21, of which 10 were waited for; matrix products, arithmetic and copies ran while one was open for 0% of the time, Pallas kernels for 21%

profile of v3, /device:TPU:8, one launch (start us, length us, event | category | flops | bytes accessed | tf_op | source)
XLA Modules:
  0.0 84.3 jit_solution(9028070329690989391)
XLA Ops:
  0.0 1.8 %pack.1 = (bf16[64,768]{1,0:T(8,128)(2,1)}, bf16[64,768]{1,0:T(8,128)(2,1)}, bf16[64,768]{1,0:T(8,128)(2,1)}) custom-call(bf16[64,512]{1,0:T(8,128)(2,1)} %bitcast.6, bf16[64,512]{1,0:T(8,128)(2,1)} %bitcast.8, bf16[64,2048]{1,0:T(8,128)(2,1)} %bitcast.4), custom_call_target="tpu_custom_call" | custom-call | tf_op jit(solution)/shard_map/heads/pack/pallas_call | solution.py:75
  1.9 3.3 %collective-permute-start = (bf16[64,768]{1,0:T(8,128)(2,1)}, bf16[64,768]{1,0:T(8,128)(2,1)S(1)}, u32[]{:S(2)}, u32[]{:S(2)}) collective-permute-start(bf16[64,768]{1,0:T(8,128)(2,1)} %get-tuple-element.28), channel_id=1, source_target_pairs={{0,64},{1,65},{2,66},{3,67},{4,68},{5,69},{6,70},{7,71},{8,72},{9,... | collective-permute-start | bytes 294920 | tf_op jit(solution)/shard_map/heads/ppermute | solution.py:33
  5.2 5.4 %collective-permute-start.1 = (bf16[64,768]{1,0:T(8,128)(2,1)}, bf16[64,768]{1,0:T(8,128)(2,1)S(1)}, u32[]{:S(2)}, u32[]{:S(2)}) collective-permute-start(bf16[64,768]{1,0:T(8,128)(2,1)} %get-tuple-element.29), channel_id=1, source_target_pairs={{0,128},{1,129},{2,130},{3,131},{4,132},{5,133},{6,134},{7,135},{8... | collective-permute-start | bytes 294920 | tf_op jit(solution)/shard_map/heads/ppermute | solution.py:33
  10.6 2.7 %collective-permute-start.2 = (bf16[64,768]{1,0:T(8,128)(2,1)}, bf16[64,768]{1,0:T(8,128)(2,1)S(1)}, u32[]{:S(2)}, u32[]{:S(2)}) collective-permute-start(bf16[64,768]{1,0:T(8,128)(2,1)} %get-tuple-element.30), channel_id=1, source_target_pairs={{0,192},{1,193},{2,194},{3,195},{4,196},{5,197},{6,198},{7,199},{8... | collective-permute-start | bytes 294920 | tf_op jit(solution)/shard_map/heads/ppermute | solution.py:33
  13.3 2.9 %plan.1.refs_0_ = s32[440]{0:T(512)S(1)} custom-call(s32[32,512]{1,0:T(8,128)S(1)} %copy-done.3, s32[32,512]{1,0:T(8,128)S(1)} %copy-done.4), custom_call_target="tpu_custom_call" | custom-call | tf_op jit(solution)/shard_map/heads/plan/pallas_call | solution.py:208
  16.2 0.0 collective-permute-done.refs_3_
  16.2 1.4 %collective-permute-done.1.refs_4_ = bf16[64,768]{1,0:T(8,128)(2,1)S(1)} collective-permute-done((bf16[64,768]{1,0:T(8,128)(2,1)}, bf16[64,768]{1,0:T(8,128)(2,1)S(1)}, u32[]{:S(2)}, u32[]{:S(2)}) %collective-permute-start.1) | collective-permute-done | bytes 98336 | tf_op jit(solution)/shard_map/heads/ppermute | solution.py:33
  17.6 2.6 %collective-permute-done.2.refs_5_ = bf16[64,768]{1,0:T(8,128)(2,1)S(1)} collective-permute-done((bf16[64,768]{1,0:T(8,128)(2,1)}, bf16[64,768]{1,0:T(8,128)(2,1)S(1)}, u32[]{:S(2)}, u32[]{:S(2)}) %collective-permute-start.2) | collective-permute-done | bytes 98336 | tf_op jit(solution)/shard_map/heads/ppermute | solution.py:33
  20.2 0.1 unpack.1
  20.3 2.8 %collective-permute-start.3 = (bf16[256,256]{1,0:T(8,128)(2,1)S(1)}, bf16[256,256]{1,0:T(8,128)(2,1)S(1)}, u32[]{:S(2)}, u32[]{:S(2)}) collective-permute-start(bf16[256,256]{1,0:T(8,128)(2,1)S(1)} %get-tuple-element.34), channel_id=1, source_target_pairs={{0,12},{1,13},{2,14},{3,15},{4,0},{5,1},{6,2},{7,3},{8,4},{9,5},{1... | collective-permute-start | bytes 393224 | tf_op jit(solution)/shard_map/kv_first/ppermute | solution.py:33
  23.1 0.8 collective-permute-start.4
  23.9 1.0 %collective-permute-start.8 = (bf16[256,256]{1,0:T(8,128)(2,1)S(1)}, bf16[256,256]{1,0:T(8,128)(2,1)S(1)}, u32[]{:S(2)}, u32[]{:S(2)}) collective-permute-start(bf16[256,256]{1,0:T(8,128)(2,1)S(1)} %get-tuple-element.34), channel_id=1, source_target_pairs={{0,4},{1,5},{2,6},{3,7},{4,8},{5,9},{6,10},{7,11},{8,12},{9,13},{1... | collective-permute-start | bytes 393224 | tf_op jit(solution)/shard_map/kv_first/ppermute | solution.py:33
  24.9 0.0 collective-permute-start.6
  24.9 2.1 %collective-permute-done.3 = bf16[256,256]{1,0:T(8,128)(2,1)S(1)} collective-permute-done((bf16[256,256]{1,0:T(8,128)(2,1)S(1)}, bf16[256,256]{1,0:T(8,128)(2,1)S(1)}, u32[]{:S(2)}, u32[]{:S(2)}) %collective-permute-start.3) | collective-permute-done | bytes 131104 | tf_op jit(solution)/shard_map/kv_first/ppermute | solution.py:33
  27.0 2.6 %collective-permute-done.4 = bf16[256,256]{1,0:T(8,128)(2,1)S(1)} collective-permute-done((bf16[256,256]{1,0:T(8,128)(2,1)S(1)}, bf16[256,256]{1,0:T(8,128)(2,1)S(1)}, u32[]{:S(2)}, u32[]{:S(2)}) %collective-permute-start.4) | collective-permute-done | bytes 131104 | tf_op jit(solution)/shard_map/kv_first/ppermute | solution.py:33
  29.7 1.7 %collective-permute-start.5 = (bf16[512,256]{1,0:T(8,128)(2,1)S(1)}, bf16[512,256]{1,0:T(8,128)(2,1)S(1)}, u32[]{:S(2)}, u32[]{:S(2)}) collective-permute-start(bf16[512,256]{1,0:T(8,128)(2,1)S(1)} %constant_dynamic-update-slice_fusion.refs_4_), channel_id=1, source_target_pairs={{0,1},{1,2},{2,3},{3,0},{4,5},{5,6},{6,7},{7,4},{8,9},{9,10},{10,1... | collective-permute-start | bytes 786440 | tf_op jit(solution)/shard_map/kv_second/ppermute | solution.py:33
  31.3 0.0 collective-permute-done.8
  31.4 2.4 %collective-permute-start.9 = (bf16[512,256]{1,0:T(8,128)(2,1)S(1)}, bf16[512,256]{1,0:T(8,128)(2,1)S(1)}, u32[]{:S(2)}, u32[]{:S(2)}) collective-permute-start(bf16[512,256]{1,0:T(8,128)(2,1)S(1)} %constant_dynamic-update-slice_fusion.2.refs_3_), channel_id=1, source_target_pairs={{0,1},{1,2},{2,3},{3,0},{4,5},{5,6},{6,7},{7,4},{8,9},{9,10},{10,1... | collective-permute-start | bytes 786440 | tf_op jit(solution)/shard_map/kv_second/ppermute | solution.py:33
  33.8 0.0 collective-permute-start.11
  33.8 1.3 %collective-permute-start.13 = (bf16[512,256]{1,0:T(8,128)(2,1)S(1)}, bf16[512,256]{1,0:T(8,128)(2,1)S(1)}, u32[]{:S(2)}, u32[]{:S(2)}) collective-permute-start(bf16[512,256]{1,0:T(8,128)(2,1)S(1)} %constant_dynamic-update-slice_fusion.2.refs_3_), channel_id=1, source_target_pairs={{0,3},{1,0},{2,1},{3,2},{4,7},{5,4},{6,5},{7,6},{8,11},{9,8},{10,9... | collective-permute-start | bytes 786440 | tf_op jit(solution)/shard_map/kv_second/ppermute | solution.py:33
  35.1 0.0 collective-permute-done.6.refs_1_
  35.1 1.0 %collective-permute-done.5.refs_6_ = bf16[512,256]{1,0:T(8,128)(2,1)S(1)} collective-permute-done((bf16[512,256]{1,0:T(8,128)(2,1)S(1)}, bf16[512,256]{1,0:T(8,128)(2,1)S(1)}, u32[]{:S(2)}, u32[]{:S(2)}) %collective-permute-start.5) | collective-permute-done | bytes 262176 | tf_op jit(solution)/shard_map/kv_second/ppermute | solution.py:33
  36.1 0.0 collective-permute-start.7
  36.1 2.8 %collective-permute-done.9.refs_5_ = bf16[512,256]{1,0:T(8,128)(2,1)S(1)} collective-permute-done((bf16[512,256]{1,0:T(8,128)(2,1)S(1)}, bf16[512,256]{1,0:T(8,128)(2,1)S(1)}, u32[]{:S(2)}, u32[]{:S(2)}) %collective-permute-start.9) | collective-permute-done | bytes 262176 | tf_op jit(solution)/shard_map/kv_second/ppermute | solution.py:33
  38.9 1.6 %collective-permute-start.10 = (bf16[512,256]{1,0:T(8,128)(2,1)S(1)}, bf16[512,256]{1,0:T(8,128)(2,1)S(1)}, u32[]{:S(2)}, u32[]{:S(2)}) collective-permute-start(bf16[512,256]{1,0:T(8,128)(2,1)S(1)} %collective-permute-done.9.refs_5_), channel_id=1, source_target_pairs={{0,1},{1,2},{2,3},{3,0},{4,5},{5,6},{6,7},{7,4},{8,9},{9,10},{10,1... | collective-permute-start | bytes 786440 | tf_op jit(solution)/shard_map/kv_second/ppermute | solution.py:33
  40.5 0.0 collective-permute-done.11.refs_8_
  40.5 0.5 collective-permute-start.12
  41.0 2.0 %collective-permute-done.13.refs_7_ = bf16[512,256]{1,0:T(8,128)(2,1)S(1)} collective-permute-done((bf16[512,256]{1,0:T(8,128)(2,1)S(1)}, bf16[512,256]{1,0:T(8,128)(2,1)S(1)}, u32[]{:S(2)}, u32[]{:S(2)}) %collective-permute-start.13) | collective-permute-done | bytes 262176 | tf_op jit(solution)/shard_map/kv_second/ppermute | solution.py:33
  43.0 4.4 %flash.3 = (f32[8,256,128]{2,1,0:T(8,128)S(1)}, f32[2,256,128]{2,1,0:T(8,128)S(1)}) custom-call(s32[440]{0:T(512)S(1)} %plan.1.refs_0_, bf16[256,512]{1,0:T(8,128)(2,1)S(1)} %collective-permute-done.6.refs_1_, bf16[256,512]{1,0:T(8,128)(2,1)S(1)} %collective-permute-done.7.refs_2_, bf16[512,256]{1,0:T(8,128)(2,1)S(1)} %constant_dynamic-update-slice_fusion.2.refs_3_, ...), custom_call_target="tpu_custom_call" | custom-call | flops 805306368 | bytes 1572864 | tf_op jit(solution)/shard_map/attend_far/flash/pallas_call | solution.py:410
  47.4 0.0 collective-permute-done.12.refs_4_.refs_10_
  47.4 3.3 %flash.4 = (f32[256,640]{1,0:T(8,128)S(1)}, bf16[256,640]{1,0:T(8,128)(2,1)S(1)}) custom-call(s32[440]{0:T(512)S(1)} %plan.1.refs_0_, bf16[256,512]{1,0:T(8,128)(2,1)S(1)} %collective-permute-done.6.refs_1_, bf16[256,512]{1,0:T(8,128)(2,1)S(1)} %collective-permute-done.7.refs_2_, bf16[512,256]{1,0:T(8,128)(2,1)S(1)} %collective-permute-done.10.refs_3_.refs_9_, ...), custom_call_target="tpu_custom_call" | custom-call | flops 268435456 | bytes 524288 | tf_op jit(solution)/shard_map/attend_far/flash/pallas_call | solution.py:410
  50.7 0.1 collective-permute-start.14
  50.8 0.5 collective-permute-start.15
  51.3 1.1 %collective-permute-done.14.refs_1_ = bf16[256,640]{1,0:T(8,128)(2,1)S(1)} collective-permute-done((bf16[256,640]{1,0:T(8,128)(2,1)S(1)}, bf16[256,640]{1,0:T(8,128)(2,1)S(1)}, u32[]{:S(2)}, u32[]{:S(2)}) %collective-permute-start.14) | collective-permute-done | bytes 327712 | tf_op jit(solution)/shard_map/merge_far/ppermute | solution.py:33
  52.4 0.6 merge.2
  53.0 4.6 %collective-permute-start.16 = (bf16[256,640]{1,0:T(8,128)(2,1)S(1)}, bf16[256,640]{1,0:T(8,128)(2,1)S(1)}, u32[]{:S(2)}, u32[]{:S(2)}) collective-permute-start(bf16[256,640]{1,0:T(8,128)(2,1)S(1)} %merge.2), channel_id=1, source_target_pairs={{0,16},{1,17},{2,18},{3,19},{4,20},{5,21},{6,22},{7,23},{8,24},{9,... | collective-permute-start | bytes 983048 | tf_op jit(solution)/shard_map/merge_far/ppermute | solution.py:33
  57.6 0.0 collective-permute-done.15.refs_2_
  57.6 10.2 %flash.5 = (f32[256,640]{1,0:T(8,128)S(1)}, bf16[256,640]{1,0:T(8,128)(2,1)S(1)}) custom-call(s32[440]{0:T(512)S(1)} %plan.1.refs_0_, bf16[256,512]{1,0:T(8,128)(2,1)S(1)} %get-tuple-element.42.refs_1_, bf16[256,512]{1,0:T(8,128)(2,1)S(1)} %collective-permute-done.15.refs_2_, bf16[512,256]{1,0:T(8,128)(2,1)S(1)} %constant_dynamic-update-slice_fusion.2.refs_3_, ...), custom_call_target="tpu_custom_call" | custom-call | flops 25769803776 | bytes 2097152 | tf_op jit(solution)/shard_map/attend_own/flash/pallas_call | solution.py:410
  67.8 0.1 collective-permute-start.17
  67.9 1.6 %collective-permute-done.17.refs_1_ = bf16[256,640]{1,0:T(8,128)(2,1)S(1)} collective-permute-done((bf16[256,640]{1,0:T(8,128)(2,1)S(1)}, bf16[256,640]{1,0:T(8,128)(2,1)S(1)}, u32[]{:S(2)}, u32[]{:S(2)}) %collective-permute-start.17) | collective-permute-done | bytes 327712 | tf_op jit(solution)/shard_map/merge_own/ppermute | solution.py:33
  69.5 1.1 %merge.3 = (bf16[64,512]{1,0:T(8,128)(2,1)S(1)}, bf16[64,512]{1,0:T(8,128)(2,1)S(1)}, bf16[64,512]{1,0:T(8,128)(2,1)S(1)}, bf16[64,512]{1,0:T(8,128)(2,1)S(1)}) custom-call(f32[256,640]{1,0:T(8,128)S(1)} %get-tuple-element.44.refs_0_, bf16[256,640]{1,0:T(8,128)(2,1)S(1)} %collective-permute-done.17.refs_1_, bf16[256,640]{1,0:T(8,128)(2,1)S(1)} %collective-permute-done.16.refs_2_), custom_call_target="tpu_custom_call" | custom-call | tf_op jit(solution)/shard_map/merge_own/merge/pallas_call | solution.py:465
  70.7 4.4 %collective-permute-start.18 = (bf16[64,512]{1,0:T(8,128)(2,1)S(1)}, bf16[64,512]{1,0:T(8,128)(2,1)S(1)}, u32[]{:S(2)}, u32[]{:S(2)}) collective-permute-start(bf16[64,512]{1,0:T(8,128)(2,1)S(1)} %get-tuple-element.48), channel_id=1, source_target_pairs={{0,64},{1,65},{2,66},{3,67},{4,68},{5,69},{6,70},{7,71},{8,72},{9,... | collective-permute-start | bytes 196616 | tf_op jit(solution)/shard_map/out_heads/ppermute | solution.py:33
  75.1 1.5 %collective-permute-start.19 = (bf16[64,512]{1,0:T(8,128)(2,1)S(1)}, bf16[64,512]{1,0:T(8,128)(2,1)S(1)}, u32[]{:S(2)}, u32[]{:S(2)}) collective-permute-start(bf16[64,512]{1,0:T(8,128)(2,1)S(1)} %get-tuple-element.49), channel_id=1, source_target_pairs={{0,128},{1,129},{2,130},{3,131},{4,132},{5,133},{6,134},{7,135},{8... | collective-permute-start | bytes 196616 | tf_op jit(solution)/shard_map/out_heads/ppermute | solution.py:33
  76.6 3.4 %collective-permute-start.20 = (bf16[64,512]{1,0:T(8,128)(2,1)S(1)}, bf16[64,512]{1,0:T(8,128)(2,1)S(1)}, u32[]{:S(2)}, u32[]{:S(2)}) collective-permute-start(bf16[64,512]{1,0:T(8,128)(2,1)S(1)} %get-tuple-element.50), channel_id=1, source_target_pairs={{0,192},{1,193},{2,194},{3,195},{4,196},{5,197},{6,198},{7,199},{8... | collective-permute-start | bytes 196616 | tf_op jit(solution)/shard_map/out_heads/ppermute | solution.py:33
  80.0 0.0 collective-permute-done.18.refs_1_
  80.0 3.6 %collective-permute-done.19.refs_2_ = bf16[64,512]{1,0:T(8,128)(2,1)S(1)} collective-permute-done((bf16[64,512]{1,0:T(8,128)(2,1)S(1)}, bf16[64,512]{1,0:T(8,128)(2,1)S(1)}, u32[]{:S(2)}, u32[]{:S(2)}) %collective-permute-start.19) | collective-permute-done | bytes 65568 | tf_op jit(solution)/shard_map/out_heads/ppermute | solution.py:33
  83.6 0.0 collective-permute-done.20.refs_3_
  83.6 0.7 finish.1
  (17 shorter events, 0.1 us)
Async XLA Ops:
  0.0 13.3 %copy-start.3 = (s32[32,512]{1,0:T(8,128)S(1)}, s32[32,512]{1,0:T(8,128)}, u32[]{:S(2)}) copy-start(s32[32,512]{1,0:T(8,128)} %pos_hbm.1) | copy-start | bytes 196612
  0.0 13.3 %copy-start.4 = (s32[32,512]{1,0:T(8,128)S(1)}, s32[32,512]{1,0:T(8,128)}, u32[]{:S(2)}) copy-start(s32[32,512]{1,0:T(8,128)} %seg_hbm.1) | copy-start | bytes 196612
  0.0 20.2 %copy-start = (bf16[1,64,2048]{2,1,0:T(8,128)(2,1)S(1)}, bf16[1,64,2048]{2,1,0:T(8,128)(2,1)}, u32[]{:S(2)}) copy-start(bf16[1,64,2048]{2,1,0:T(8,128)(2,1)} %param.5) | copy-start | bytes 786436
  1.9 14.3 %collective-permute-start = (bf16[64,768]{1,0:T(8,128)(2,1)}, bf16[64,768]{1,0:T(8,128)(2,1)S(1)}, u32[]{:S(2)}, u32[]{:S(2)}) collective-permute-start(bf16[64,768]{1,0:T(8,128)(2,1)} %get-tuple-element.28), channel_id=1, source_target_pairs={{0,64},{1,65},{2,66},{3,67},{4,68},{5,69},{6,70},{7,71},{8,72},{9,... | collective-permute-start | bytes 294920 | tf_op jit(solution)/shard_map/heads/ppermute | solution.py:33
  5.2 12.4 %collective-permute-start.1 = (bf16[64,768]{1,0:T(8,128)(2,1)}, bf16[64,768]{1,0:T(8,128)(2,1)S(1)}, u32[]{:S(2)}, u32[]{:S(2)}) collective-permute-start(bf16[64,768]{1,0:T(8,128)(2,1)} %get-tuple-element.29), channel_id=1, source_target_pairs={{0,128},{1,129},{2,130},{3,131},{4,132},{5,133},{6,134},{7,135},{8... | collective-permute-start | bytes 294920 | tf_op jit(solution)/shard_map/heads/ppermute | solution.py:33
  10.6 9.6 %copy-start.1 = (bf16[1,64,512]{2,1,0:T(8,128)(2,1)S(1)}, bf16[1,64,512]{2,1,0:T(8,128)(2,1)}, u32[]{:S(2)}) copy-start(bf16[1,64,512]{2,1,0:T(8,128)(2,1)} %param.6) | copy-start | bytes 196612
  10.6 9.6 %copy-start.2 = (bf16[1,64,512]{2,1,0:T(8,128)(2,1)S(1)}, bf16[1,64,512]{2,1,0:T(8,128)(2,1)}, u32[]{:S(2)}) copy-start(bf16[1,64,512]{2,1,0:T(8,128)(2,1)} %param.7) | copy-start | bytes 196612
  10.6 9.6 %collective-permute-start.2 = (bf16[64,768]{1,0:T(8,128)(2,1)}, bf16[64,768]{1,0:T(8,128)(2,1)S(1)}, u32[]{:S(2)}, u32[]{:S(2)}) collective-permute-start(bf16[64,768]{1,0:T(8,128)(2,1)} %get-tuple-element.30), channel_id=1, source_target_pairs={{0,192},{1,193},{2,194},{3,195},{4,196},{5,197},{6,198},{7,199},{8... | collective-permute-start | bytes 294920 | tf_op jit(solution)/shard_map/heads/ppermute | solution.py:33
  20.3 6.8 %collective-permute-start.3 = (bf16[256,256]{1,0:T(8,128)(2,1)S(1)}, bf16[256,256]{1,0:T(8,128)(2,1)S(1)}, u32[]{:S(2)}, u32[]{:S(2)}) collective-permute-start(bf16[256,256]{1,0:T(8,128)(2,1)S(1)} %get-tuple-element.34), channel_id=1, source_target_pairs={{0,12},{1,13},{2,14},{3,15},{4,0},{5,1},{6,2},{7,3},{8,4},{9,5},{1... | collective-permute-start | bytes 393224 | tf_op jit(solution)/shard_map/kv_first/ppermute | solution.py:33
  23.1 6.6 %collective-permute-start.4 = (bf16[256,256]{1,0:T(8,128)(2,1)S(1)}, bf16[256,256]{1,0:T(8,128)(2,1)S(1)}, u32[]{:S(2)}, u32[]{:S(2)}) collective-permute-start(bf16[256,256]{1,0:T(8,128)(2,1)S(1)} %get-tuple-element.34), channel_id=1, source_target_pairs={{0,8},{1,9},{2,10},{3,11},{4,12},{5,13},{6,14},{7,15},{8,0},{9,1},... | collective-permute-start | bytes 393224 | tf_op jit(solution)/shard_map/kv_first/ppermute | solution.py:33
  23.9 7.4 %collective-permute-start.8 = (bf16[256,256]{1,0:T(8,128)(2,1)S(1)}, bf16[256,256]{1,0:T(8,128)(2,1)S(1)}, u32[]{:S(2)}, u32[]{:S(2)}) collective-permute-start(bf16[256,256]{1,0:T(8,128)(2,1)S(1)} %get-tuple-element.34), channel_id=1, source_target_pairs={{0,4},{1,5},{2,6},{3,7},{4,8},{5,9},{6,10},{7,11},{8,12},{9,13},{1... | collective-permute-start | bytes 393224 | tf_op jit(solution)/shard_map/kv_first/ppermute | solution.py:33
  24.9 10.2 %collective-permute-start.6 = (bf16[256,512]{1,0:T(8,128)(2,1)S(1)}, bf16[256,512]{1,0:T(8,128)(2,1)S(1)}, u32[]{:S(2)}, u32[]{:S(2)}) collective-permute-start(bf16[256,512]{1,0:T(8,128)(2,1)S(1)} %get-tuple-element.42.refs_1_), channel_id=1, source_target_pairs={{0,16},{1,17},{2,18},{3,19},{4,20},{5,21},{6,22},{7,23},{8,24},{9,... | collective-permute-start | bytes 786440 | tf_op jit(solution)/shard_map/q_other/ppermute | solution.py:33
  29.7 6.4 %collective-permute-start.5 = (bf16[512,256]{1,0:T(8,128)(2,1)S(1)}, bf16[512,256]{1,0:T(8,128)(2,1)S(1)}, u32[]{:S(2)}, u32[]{:S(2)}) collective-permute-start(bf16[512,256]{1,0:T(8,128)(2,1)S(1)} %constant_dynamic-update-slice_fusion.refs_4_), channel_id=1, source_target_pairs={{0,1},{1,2},{2,3},{3,0},{4,5},{5,6},{6,7},{7,4},{8,9},{9,10},{10,1... | collective-permute-start | bytes 786440 | tf_op jit(solution)/shard_map/kv_second/ppermute | solution.py:33
  31.4 7.6 %collective-permute-start.9 = (bf16[512,256]{1,0:T(8,128)(2,1)S(1)}, bf16[512,256]{1,0:T(8,128)(2,1)S(1)}, u32[]{:S(2)}, u32[]{:S(2)}) collective-permute-start(bf16[512,256]{1,0:T(8,128)(2,1)S(1)} %constant_dynamic-update-slice_fusion.2.refs_3_), channel_id=1, source_target_pairs={{0,1},{1,2},{2,3},{3,0},{4,5},{5,6},{6,7},{7,4},{8,9},{9,10},{10,1... | collective-permute-start | bytes 786440 | tf_op jit(solution)/shard_map/kv_second/ppermute | solution.py:33
  33.8 6.7 %collective-permute-start.11 = (bf16[512,256]{1,0:T(8,128)(2,1)S(1)}, bf16[512,256]{1,0:T(8,128)(2,1)S(1)}, u32[]{:S(2)}, u32[]{:S(2)}) collective-permute-start(bf16[512,256]{1,0:T(8,128)(2,1)S(1)} %constant_dynamic-update-slice_fusion.refs_4_), channel_id=1, source_target_pairs={{0,3},{1,0},{2,1},{3,2},{4,7},{5,4},{6,5},{7,6},{8,11},{9,8},{10,9... | collective-permute-start | bytes 786440 | tf_op jit(solution)/shard_map/kv_second/ppermute | solution.py:33
  33.8 9.2 %collective-permute-start.13 = (bf16[512,256]{1,0:T(8,128)(2,1)S(1)}, bf16[512,256]{1,0:T(8,128)(2,1)S(1)}, u32[]{:S(2)}, u32[]{:S(2)}) collective-permute-start(bf16[512,256]{1,0:T(8,128)(2,1)S(1)} %constant_dynamic-update-slice_fusion.2.refs_3_), channel_id=1, source_target_pairs={{0,3},{1,0},{2,1},{3,2},{4,7},{5,4},{6,5},{7,6},{8,11},{9,8},{10,9... | collective-permute-start | bytes 786440 | tf_op jit(solution)/shard_map/kv_second/ppermute | solution.py:33
  36.1 6.8 %collective-permute-start.7 = (bf16[256,512]{1,0:T(8,128)(2,1)S(1)}, bf16[256,512]{1,0:T(8,128)(2,1)S(1)}, u32[]{:S(2)}, u32[]{:S(2)}) collective-permute-start(bf16[256,512]{1,0:T(8,128)(2,1)S(1)} %collective-permute-done.6.refs_1_), channel_id=1, source_target_pairs={{0,32},{1,33},{2,34},{3,35},{4,36},{5,37},{6,38},{7,39},{8,40},{9,... | collective-permute-start | bytes 786440 | tf_op jit(solution)/shard_map/q_other/ppermute | solution.py:33
  38.9 8.4 %collective-permute-start.10 = (bf16[512,256]{1,0:T(8,128)(2,1)S(1)}, bf16[512,256]{1,0:T(8,128)(2,1)S(1)}, u32[]{:S(2)}, u32[]{:S(2)}) collective-permute-start(bf16[512,256]{1,0:T(8,128)(2,1)S(1)} %collective-permute-done.9.refs_5_), channel_id=1, source_target_pairs={{0,1},{1,2},{2,3},{3,0},{4,5},{5,6},{6,7},{7,4},{8,9},{9,10},{10,1... | collective-permute-start | bytes 786440 | tf_op jit(solution)/shard_map/kv_second/ppermute | solution.py:33
  40.5 6.9 %collective-permute-start.12 = (bf16[512,256]{1,0:T(8,128)(2,1)S(1)}, bf16[512,256]{1,0:T(8,128)(2,1)S(1)}, u32[]{:S(2)}, u32[]{:S(2)}) collective-permute-start(bf16[512,256]{1,0:T(8,128)(2,1)S(1)} %collective-permute-done.11.refs_8_), channel_id=1, source_target_pairs={{0,3},{1,0},{2,1},{3,2},{4,7},{5,4},{6,5},{7,6},{8,11},{9,8},{10,9... | collective-permute-start | bytes 786440 | tf_op jit(solution)/shard_map/kv_second/ppermute | solution.py:33
  50.7 1.7 %collective-permute-start.14 = (bf16[256,640]{1,0:T(8,128)(2,1)S(1)}, bf16[256,640]{1,0:T(8,128)(2,1)S(1)}, u32[]{:S(2)}, u32[]{:S(2)}) collective-permute-start(bf16[256,640]{1,0:T(8,128)(2,1)S(1)} %get-tuple-element.40), channel_id=1, source_target_pairs={{0,32},{1,33},{2,34},{3,35},{4,36},{5,37},{6,38},{7,39},{8,40},{9,... | collective-permute-start | bytes 983048 | tf_op jit(solution)/shard_map/merge_far/ppermute | solution.py:33
  50.8 6.9 %collective-permute-start.15 = (bf16[256,512]{1,0:T(8,128)(2,1)S(1)}, bf16[256,512]{1,0:T(8,128)(2,1)S(1)}, u32[]{:S(2)}, u32[]{:S(2)}) collective-permute-start(bf16[256,512]{1,0:T(8,128)(2,1)S(1)} %get-tuple-element.42.refs_1_), channel_id=1, source_target_pairs={{0,32},{1,33},{2,34},{3,35},{4,36},{5,37},{6,38},{7,39},{8,40},{9,... | collective-permute-start | bytes 786440 | tf_op jit(solution)/shard_map/q_other/ppermute | solution.py:33
  53.0 14.8 %collective-permute-start.16 = (bf16[256,640]{1,0:T(8,128)(2,1)S(1)}, bf16[256,640]{1,0:T(8,128)(2,1)S(1)}, u32[]{:S(2)}, u32[]{:S(2)}) collective-permute-start(bf16[256,640]{1,0:T(8,128)(2,1)S(1)} %merge.2), channel_id=1, source_target_pairs={{0,16},{1,17},{2,18},{3,19},{4,20},{5,21},{6,22},{7,23},{8,24},{9,... | collective-permute-start | bytes 983048 | tf_op jit(solution)/shard_map/merge_far/ppermute | solution.py:33
  67.8 1.7 %collective-permute-start.17 = (bf16[256,640]{1,0:T(8,128)(2,1)S(1)}, bf16[256,640]{1,0:T(8,128)(2,1)S(1)}, u32[]{:S(2)}, u32[]{:S(2)}) collective-permute-start(bf16[256,640]{1,0:T(8,128)(2,1)S(1)} %get-tuple-element.46), channel_id=1, source_target_pairs={{0,32},{1,33},{2,34},{3,35},{4,36},{5,37},{6,38},{7,39},{8,40},{9,... | collective-permute-start | bytes 983048 | tf_op jit(solution)/shard_map/merge_own/ppermute | solution.py:33
  70.7 9.4 %collective-permute-start.18 = (bf16[64,512]{1,0:T(8,128)(2,1)S(1)}, bf16[64,512]{1,0:T(8,128)(2,1)S(1)}, u32[]{:S(2)}, u32[]{:S(2)}) collective-permute-start(bf16[64,512]{1,0:T(8,128)(2,1)S(1)} %get-tuple-element.48), channel_id=1, source_target_pairs={{0,64},{1,65},{2,66},{3,67},{4,68},{5,69},{6,70},{7,71},{8,72},{9,... | collective-permute-start | bytes 196616 | tf_op jit(solution)/shard_map/out_heads/ppermute | solution.py:33
  75.1 8.5 %collective-permute-start.19 = (bf16[64,512]{1,0:T(8,128)(2,1)S(1)}, bf16[64,512]{1,0:T(8,128)(2,1)S(1)}, u32[]{:S(2)}, u32[]{:S(2)}) collective-permute-start(bf16[64,512]{1,0:T(8,128)(2,1)S(1)} %get-tuple-element.49), channel_id=1, source_target_pairs={{0,128},{1,129},{2,130},{3,131},{4,132},{5,133},{6,134},{7,135},{8... | collective-permute-start | bytes 196616 | tf_op jit(solution)/shard_map/out_heads/ppermute | solution.py:33
  76.6 7.0 %collective-permute-start.20 = (bf16[64,512]{1,0:T(8,128)(2,1)S(1)}, bf16[64,512]{1,0:T(8,128)(2,1)S(1)}, u32[]{:S(2)}, u32[]{:S(2)}) collective-permute-start(bf16[64,512]{1,0:T(8,128)(2,1)S(1)} %get-tuple-element.50), channel_id=1, source_target_pairs={{0,192},{1,193},{2,194},{3,195},{4,196},{5,197},{6,198},{7,199},{8... | collective-permute-start | bytes 196616 | tf_op jit(solution)/shard_map/out_heads/ppermute | solution.py:33

commit v4 on v3

--- a/solution.py
+++ b/solution.py
@@ -238,6 +238,8 @@
         acc_in, ml_in = rest.pop(0), rest.pop(0)
     out_a, out_b = rest.pop(0), rest.pop(0)
     kt, v_s, q_s, acc, m_s, l_s = rest
+    if not final:
+        acc = out_a
     core = meta[CORE_AT]
 
     tile = 0
@@ -385,7 +387,6 @@
             else:
                 stats = jnp.where(lane == h, m_s[i], stats)
                 stats = jnp.where(lane == 4 + h, total, stats)
-                out_a[i] = acc[i]
         if final:
             out_a[rows, pl.ds(512, 128)] = stats[:128]
             out_b[rows, pl.ds(512, 128)] = three_parts(stats[128:])
@@ -416,7 +417,7 @@
             pltpu.VMEM((keys // 128, 128, 128), jnp.bfloat16),
             pltpu.VMEM((keys // 128, 128, 128), jnp.bfloat16),
             pltpu.VMEM((8, 256, 128), jnp.bfloat16),
-            pltpu.VMEM((8, 256, 128), jnp.float32),
+            pltpu.VMEM((8 if final else 1, 256, 128), jnp.float32),
             pltpu.VMEM((8, 256, 128), jnp.float32),
             pltpu.VMEM((8, 256, 128), jnp.float32),
         ],

time: 83.9 us -> 81.8 us (0.975)
  the two profiles are of different devices: /device:TPU:8 before, /device:TPU:1 now
where the time goes in v4:
time: 81.8 us; the launch traced here: 81 us
  starting transfers between devices  36.7 us (45%)
  waiting for transfers between devices  22.7 us (28%)
  Pallas kernels  21.5 us (26%)
    ppermute x21, starting transfers between devices, send(): return lax.ppermute(a, AXES, pairs)  36.7 us
    ppermute x21, waiting for transfers between devices, send(): return lax.ppermute(a, AXES, pairs)  22.7 us
    pallas_call x3, Pallas kernels, flash(): pl.pallas_call(functools.partial(flash_kernel, rows, call, carry, final),...  14.3 us
    pallas_call x1, Pallas kernels, make_plan(): pl.pallas_call(plan_kernel, out_shape=jax.ShapeDtypeStruct((EDGE_AT + 3,)...  2.88 us
    pallas_call x1, Pallas kernels, pack(): pl.pallas_call(pack_kernel, out_shape=[jax.ShapeDtypeStruct((64, width),...  1.83 us
    pallas_call x2, Pallas kernels, merge(): pl.pallas_call(functools.partial(merge_kernel, len(partials)), out_shape=...  1.74 us
  transfers between devices with their start and end apart: 21, of which 12 were waited for; matrix products, arithmetic and copies ran while one was open for 0% of the time, Pallas kernels for 18%

profile of v4, /device:TPU:1, one launch (start us, length us, event | category | flops | bytes accessed | tf_op | source)
XLA Modules:
  0.0 81.0 jit_solution(11161249967112106102)
XLA Ops:
  0.0 1.8 %pack.1 = (bf16[64,768]{1,0:T(8,128)(2,1)}, bf16[64,768]{1,0:T(8,128)(2,1)}, bf16[64,768]{1,0:T(8,128)(2,1)}) custom-call(bf16[64,512]{1,0:T(8,128)(2,1)} %bitcast.6, bf16[64,512]{1,0:T(8,128)(2,1)} %bitcast.8, bf16[64,2048]{1,0:T(8,128)(2,1)} %bitcast.4), custom_call_target="tpu_custom_call" | custom-call | tf_op jit(solution)/shard_map/heads/pack/pallas_call | solution.py:75
  1.9 3.9 %collective-permute-start = (bf16[64,768]{1,0:T(8,128)(2,1)}, bf16[64,768]{1,0:T(8,128)(2,1)S(1)}, u32[]{:S(2)}, u32[]{:S(2)}) collective-permute-start(bf16[64,768]{1,0:T(8,128)(2,1)} %get-tuple-element.28), channel_id=1, source_target_pairs={{0,64},{1,65},{2,66},{3,67},{4,68},{5,69},{6,70},{7,71},{8,72},{9,... | collective-permute-start | bytes 294920 | tf_op jit(solution)/shard_map/heads/ppermute | solution.py:33
  5.8 5.1 %collective-permute-start.1 = (bf16[64,768]{1,0:T(8,128)(2,1)}, bf16[64,768]{1,0:T(8,128)(2,1)S(1)}, u32[]{:S(2)}, u32[]{:S(2)}) collective-permute-start(bf16[64,768]{1,0:T(8,128)(2,1)} %get-tuple-element.29), channel_id=1, source_target_pairs={{0,128},{1,129},{2,130},{3,131},{4,132},{5,133},{6,134},{7,135},{8... | collective-permute-start | bytes 294920 | tf_op jit(solution)/shard_map/heads/ppermute | solution.py:33
  10.9 2.4 %collective-permute-start.2 = (bf16[64,768]{1,0:T(8,128)(2,1)}, bf16[64,768]{1,0:T(8,128)(2,1)S(1)}, u32[]{:S(2)}, u32[]{:S(2)}) collective-permute-start(bf16[64,768]{1,0:T(8,128)(2,1)} %get-tuple-element.30), channel_id=1, source_target_pairs={{0,192},{1,193},{2,194},{3,195},{4,196},{5,197},{6,198},{7,199},{8... | collective-permute-start | bytes 294920 | tf_op jit(solution)/shard_map/heads/ppermute | solution.py:33
  13.3 2.9 %plan.1.refs_0_ = s32[440]{0:T(512)S(1)} custom-call(s32[32,512]{1,0:T(8,128)S(1)} %copy-done.3, s32[32,512]{1,0:T(8,128)S(1)} %copy-done.4), custom_call_target="tpu_custom_call" | custom-call | tf_op jit(solution)/shard_map/heads/plan/pallas_call | solution.py:208
  16.1 0.0 collective-permute-done.refs_3_
  16.2 1.1 %collective-permute-done.1.refs_4_ = bf16[64,768]{1,0:T(8,128)(2,1)S(1)} collective-permute-done((bf16[64,768]{1,0:T(8,128)(2,1)}, bf16[64,768]{1,0:T(8,128)(2,1)S(1)}, u32[]{:S(2)}, u32[]{:S(2)}) %collective-permute-start.1) | collective-permute-done | bytes 98336 | tf_op jit(solution)/shard_map/heads/ppermute | solution.py:33
  17.3 3.9 %collective-permute-done.2.refs_5_ = bf16[64,768]{1,0:T(8,128)(2,1)S(1)} collective-permute-done((bf16[64,768]{1,0:T(8,128)(2,1)}, bf16[64,768]{1,0:T(8,128)(2,1)S(1)}, u32[]{:S(2)}, u32[]{:S(2)}) %collective-permute-start.2) | collective-permute-done | bytes 98336 | tf_op jit(solution)/shard_map/heads/ppermute | solution.py:33
  21.2 0.1 unpack.1
  21.3 2.8 %collective-permute-start.3 = (bf16[256,256]{1,0:T(8,128)(2,1)S(1)}, bf16[256,256]{1,0:T(8,128)(2,1)S(1)}, u32[]{:S(2)}, u32[]{:S(2)}) collective-permute-start(bf16[256,256]{1,0:T(8,128)(2,1)S(1)} %get-tuple-element.34), channel_id=1, source_target_pairs={{0,12},{1,13},{2,14},{3,15},{4,0},{5,1},{6,2},{7,3},{8,4},{9,5},{1... | collective-permute-start | bytes 393224 | tf_op jit(solution)/shard_map/kv_first/ppermute | solution.py:33
  24.1 0.3 collective-permute-start.4
  24.5 0.8 collective-permute-start.8
  25.2 2.2 %collective-permute-done.3 = bf16[256,256]{1,0:T(8,128)(2,1)S(1)} collective-permute-done((bf16[256,256]{1,0:T(8,128)(2,1)S(1)}, bf16[256,256]{1,0:T(8,128)(2,1)S(1)}, u32[]{:S(2)}, u32[]{:S(2)}) %collective-permute-start.3) | collective-permute-done | bytes 131104 | tf_op jit(solution)/shard_map/kv_first/ppermute | solution.py:33
  27.4 2.3 %collective-permute-done.4 = bf16[256,256]{1,0:T(8,128)(2,1)S(1)} collective-permute-done((bf16[256,256]{1,0:T(8,128)(2,1)S(1)}, bf16[256,256]{1,0:T(8,128)(2,1)S(1)}, u32[]{:S(2)}, u32[]{:S(2)}) %collective-permute-start.4) | collective-permute-done | bytes 131104 | tf_op jit(solution)/shard_map/kv_first/ppermute | solution.py:33
  29.7 1.1 %collective-permute-start.5 = (bf16[512,256]{1,0:T(8,128)(2,1)S(1)}, bf16[512,256]{1,0:T(8,128)(2,1)S(1)}, u32[]{:S(2)}, u32[]{:S(2)}) collective-permute-start(bf16[512,256]{1,0:T(8,128)(2,1)S(1)} %constant_dynamic-update-slice_fusion.refs_4_), channel_id=1, source_target_pairs={{0,1},{1,2},{2,3},{3,0},{4,5},{5,6},{6,7},{7,4},{8,9},{9,10},{10,1... | collective-permute-start | bytes 786440 | tf_op jit(solution)/shard_map/kv_second/ppermute | solution.py:33
  30.8 0.3 collective-permute-done.8
  31.1 1.0 %collective-permute-start.9 = (bf16[512,256]{1,0:T(8,128)(2,1)S(1)}, bf16[512,256]{1,0:T(8,128)(2,1)S(1)}, u32[]{:S(2)}, u32[]{:S(2)}) collective-permute-start(bf16[512,256]{1,0:T(8,128)(2,1)S(1)} %constant_dynamic-update-slice_fusion.2.refs_3_), channel_id=1, source_target_pairs={{0,1},{1,2},{2,3},{3,0},{4,5},{5,6},{6,7},{7,4},{8,9},{9,10},{10,1... | collective-permute-start | bytes 786440 | tf_op jit(solution)/shard_map/kv_second/ppermute | solution.py:33
  32.1 1.8 %collective-permute-start.11 = (bf16[512,256]{1,0:T(8,128)(2,1)S(1)}, bf16[512,256]{1,0:T(8,128)(2,1)S(1)}, u32[]{:S(2)}, u32[]{:S(2)}) collective-permute-start(bf16[512,256]{1,0:T(8,128)(2,1)S(1)} %constant_dynamic-update-slice_fusion.refs_4_), channel_id=1, source_target_pairs={{0,3},{1,0},{2,1},{3,2},{4,7},{5,4},{6,5},{7,6},{8,11},{9,8},{10,9... | collective-permute-start | bytes 786440 | tf_op jit(solution)/shard_map/kv_second/ppermute | solution.py:33
  33.9 1.0 %collective-permute-start.13 = (bf16[512,256]{1,0:T(8,128)(2,1)S(1)}, bf16[512,256]{1,0:T(8,128)(2,1)S(1)}, u32[]{:S(2)}, u32[]{:S(2)}) collective-permute-start(bf16[512,256]{1,0:T(8,128)(2,1)S(1)} %constant_dynamic-update-slice_fusion.2.refs_3_), channel_id=1, source_target_pairs={{0,3},{1,0},{2,1},{3,2},{4,7},{5,4},{6,5},{7,6},{8,11},{9,8},{10,9... | collective-permute-start | bytes 786440 | tf_op jit(solution)/shard_map/kv_second/ppermute | solution.py:33
  34.9 0.0 collective-permute-done.6.refs_1_
  34.9 1.7 %collective-permute-done.5.refs_6_ = bf16[512,256]{1,0:T(8,128)(2,1)S(1)} collective-permute-done((bf16[512,256]{1,0:T(8,128)(2,1)S(1)}, bf16[512,256]{1,0:T(8,128)(2,1)S(1)}, u32[]{:S(2)}, u32[]{:S(2)}) %collective-permute-start.5) | collective-permute-done | bytes 262176 | tf_op jit(solution)/shard_map/kv_second/ppermute | solution.py:33
  36.5 2.3 %collective-permute-start.7 = (bf16[256,512]{1,0:T(8,128)(2,1)S(1)}, bf16[256,512]{1,0:T(8,128)(2,1)S(1)}, u32[]{:S(2)}, u32[]{:S(2)}) collective-permute-start(bf16[256,512]{1,0:T(8,128)(2,1)S(1)} %collective-permute-done.6.refs_1_), channel_id=1, source_target_pairs={{0,32},{1,33},{2,34},{3,35},{4,36},{5,37},{6,38},{7,39},{8,40},{9,... | collective-permute-start | bytes 786440 | tf_op jit(solution)/shard_map/q_other/ppermute | solution.py:33
  38.8 0.5 collective-permute-done.9.refs_5_
  39.3 0.0 collective-permute-start.10
  39.3 0.0 collective-permute-done.11.refs_8_
  39.3 2.7 %collective-permute-start.12 = (bf16[512,256]{1,0:T(8,128)(2,1)S(1)}, bf16[512,256]{1,0:T(8,128)(2,1)S(1)}, u32[]{:S(2)}, u32[]{:S(2)}) collective-permute-start(bf16[512,256]{1,0:T(8,128)(2,1)S(1)} %collective-permute-done.11.refs_8_), channel_id=1, source_target_pairs={{0,3},{1,0},{2,1},{3,2},{4,7},{5,4},{6,5},{7,6},{8,11},{9,8},{10,9... | collective-permute-start | bytes 786440 | tf_op jit(solution)/shard_map/kv_second/ppermute | solution.py:33
  42.0 0.0 collective-permute-done.13.refs_7_
  42.0 5.1 %flash.3 = (f32[8,256,128]{2,1,0:T(8,128)S(1)}, f32[2,256,128]{2,1,0:T(8,128)S(1)}) custom-call(s32[440]{0:T(512)S(1)} %plan.1.refs_0_, bf16[256,512]{1,0:T(8,128)(2,1)S(1)} %collective-permute-done.6.refs_1_, bf16[256,512]{1,0:T(8,128)(2,1)S(1)} %collective-permute-done.7.refs_2_, bf16[512,256]{1,0:T(8,128)(2,1)S(1)} %constant_dynamic-update-slice_fusion.2.refs_3_, ...), custom_call_target="tpu_custom_call" | custom-call | flops 805306368 | bytes 1572864 | tf_op jit(solution)/shard_map/attend_far/flash/pallas_call | solution.py:411
  47.1 0.0 collective-permute-done.10.refs_3_.refs_9_
  47.1 0.0 collective-permute-done.12.refs_4_.refs_10_
  47.1 3.3 %flash.4 = (f32[256,640]{1,0:T(8,128)S(1)}, bf16[256,640]{1,0:T(8,128)(2,1)S(1)}) custom-call(s32[440]{0:T(512)S(1)} %plan.1.refs_0_, bf16[256,512]{1,0:T(8,128)(2,1)S(1)} %collective-permute-done.6.refs_1_, bf16[256,512]{1,0:T(8,128)(2,1)S(1)} %collective-permute-done.7.refs_2_, bf16[512,256]{1,0:T(8,128)(2,1)S(1)} %collective-permute-done.10.refs_3_.refs_9_, ...), custom_call_target="tpu_custom_call" | custom-call | flops 268435456 | bytes 524288 | tf_op jit(solution)/shard_map/attend_far/flash/pallas_call | solution.py:411
  50.4 2.3 %collective-permute-start.14 = (bf16[256,640]{1,0:T(8,128)(2,1)S(1)}, bf16[256,640]{1,0:T(8,128)(2,1)S(1)}, u32[]{:S(2)}, u32[]{:S(2)}) collective-permute-start(bf16[256,640]{1,0:T(8,128)(2,1)S(1)} %get-tuple-element.40), channel_id=1, source_target_pairs={{0,32},{1,33},{2,34},{3,35},{4,36},{5,37},{6,38},{7,39},{8,40},{9,... | collective-permute-start | bytes 983048 | tf_op jit(solution)/shard_map/merge_far/ppermute | solution.py:33
  52.7 0.1 collective-permute-start.15
  52.8 1.2 %collective-permute-done.14.refs_1_ = bf16[256,640]{1,0:T(8,128)(2,1)S(1)} collective-permute-done((bf16[256,640]{1,0:T(8,128)(2,1)S(1)}, bf16[256,640]{1,0:T(8,128)(2,1)S(1)}, u32[]{:S(2)}, u32[]{:S(2)}) %collective-permute-start.14) | collective-permute-done | bytes 327712 | tf_op jit(solution)/shard_map/merge_far/ppermute | solution.py:33
  54.0 0.6 merge.2
  54.6 0.3 collective-permute-start.16
  54.9 0.0 collective-permute-done.15.refs_2_
  54.9 5.9 %flash.5 = (f32[256,640]{1,0:T(8,128)S(1)}, bf16[256,640]{1,0:T(8,128)(2,1)S(1)}) custom-call(s32[440]{0:T(512)S(1)} %plan.1.refs_0_, bf16[256,512]{1,0:T(8,128)(2,1)S(1)} %get-tuple-element.42.refs_1_, bf16[256,512]{1,0:T(8,128)(2,1)S(1)} %collective-permute-done.15.refs_2_, bf16[512,256]{1,0:T(8,128)(2,1)S(1)} %constant_dynamic-update-slice_fusion.2.refs_3_, ...), custom_call_target="tpu_custom_call" | custom-call | flops 25769803776 | bytes 2097152 | tf_op jit(solution)/shard_map/attend_own/flash/pallas_call | solution.py:411
  60.9 3.0 %collective-permute-done.16.refs_2_ = bf16[256,640]{1,0:T(8,128)(2,1)S(1)} collective-permute-done((bf16[256,640]{1,0:T(8,128)(2,1)S(1)}, bf16[256,640]{1,0:T(8,128)(2,1)S(1)}, u32[]{:S(2)}, u32[]{:S(2)}) %collective-permute-start.16) | collective-permute-done | bytes 327712 | tf_op jit(solution)/shard_map/merge_far/ppermute | solution.py:33
  63.8 1.2 %collective-permute-start.17 = (bf16[256,640]{1,0:T(8,128)(2,1)S(1)}, bf16[256,640]{1,0:T(8,128)(2,1)S(1)}, u32[]{:S(2)}, u32[]{:S(2)}) collective-permute-start(bf16[256,640]{1,0:T(8,128)(2,1)S(1)} %get-tuple-element.46), channel_id=1, source_target_pairs={{0,32},{1,33},{2,34},{3,35},{4,36},{5,37},{6,38},{7,39},{8,40},{9,... | collective-permute-start | bytes 983048 | tf_op jit(solution)/shard_map/merge_own/ppermute | solution.py:33
  65.0 1.3 %collective-permute-done.17.refs_1_ = bf16[256,640]{1,0:T(8,128)(2,1)S(1)} collective-permute-done((bf16[256,640]{1,0:T(8,128)(2,1)S(1)}, bf16[256,640]{1,0:T(8,128)(2,1)S(1)}, u32[]{:S(2)}, u32[]{:S(2)}) %collective-permute-start.17) | collective-permute-done | bytes 327712 | tf_op jit(solution)/shard_map/merge_own/ppermute | solution.py:33
  66.3 1.1 %merge.3 = (bf16[64,512]{1,0:T(8,128)(2,1)S(1)}, bf16[64,512]{1,0:T(8,128)(2,1)S(1)}, bf16[64,512]{1,0:T(8,128)(2,1)S(1)}, bf16[64,512]{1,0:T(8,128)(2,1)S(1)}) custom-call(f32[256,640]{1,0:T(8,128)S(1)} %get-tuple-element.44.refs_0_, bf16[256,640]{1,0:T(8,128)(2,1)S(1)} %collective-permute-done.17.refs_1_, bf16[256,640]{1,0:T(8,128)(2,1)S(1)} %collective-permute-done.16.refs_2_), custom_call_target="tpu_custom_call" | custom-call | tf_op jit(solution)/shard_map/merge_own/merge/pallas_call | solution.py:466
  67.4 1.5 %collective-permute-start.18 = (bf16[64,512]{1,0:T(8,128)(2,1)S(1)}, bf16[64,512]{1,0:T(8,128)(2,1)S(1)}, u32[]{:S(2)}, u32[]{:S(2)}) collective-permute-start(bf16[64,512]{1,0:T(8,128)(2,1)S(1)} %get-tuple-element.48), channel_id=1, source_target_pairs={{0,64},{1,65},{2,66},{3,67},{4,68},{5,69},{6,70},{7,71},{8,72},{9,... | collective-permute-start | bytes 196616 | tf_op jit(solution)/shard_map/out_heads/ppermute | solution.py:33
  68.9 4.0 %collective-permute-start.19 = (bf16[64,512]{1,0:T(8,128)(2,1)S(1)}, bf16[64,512]{1,0:T(8,128)(2,1)S(1)}, u32[]{:S(2)}, u32[]{:S(2)}) collective-permute-start(bf16[64,512]{1,0:T(8,128)(2,1)S(1)} %get-tuple-element.49), channel_id=1, source_target_pairs={{0,128},{1,129},{2,130},{3,131},{4,132},{5,133},{6,134},{7,135},{8... | collective-permute-start | bytes 196616 | tf_op jit(solution)/shard_map/out_heads/ppermute | solution.py:33
  72.9 2.1 %collective-permute-start.20 = (bf16[64,512]{1,0:T(8,128)(2,1)S(1)}, bf16[64,512]{1,0:T(8,128)(2,1)S(1)}, u32[]{:S(2)}, u32[]{:S(2)}) collective-permute-start(bf16[64,512]{1,0:T(8,128)(2,1)S(1)} %get-tuple-element.50), channel_id=1, source_target_pairs={{0,192},{1,193},{2,194},{3,195},{4,196},{5,197},{6,198},{7,199},{8... | collective-permute-start | bytes 196616 | tf_op jit(solution)/shard_map/out_heads/ppermute | solution.py:33
  75.0 2.7 %collective-permute-done.19.refs_2_ = bf16[64,512]{1,0:T(8,128)(2,1)S(1)} collective-permute-done((bf16[64,512]{1,0:T(8,128)(2,1)S(1)}, bf16[64,512]{1,0:T(8,128)(2,1)S(1)}, u32[]{:S(2)}, u32[]{:S(2)}) %collective-permute-start.19) | collective-permute-done | bytes 65568 | tf_op jit(solution)/shard_map/out_heads/ppermute | solution.py:33
  77.7 2.6 %collective-permute-done.20.refs_3_ = bf16[64,512]{1,0:T(8,128)(2,1)S(1)} collective-permute-done((bf16[64,512]{1,0:T(8,128)(2,1)S(1)}, bf16[64,512]{1,0:T(8,128)(2,1)S(1)}, u32[]{:S(2)}, u32[]{:S(2)}) %collective-permute-start.20) | collective-permute-done | bytes 65568 | tf_op jit(solution)/shard_map/out_heads/ppermute | solution.py:33
  80.3 0.7 finish.1
  (17 shorter events, 0.1 us)
Async XLA Ops:
  0.0 13.3 %copy-start.3 = (s32[32,512]{1,0:T(8,128)S(1)}, s32[32,512]{1,0:T(8,128)}, u32[]{:S(2)}) copy-start(s32[32,512]{1,0:T(8,128)} %pos_hbm.1) | copy-start | bytes 196612
  0.0 13.3 %copy-start.4 = (s32[32,512]{1,0:T(8,128)S(1)}, s32[32,512]{1,0:T(8,128)}, u32[]{:S(2)}) copy-start(s32[32,512]{1,0:T(8,128)} %seg_hbm.1) | copy-start | bytes 196612
  0.0 21.2 %copy-start = (bf16[1,64,2048]{2,1,0:T(8,128)(2,1)S(1)}, bf16[1,64,2048]{2,1,0:T(8,128)(2,1)}, u32[]{:S(2)}) copy-start(bf16[1,64,2048]{2,1,0:T(8,128)(2,1)} %param.5) | copy-start | bytes 786436
  1.9 14.3 %collective-permute-start = (bf16[64,768]{1,0:T(8,128)(2,1)}, bf16[64,768]{1,0:T(8,128)(2,1)S(1)}, u32[]{:S(2)}, u32[]{:S(2)}) collective-permute-start(bf16[64,768]{1,0:T(8,128)(2,1)} %get-tuple-element.28), channel_id=1, source_target_pairs={{0,64},{1,65},{2,66},{3,67},{4,68},{5,69},{6,70},{7,71},{8,72},{9,... | collective-permute-start | bytes 294920 | tf_op jit(solution)/shard_map/heads/ppermute | solution.py:33
  5.8 11.5 %collective-permute-start.1 = (bf16[64,768]{1,0:T(8,128)(2,1)}, bf16[64,768]{1,0:T(8,128)(2,1)S(1)}, u32[]{:S(2)}, u32[]{:S(2)}) collective-permute-start(bf16[64,768]{1,0:T(8,128)(2,1)} %get-tuple-element.29), channel_id=1, source_target_pairs={{0,128},{1,129},{2,130},{3,131},{4,132},{5,133},{6,134},{7,135},{8... | collective-permute-start | bytes 294920 | tf_op jit(solution)/shard_map/heads/ppermute | solution.py:33
  10.9 10.3 %copy-start.1 = (bf16[1,64,512]{2,1,0:T(8,128)(2,1)S(1)}, bf16[1,64,512]{2,1,0:T(8,128)(2,1)}, u32[]{:S(2)}) copy-start(bf16[1,64,512]{2,1,0:T(8,128)(2,1)} %param.6) | copy-start | bytes 196612
  10.9 10.3 %copy-start.2 = (bf16[1,64,512]{2,1,0:T(8,128)(2,1)S(1)}, bf16[1,64,512]{2,1,0:T(8,128)(2,1)}, u32[]{:S(2)}) copy-start(bf16[1,64,512]{2,1,0:T(8,128)(2,1)} %param.7) | copy-start | bytes 196612
  10.9 10.3 %collective-permute-start.2 = (bf16[64,768]{1,0:T(8,128)(2,1)}, bf16[64,768]{1,0:T(8,128)(2,1)S(1)}, u32[]{:S(2)}, u32[]{:S(2)}) collective-permute-start(bf16[64,768]{1,0:T(8,128)(2,1)} %get-tuple-element.30), channel_id=1, source_target_pairs={{0,192},{1,193},{2,194},{3,195},{4,196},{5,197},{6,198},{7,199},{8... | collective-permute-start | bytes 294920 | tf_op jit(solution)/shard_map/heads/ppermute | solution.py:33
  21.3 6.1 %collective-permute-start.3 = (bf16[256,256]{1,0:T(8,128)(2,1)S(1)}, bf16[256,256]{1,0:T(8,128)(2,1)S(1)}, u32[]{:S(2)}, u32[]{:S(2)}) collective-permute-start(bf16[256,256]{1,0:T(8,128)(2,1)S(1)} %get-tuple-element.34), channel_id=1, source_target_pairs={{0,12},{1,13},{2,14},{3,15},{4,0},{5,1},{6,2},{7,3},{8,4},{9,5},{1... | collective-permute-start | bytes 393224 | tf_op jit(solution)/shard_map/kv_first/ppermute | solution.py:33
  24.1 5.6 %collective-permute-start.4 = (bf16[256,256]{1,0:T(8,128)(2,1)S(1)}, bf16[256,256]{1,0:T(8,128)(2,1)S(1)}, u32[]{:S(2)}, u32[]{:S(2)}) collective-permute-start(bf16[256,256]{1,0:T(8,128)(2,1)S(1)} %get-tuple-element.34), channel_id=1, source_target_pairs={{0,8},{1,9},{2,10},{3,11},{4,12},{5,13},{6,14},{7,15},{8,0},{9,1},... | collective-permute-start | bytes 393224 | tf_op jit(solution)/shard_map/kv_first/ppermute | solution.py:33
  24.5 6.7 %collective-permute-start.8 = (bf16[256,256]{1,0:T(8,128)(2,1)S(1)}, bf16[256,256]{1,0:T(8,128)(2,1)S(1)}, u32[]{:S(2)}, u32[]{:S(2)}) collective-permute-start(bf16[256,256]{1,0:T(8,128)(2,1)S(1)} %get-tuple-element.34), channel_id=1, source_target_pairs={{0,4},{1,5},{2,6},{3,7},{4,8},{5,9},{6,10},{7,11},{8,12},{9,13},{1... | collective-permute-start | bytes 393224 | tf_op jit(solution)/shard_map/kv_first/ppermute | solution.py:33
  25.2 9.6 %collective-permute-start.6 = (bf16[256,512]{1,0:T(8,128)(2,1)S(1)}, bf16[256,512]{1,0:T(8,128)(2,1)S(1)}, u32[]{:S(2)}, u32[]{:S(2)}) collective-permute-start(bf16[256,512]{1,0:T(8,128)(2,1)S(1)} %get-tuple-element.42.refs_1_), channel_id=1, source_target_pairs={{0,16},{1,17},{2,18},{3,19},{4,20},{5,21},{6,22},{7,23},{8,24},{9,... | collective-permute-start | bytes 786440 | tf_op jit(solution)/shard_map/q_other/ppermute | solution.py:33
  29.7 6.8 %collective-permute-start.5 = (bf16[512,256]{1,0:T(8,128)(2,1)S(1)}, bf16[512,256]{1,0:T(8,128)(2,1)S(1)}, u32[]{:S(2)}, u32[]{:S(2)}) collective-permute-start(bf16[512,256]{1,0:T(8,128)(2,1)S(1)} %constant_dynamic-update-slice_fusion.refs_4_), channel_id=1, source_target_pairs={{0,1},{1,2},{2,3},{3,0},{4,5},{5,6},{6,7},{7,4},{8,9},{9,10},{10,1... | collective-permute-start | bytes 786440 | tf_op jit(solution)/shard_map/kv_second/ppermute | solution.py:33
  31.1 8.2 %collective-permute-start.9 = (bf16[512,256]{1,0:T(8,128)(2,1)S(1)}, bf16[512,256]{1,0:T(8,128)(2,1)S(1)}, u32[]{:S(2)}, u32[]{:S(2)}) collective-permute-start(bf16[512,256]{1,0:T(8,128)(2,1)S(1)} %constant_dynamic-update-slice_fusion.2.refs_3_), channel_id=1, source_target_pairs={{0,1},{1,2},{2,3},{3,0},{4,5},{5,6},{6,7},{7,4},{8,9},{9,10},{10,1... | collective-permute-start | bytes 786440 | tf_op jit(solution)/shard_map/kv_second/ppermute | solution.py:33
  32.1 7.2 %collective-permute-start.11 = (bf16[512,256]{1,0:T(8,128)(2,1)S(1)}, bf16[512,256]{1,0:T(8,128)(2,1)S(1)}, u32[]{:S(2)}, u32[]{:S(2)}) collective-permute-start(bf16[512,256]{1,0:T(8,128)(2,1)S(1)} %constant_dynamic-update-slice_fusion.refs_4_), channel_id=1, source_target_pairs={{0,3},{1,0},{2,1},{3,2},{4,7},{5,4},{6,5},{7,6},{8,11},{9,8},{10,9... | collective-permute-start | bytes 786440 | tf_op jit(solution)/shard_map/kv_second/ppermute | solution.py:33
  33.9 8.1 %collective-permute-start.13 = (bf16[512,256]{1,0:T(8,128)(2,1)S(1)}, bf16[512,256]{1,0:T(8,128)(2,1)S(1)}, u32[]{:S(2)}, u32[]{:S(2)}) collective-permute-start(bf16[512,256]{1,0:T(8,128)(2,1)S(1)} %constant_dynamic-update-slice_fusion.2.refs_3_), channel_id=1, source_target_pairs={{0,3},{1,0},{2,1},{3,2},{4,7},{5,4},{6,5},{7,6},{8,11},{9,8},{10,9... | collective-permute-start | bytes 786440 | tf_op jit(solution)/shard_map/kv_second/ppermute | solution.py:33
  36.5 5.5 %collective-permute-start.7 = (bf16[256,512]{1,0:T(8,128)(2,1)S(1)}, bf16[256,512]{1,0:T(8,128)(2,1)S(1)}, u32[]{:S(2)}, u32[]{:S(2)}) collective-permute-start(bf16[256,512]{1,0:T(8,128)(2,1)S(1)} %collective-permute-done.6.refs_1_), channel_id=1, source_target_pairs={{0,32},{1,33},{2,34},{3,35},{4,36},{5,37},{6,38},{7,39},{8,40},{9,... | collective-permute-start | bytes 786440 | tf_op jit(solution)/shard_map/q_other/ppermute | solution.py:33
  39.3 7.8 %collective-permute-start.10 = (bf16[512,256]{1,0:T(8,128)(2,1)S(1)}, bf16[512,256]{1,0:T(8,128)(2,1)S(1)}, u32[]{:S(2)}, u32[]{:S(2)}) collective-permute-start(bf16[512,256]{1,0:T(8,128)(2,1)S(1)} %collective-permute-done.9.refs_5_), channel_id=1, source_target_pairs={{0,1},{1,2},{2,3},{3,0},{4,5},{5,6},{6,7},{7,4},{8,9},{9,10},{10,1... | collective-permute-start | bytes 786440 | tf_op jit(solution)/shard_map/kv_second/ppermute | solution.py:33
  39.3 7.8 %collective-permute-start.12 = (bf16[512,256]{1,0:T(8,128)(2,1)S(1)}, bf16[512,256]{1,0:T(8,128)(2,1)S(1)}, u32[]{:S(2)}, u32[]{:S(2)}) collective-permute-start(bf16[512,256]{1,0:T(8,128)(2,1)S(1)} %collective-permute-done.11.refs_8_), channel_id=1, source_target_pairs={{0,3},{1,0},{2,1},{3,2},{4,7},{5,4},{6,5},{7,6},{8,11},{9,8},{10,9... | collective-permute-start | bytes 786440 | tf_op jit(solution)/shard_map/kv_second/ppermute | solution.py:33
  50.4 3.6 %collective-permute-start.14 = (bf16[256,640]{1,0:T(8,128)(2,1)S(1)}, bf16[256,640]{1,0:T(8,128)(2,1)S(1)}, u32[]{:S(2)}, u32[]{:S(2)}) collective-permute-start(bf16[256,640]{1,0:T(8,128)(2,1)S(1)} %get-tuple-element.40), channel_id=1, source_target_pairs={{0,32},{1,33},{2,34},{3,35},{4,36},{5,37},{6,38},{7,39},{8,40},{9,... | collective-permute-start | bytes 983048 | tf_op jit(solution)/shard_map/merge_far/ppermute | solution.py:33
  52.7 2.2 %collective-permute-start.15 = (bf16[256,512]{1,0:T(8,128)(2,1)S(1)}, bf16[256,512]{1,0:T(8,128)(2,1)S(1)}, u32[]{:S(2)}, u32[]{:S(2)}) collective-permute-start(bf16[256,512]{1,0:T(8,128)(2,1)S(1)} %get-tuple-element.42.refs_1_), channel_id=1, source_target_pairs={{0,32},{1,33},{2,34},{3,35},{4,36},{5,37},{6,38},{7,39},{8,40},{9,... | collective-permute-start | bytes 786440 | tf_op jit(solution)/shard_map/q_other/ppermute | solution.py:33
  54.6 9.2 %collective-permute-start.16 = (bf16[256,640]{1,0:T(8,128)(2,1)S(1)}, bf16[256,640]{1,0:T(8,128)(2,1)S(1)}, u32[]{:S(2)}, u32[]{:S(2)}) collective-permute-start(bf16[256,640]{1,0:T(8,128)(2,1)S(1)} %merge.2), channel_id=1, source_target_pairs={{0,16},{1,17},{2,18},{3,19},{4,20},{5,21},{6,22},{7,23},{8,24},{9,... | collective-permute-start | bytes 983048 | tf_op jit(solution)/shard_map/merge_far/ppermute | solution.py:33
  63.8 2.5 %collective-permute-start.17 = (bf16[256,640]{1,0:T(8,128)(2,1)S(1)}, bf16[256,640]{1,0:T(8,128)(2,1)S(1)}, u32[]{:S(2)}, u32[]{:S(2)}) collective-permute-start(bf16[256,640]{1,0:T(8,128)(2,1)S(1)} %get-tuple-element.46), channel_id=1, source_target_pairs={{0,32},{1,33},{2,34},{3,35},{4,36},{5,37},{6,38},{7,39},{8,40},{9,... | collective-permute-start | bytes 983048 | tf_op jit(solution)/shard_map/merge_own/ppermute | solution.py:33
  67.4 7.6 %collective-permute-start.18 = (bf16[64,512]{1,0:T(8,128)(2,1)S(1)}, bf16[64,512]{1,0:T(8,128)(2,1)S(1)}, u32[]{:S(2)}, u32[]{:S(2)}) collective-permute-start(bf16[64,512]{1,0:T(8,128)(2,1)S(1)} %get-tuple-element.48), channel_id=1, source_target_pairs={{0,64},{1,65},{2,66},{3,67},{4,68},{5,69},{6,70},{7,71},{8,72},{9,... | collective-permute-start | bytes 196616 | tf_op jit(solution)/shard_map/out_heads/ppermute | solution.py:33
  68.9 8.8 %collective-permute-start.19 = (bf16[64,512]{1,0:T(8,128)(2,1)S(1)}, bf16[64,512]{1,0:T(8,128)(2,1)S(1)}, u32[]{:S(2)}, u32[]{:S(2)}) collective-permute-start(bf16[64,512]{1,0:T(8,128)(2,1)S(1)} %get-tuple-element.49), channel_id=1, source_target_pairs={{0,128},{1,129},{2,130},{3,131},{4,132},{5,133},{6,134},{7,135},{8... | collective-permute-start | bytes 196616 | tf_op jit(solution)/shard_map/out_heads/ppermute | solution.py:33
  72.9 7.4 %collective-permute-start.20 = (bf16[64,512]{1,0:T(8,128)(2,1)S(1)}, bf16[64,512]{1,0:T(8,128)(2,1)S(1)}, u32[]{:S(2)}, u32[]{:S(2)}) collective-permute-start(bf16[64,512]{1,0:T(8,128)(2,1)S(1)} %get-tuple-element.50), channel_id=1, source_target_pairs={{0,192},{1,193},{2,194},{3,195},{4,196},{5,197},{6,198},{7,199},{8... | collective-permute-start | bytes 196616 | tf_op jit(solution)/shard_map/out_heads/ppermute | solution.py:33

commit v5 on v4

--- a/solution.py
+++ b/solution.py
@@ -128,9 +128,10 @@
 
 
 def over_z(arrays):
-    return [
-        send(a, lambda zl, x, y, z, c, s=s: (zl, x, y, z + s, c)) for s, a in enumerate(arrays, 1)
-    ]
+    got = {}
+    for s in (2, 1, 3):
+        got[s] = send(arrays[s - 1], lambda zl, x, y, z, c, s=s: (zl, x, y, z + s, c))
+    return [got[s] for s in (1, 2, 3)]
 
 
 CALLS = ((1, 0, 12, 1, False), (1, 12, 4, 1, True), (0, 0, 16, 24, False))

time: 81.8 us -> 84.8 us (1.037)
  Pallas kernels: 21.5 us -> 27.1 us
  waiting for transfers between devices: 22.7 us -> 20.2 us
    pallas_call x3, Pallas kernels: 14.3 us -> 19.8 us  [flash(): pl.pallas_call(functools.partial(flash_kernel, rows, call, carry, final),...]
    ppermute x21, waiting for transfers between devices: 22.7 us -> 20.2 us  [send(): return lax.ppermute(a, AXES, pairs)]
  transfers between devices with their start and end apart: 21 -> 21, of which waited for: 12 -> 12; matrix products, arithmetic and copies ran while one was open for 0% -> 0% of each run, Pallas kernels for 18% -> 22%
where the time goes in v5:
time: 84.8 us; the launch traced here: 84.4 us
  starting transfers between devices  36.9 us (44%)
  Pallas kernels  27.1 us (32%)
  waiting for transfers between devices  20.2 us (24%)
    ppermute x21, starting transfers between devices, send(): return lax.ppermute(a, AXES, pairs)  36.9 us
    ppermute x21, waiting for transfers between devices, send(): return lax.ppermute(a, AXES, pairs)  20.2 us
    pallas_call x3, Pallas kernels, flash(): pl.pallas_call(functools.partial(flash_kernel, rows, call, carry, final),...  19.8 us
    pallas_call x1, Pallas kernels, make_plan(): pl.pallas_call(plan_kernel, out_shape=jax.ShapeDtypeStruct((EDGE_AT + 3,)...  2.88 us
    pallas_call x1, Pallas kernels, pack(): pl.pallas_call(pack_kernel, out_shape=[jax.ShapeDtypeStruct((64, width),...  1.83 us
    pallas_call x2, Pallas kernels, merge(): pl.pallas_call(functools.partial(merge_kernel, len(partials)), out_shape=...  1.74 us
  transfers between devices with their start and end apart: 21, of which 12 were waited for; matrix products, arithmetic and copies ran while one was open for 0% of the time, Pallas kernels for 22%

profile of v5, /device:TPU:1, one launch (start us, length us, event | category | flops | bytes accessed | tf_op | source)
XLA Modules:
  0.0 84.4 jit_solution(11161249967112106102)
XLA Ops:
  0.0 1.8 %pack.1 = (bf16[64,768]{1,0:T(8,128)(2,1)}, bf16[64,768]{1,0:T(8,128)(2,1)}, bf16[64,768]{1,0:T(8,128)(2,1)}) custom-call(bf16[64,512]{1,0:T(8,128)(2,1)} %bitcast.6, bf16[64,512]{1,0:T(8,128)(2,1)} %bitcast.8, bf16[64,2048]{1,0:T(8,128)(2,1)} %bitcast.4), custom_call_target="tpu_custom_call" | custom-call | tf_op jit(solution)/shard_map/heads/pack/pallas_call | solution.py:75
  1.9 3.9 %collective-permute-start = (bf16[64,768]{1,0:T(8,128)(2,1)}, bf16[64,768]{1,0:T(8,128)(2,1)S(1)}, u32[]{:S(2)}, u32[]{:S(2)}) collective-permute-start(bf16[64,768]{1,0:T(8,128)(2,1)} %get-tuple-element.28), channel_id=1, source_target_pairs={{0,64},{1,65},{2,66},{3,67},{4,68},{5,69},{6,70},{7,71},{8,72},{9,... | collective-permute-start | bytes 294920 | tf_op jit(solution)/shard_map/heads/ppermute | solution.py:33
  5.8 5.1 %collective-permute-start.1 = (bf16[64,768]{1,0:T(8,128)(2,1)}, bf16[64,768]{1,0:T(8,128)(2,1)S(1)}, u32[]{:S(2)}, u32[]{:S(2)}) collective-permute-start(bf16[64,768]{1,0:T(8,128)(2,1)} %get-tuple-element.29), channel_id=1, source_target_pairs={{0,128},{1,129},{2,130},{3,131},{4,132},{5,133},{6,134},{7,135},{8... | collective-permute-start | bytes 294920 | tf_op jit(solution)/shard_map/heads/ppermute | solution.py:33
  10.9 2.4 %collective-permute-start.2 = (bf16[64,768]{1,0:T(8,128)(2,1)}, bf16[64,768]{1,0:T(8,128)(2,1)S(1)}, u32[]{:S(2)}, u32[]{:S(2)}) collective-permute-start(bf16[64,768]{1,0:T(8,128)(2,1)} %get-tuple-element.30), channel_id=1, source_target_pairs={{0,192},{1,193},{2,194},{3,195},{4,196},{5,197},{6,198},{7,199},{8... | collective-permute-start | bytes 294920 | tf_op jit(solution)/shard_map/heads/ppermute | solution.py:33
  13.3 2.9 %plan.1.refs_0_ = s32[440]{0:T(512)S(1)} custom-call(s32[32,512]{1,0:T(8,128)S(1)} %copy-done.3, s32[32,512]{1,0:T(8,128)S(1)} %copy-done.4), custom_call_target="tpu_custom_call" | custom-call | tf_op jit(solution)/shard_map/heads/plan/pallas_call | solution.py:209
  16.1 0.0 collective-permute-done.refs_3_
  16.2 1.1 %collective-permute-done.1.refs_4_ = bf16[64,768]{1,0:T(8,128)(2,1)S(1)} collective-permute-done((bf16[64,768]{1,0:T(8,128)(2,1)}, bf16[64,768]{1,0:T(8,128)(2,1)S(1)}, u32[]{:S(2)}, u32[]{:S(2)}) %collective-permute-start.1) | collective-permute-done | bytes 98336 | tf_op jit(solution)/shard_map/heads/ppermute | solution.py:33
  17.3 3.9 %collective-permute-done.2.refs_5_ = bf16[64,768]{1,0:T(8,128)(2,1)S(1)} collective-permute-done((bf16[64,768]{1,0:T(8,128)(2,1)}, bf16[64,768]{1,0:T(8,128)(2,1)S(1)}, u32[]{:S(2)}, u32[]{:S(2)}) %collective-permute-start.2) | collective-permute-done | bytes 98336 | tf_op jit(solution)/shard_map/heads/ppermute | solution.py:33
  21.2 0.1 unpack.1
  21.3 2.8 %collective-permute-start.3 = (bf16[256,256]{1,0:T(8,128)(2,1)S(1)}, bf16[256,256]{1,0:T(8,128)(2,1)S(1)}, u32[]{:S(2)}, u32[]{:S(2)}) collective-permute-start(bf16[256,256]{1,0:T(8,128)(2,1)S(1)} %get-tuple-element.34), channel_id=1, source_target_pairs={{0,12},{1,13},{2,14},{3,15},{4,0},{5,1},{6,2},{7,3},{8,4},{9,5},{1... | collective-permute-start | bytes 393224 | tf_op jit(solution)/shard_map/kv_first/ppermute | solution.py:33
  24.1 0.3 collective-permute-start.4
  24.5 0.8 collective-permute-start.8
  25.2 0.0 collective-permute-start.6
  25.2 2.2 %collective-permute-done.3 = bf16[256,256]{1,0:T(8,128)(2,1)S(1)} collective-permute-done((bf16[256,256]{1,0:T(8,128)(2,1)S(1)}, bf16[256,256]{1,0:T(8,128)(2,1)S(1)}, u32[]{:S(2)}, u32[]{:S(2)}) %collective-permute-start.3) | collective-permute-done | bytes 131104 | tf_op jit(solution)/shard_map/kv_first/ppermute | solution.py:33
  27.4 2.3 %collective-permute-done.4 = bf16[256,256]{1,0:T(8,128)(2,1)S(1)} collective-permute-done((bf16[256,256]{1,0:T(8,128)(2,1)S(1)}, bf16[256,256]{1,0:T(8,128)(2,1)S(1)}, u32[]{:S(2)}, u32[]{:S(2)}) %collective-permute-start.4) | collective-permute-done | bytes 131104 | tf_op jit(solution)/shard_map/kv_first/ppermute | solution.py:33
  29.7 1.1 %collective-permute-start.5 = (bf16[512,256]{1,0:T(8,128)(2,1)S(1)}, bf16[512,256]{1,0:T(8,128)(2,1)S(1)}, u32[]{:S(2)}, u32[]{:S(2)}) collective-permute-start(bf16[512,256]{1,0:T(8,128)(2,1)S(1)} %constant_dynamic-update-slice_fusion.refs_4_), channel_id=1, source_target_pairs={{0,1},{1,2},{2,3},{3,0},{4,5},{5,6},{6,7},{7,4},{8,9},{9,10},{10,1... | collective-permute-start | bytes 786440 | tf_op jit(solution)/shard_map/kv_second/ppermute | solution.py:33
  30.8 0.3 collective-permute-done.8
  31.1 1.0 %collective-permute-start.9 = (bf16[512,256]{1,0:T(8,128)(2,1)S(1)}, bf16[512,256]{1,0:T(8,128)(2,1)S(1)}, u32[]{:S(2)}, u32[]{:S(2)}) collective-permute-start(bf16[512,256]{1,0:T(8,128)(2,1)S(1)} %constant_dynamic-update-slice_fusion.2.refs_3_), channel_id=1, source_target_pairs={{0,1},{1,2},{2,3},{3,0},{4,5},{5,6},{6,7},{7,4},{8,9},{9,10},{10,1... | collective-permute-start | bytes 786440 | tf_op jit(solution)/shard_map/kv_second/ppermute | solution.py:33
  32.1 1.8 %collective-permute-start.11 = (bf16[512,256]{1,0:T(8,128)(2,1)S(1)}, bf16[512,256]{1,0:T(8,128)(2,1)S(1)}, u32[]{:S(2)}, u32[]{:S(2)}) collective-permute-start(bf16[512,256]{1,0:T(8,128)(2,1)S(1)} %constant_dynamic-update-slice_fusion.refs_4_), channel_id=1, source_target_pairs={{0,3},{1,0},{2,1},{3,2},{4,7},{5,4},{6,5},{7,6},{8,11},{9,8},{10,9... | collective-permute-start | bytes 786440 | tf_op jit(solution)/shard_map/kv_second/ppermute | solution.py:33
  33.9 1.0 %collective-permute-start.13 = (bf16[512,256]{1,0:T(8,128)(2,1)S(1)}, bf16[512,256]{1,0:T(8,128)(2,1)S(1)}, u32[]{:S(2)}, u32[]{:S(2)}) collective-permute-start(bf16[512,256]{1,0:T(8,128)(2,1)S(1)} %constant_dynamic-update-slice_fusion.2.refs_3_), channel_id=1, source_target_pairs={{0,3},{1,0},{2,1},{3,2},{4,7},{5,4},{6,5},{7,6},{8,11},{9,8},{10,9... | collective-permute-start | bytes 786440 | tf_op jit(solution)/shard_map/kv_second/ppermute | solution.py:33
  34.9 0.0 collective-permute-done.6.refs_1_
  34.9 1.7 %collective-permute-done.5.refs_6_ = bf16[512,256]{1,0:T(8,128)(2,1)S(1)} collective-permute-done((bf16[512,256]{1,0:T(8,128)(2,1)S(1)}, bf16[512,256]{1,0:T(8,128)(2,1)S(1)}, u32[]{:S(2)}, u32[]{:S(2)}) %collective-permute-start.5) | collective-permute-done | bytes 262176 | tf_op jit(solution)/shard_map/kv_second/ppermute | solution.py:33
  36.5 2.3 %collective-permute-start.7 = (bf16[256,512]{1,0:T(8,128)(2,1)S(1)}, bf16[256,512]{1,0:T(8,128)(2,1)S(1)}, u32[]{:S(2)}, u32[]{:S(2)}) collective-permute-start(bf16[256,512]{1,0:T(8,128)(2,1)S(1)} %collective-permute-done.6.refs_1_), channel_id=1, source_target_pairs={{0,32},{1,33},{2,34},{3,35},{4,36},{5,37},{6,38},{7,39},{8,40},{9,... | collective-permute-start | bytes 786440 | tf_op jit(solution)/shard_map/q_other/ppermute | solution.py:33
  38.8 0.5 collective-permute-done.9.refs_5_
  39.3 0.0 collective-permute-start.10
  39.3 0.0 collective-permute-done.11.refs_8_
  39.3 2.7 %collective-permute-start.12 = (bf16[512,256]{1,0:T(8,128)(2,1)S(1)}, bf16[512,256]{1,0:T(8,128)(2,1)S(1)}, u32[]{:S(2)}, u32[]{:S(2)}) collective-permute-start(bf16[512,256]{1,0:T(8,128)(2,1)S(1)} %collective-permute-done.11.refs_8_), channel_id=1, source_target_pairs={{0,3},{1,0},{2,1},{3,2},{4,7},{5,4},{6,5},{7,6},{8,11},{9,8},{10,9... | collective-permute-start | bytes 786440 | tf_op jit(solution)/shard_map/kv_second/ppermute | solution.py:33
  42.0 0.0 collective-permute-done.13.refs_7_
  42.0 6.6 %flash.3 = (f32[8,256,128]{2,1,0:T(8,128)S(1)}, f32[2,256,128]{2,1,0:T(8,128)S(1)}) custom-call(s32[440]{0:T(512)S(1)} %plan.1.refs_0_, bf16[256,512]{1,0:T(8,128)(2,1)S(1)} %collective-permute-done.6.refs_1_, bf16[256,512]{1,0:T(8,128)(2,1)S(1)} %collective-permute-done.7.refs_2_, bf16[512,256]{1,0:T(8,128)(2,1)S(1)} %constant_dynamic-update-slice_fusion.2.refs_3_, ...), custom_call_target="tpu_custom_call" | custom-call | flops 805306368 | bytes 1572864 | tf_op jit(solution)/shard_map/attend_far/flash/pallas_call | solution.py:412
  48.6 0.0 collective-permute-done.12.refs_4_.refs_10_
  48.7 4.5 %flash.4 = (f32[256,640]{1,0:T(8,128)S(1)}, bf16[256,640]{1,0:T(8,128)(2,1)S(1)}) custom-call(s32[440]{0:T(512)S(1)} %plan.1.refs_0_, bf16[256,512]{1,0:T(8,128)(2,1)S(1)} %collective-permute-done.6.refs_1_, bf16[256,512]{1,0:T(8,128)(2,1)S(1)} %collective-permute-done.7.refs_2_, bf16[512,256]{1,0:T(8,128)(2,1)S(1)} %collective-permute-done.10.refs_3_.refs_9_, ...), custom_call_target="tpu_custom_call" | custom-call | flops 268435456 | bytes 524288 | tf_op jit(solution)/shard_map/attend_far/flash/pallas_call | solution.py:412
  53.2 2.6 %collective-permute-start.14 = (bf16[256,640]{1,0:T(8,128)(2,1)S(1)}, bf16[256,640]{1,0:T(8,128)(2,1)S(1)}, u32[]{:S(2)}, u32[]{:S(2)}) collective-permute-start(bf16[256,640]{1,0:T(8,128)(2,1)S(1)} %get-tuple-element.40), channel_id=1, source_target_pairs={{0,32},{1,33},{2,34},{3,35},{4,36},{5,37},{6,38},{7,39},{8,40},{9,... | collective-permute-start | bytes 983048 | tf_op jit(solution)/shard_map/merge_far/ppermute | solution.py:33
  55.8 0.1 collective-permute-start.15
  55.9 1.2 %collective-permute-done.14.refs_1_ = bf16[256,640]{1,0:T(8,128)(2,1)S(1)} collective-permute-done((bf16[256,640]{1,0:T(8,128)(2,1)S(1)}, bf16[256,640]{1,0:T(8,128)(2,1)S(1)}, u32[]{:S(2)}, u32[]{:S(2)}) %collective-permute-start.14) | collective-permute-done | bytes 327712 | tf_op jit(solution)/shard_map/merge_far/ppermute | solution.py:33
  57.0 0.6 merge.2
  57.7 0.3 collective-permute-start.16
  58.0 8.7 %flash.5 = (f32[256,640]{1,0:T(8,128)S(1)}, bf16[256,640]{1,0:T(8,128)(2,1)S(1)}) custom-call(s32[440]{0:T(512)S(1)} %plan.1.refs_0_, bf16[256,512]{1,0:T(8,128)(2,1)S(1)} %get-tuple-element.42.refs_1_, bf16[256,512]{1,0:T(8,128)(2,1)S(1)} %collective-permute-done.15.refs_2_, bf16[512,256]{1,0:T(8,128)(2,1)S(1)} %constant_dynamic-update-slice_fusion.2.refs_3_, ...), custom_call_target="tpu_custom_call" | custom-call | flops 25769803776 | bytes 2097152 | tf_op jit(solution)/shard_map/attend_own/flash/pallas_call | solution.py:412
  66.7 0.2 collective-permute-done.16.refs_2_
  66.9 1.2 %collective-permute-start.17 = (bf16[256,640]{1,0:T(8,128)(2,1)S(1)}, bf16[256,640]{1,0:T(8,128)(2,1)S(1)}, u32[]{:S(2)}, u32[]{:S(2)}) collective-permute-start(bf16[256,640]{1,0:T(8,128)(2,1)S(1)} %get-tuple-element.46), channel_id=1, source_target_pairs={{0,32},{1,33},{2,34},{3,35},{4,36},{5,37},{6,38},{7,39},{8,40},{9,... | collective-permute-start | bytes 983048 | tf_op jit(solution)/shard_map/merge_own/ppermute | solution.py:33
  68.1 1.3 %collective-permute-done.17.refs_1_ = bf16[256,640]{1,0:T(8,128)(2,1)S(1)} collective-permute-done((bf16[256,640]{1,0:T(8,128)(2,1)S(1)}, bf16[256,640]{1,0:T(8,128)(2,1)S(1)}, u32[]{:S(2)}, u32[]{:S(2)}) %collective-permute-start.17) | collective-permute-done | bytes 327712 | tf_op jit(solution)/shard_map/merge_own/ppermute | solution.py:33
  69.4 1.1 %merge.3 = (bf16[64,512]{1,0:T(8,128)(2,1)S(1)}, bf16[64,512]{1,0:T(8,128)(2,1)S(1)}, bf16[64,512]{1,0:T(8,128)(2,1)S(1)}, bf16[64,512]{1,0:T(8,128)(2,1)S(1)}) custom-call(f32[256,640]{1,0:T(8,128)S(1)} %get-tuple-element.44.refs_0_, bf16[256,640]{1,0:T(8,128)(2,1)S(1)} %collective-permute-done.17.refs_1_, bf16[256,640]{1,0:T(8,128)(2,1)S(1)} %collective-permute-done.16.refs_2_), custom_call_target="tpu_custom_call" | custom-call | tf_op jit(solution)/shard_map/merge_own/merge/pallas_call | solution.py:467
  70.5 1.4 %collective-permute-start.18 = (bf16[64,512]{1,0:T(8,128)(2,1)S(1)}, bf16[64,512]{1,0:T(8,128)(2,1)S(1)}, u32[]{:S(2)}, u32[]{:S(2)}) collective-permute-start(bf16[64,512]{1,0:T(8,128)(2,1)S(1)} %get-tuple-element.48), channel_id=1, source_target_pairs={{0,64},{1,65},{2,66},{3,67},{4,68},{5,69},{6,70},{7,71},{8,72},{9,... | collective-permute-start | bytes 196616 | tf_op jit(solution)/shard_map/out_heads/ppermute | solution.py:33
  71.9 4.1 %collective-permute-start.19 = (bf16[64,512]{1,0:T(8,128)(2,1)S(1)}, bf16[64,512]{1,0:T(8,128)(2,1)S(1)}, u32[]{:S(2)}, u32[]{:S(2)}) collective-permute-start(bf16[64,512]{1,0:T(8,128)(2,1)S(1)} %get-tuple-element.49), channel_id=1, source_target_pairs={{0,128},{1,129},{2,130},{3,131},{4,132},{5,133},{6,134},{7,135},{8... | collective-permute-start | bytes 196616 | tf_op jit(solution)/shard_map/out_heads/ppermute | solution.py:33
  75.9 2.1 %collective-permute-start.20 = (bf16[64,512]{1,0:T(8,128)(2,1)S(1)}, bf16[64,512]{1,0:T(8,128)(2,1)S(1)}, u32[]{:S(2)}, u32[]{:S(2)}) collective-permute-start(bf16[64,512]{1,0:T(8,128)(2,1)S(1)} %get-tuple-element.50), channel_id=1, source_target_pairs={{0,192},{1,193},{2,194},{3,195},{4,196},{5,197},{6,198},{7,199},{8... | collective-permute-start | bytes 196616 | tf_op jit(solution)/shard_map/out_heads/ppermute | solution.py:33
  78.1 0.0 collective-permute-done.18.refs_1_
  78.1 3.5 %collective-permute-done.19.refs_2_ = bf16[64,512]{1,0:T(8,128)(2,1)S(1)} collective-permute-done((bf16[64,512]{1,0:T(8,128)(2,1)S(1)}, bf16[64,512]{1,0:T(8,128)(2,1)S(1)}, u32[]{:S(2)}, u32[]{:S(2)}) %collective-permute-start.19) | collective-permute-done | bytes 65568 | tf_op jit(solution)/shard_map/out_heads/ppermute | solution.py:33
  81.6 2.1 %collective-permute-done.20.refs_3_ = bf16[64,512]{1,0:T(8,128)(2,1)S(1)} collective-permute-done((bf16[64,512]{1,0:T(8,128)(2,1)S(1)}, bf16[64,512]{1,0:T(8,128)(2,1)S(1)}, u32[]{:S(2)}, u32[]{:S(2)}) %collective-permute-start.20) | collective-permute-done | bytes 65568 | tf_op jit(solution)/shard_map/out_heads/ppermute | solution.py:33
  83.7 0.7 finish.1
  (17 shorter events, 0.1 us)
Async XLA Ops:
  0.0 13.3 %copy-start.3 = (s32[32,512]{1,0:T(8,128)S(1)}, s32[32,512]{1,0:T(8,128)}, u32[]{:S(2)}) copy-start(s32[32,512]{1,0:T(8,128)} %pos_hbm.1) | copy-start | bytes 196612
  0.0 13.3 %copy-start.4 = (s32[32,512]{1,0:T(8,128)S(1)}, s32[32,512]{1,0:T(8,128)}, u32[]{:S(2)}) copy-start(s32[32,512]{1,0:T(8,128)} %seg_hbm.1) | copy-start | bytes 196612
  0.0 21.2 %copy-start = (bf16[1,64,2048]{2,1,0:T(8,128)(2,1)S(1)}, bf16[1,64,2048]{2,1,0:T(8,128)(2,1)}, u32[]{:S(2)}) copy-start(bf16[1,64,2048]{2,1,0:T(8,128)(2,1)} %param.5) | copy-start | bytes 786436
  1.9 14.3 %collective-permute-start = (bf16[64,768]{1,0:T(8,128)(2,1)}, bf16[64,768]{1,0:T(8,128)(2,1)S(1)}, u32[]{:S(2)}, u32[]{:S(2)}) collective-permute-start(bf16[64,768]{1,0:T(8,128)(2,1)} %get-tuple-element.28), channel_id=1, source_target_pairs={{0,64},{1,65},{2,66},{3,67},{4,68},{5,69},{6,70},{7,71},{8,72},{9,... | collective-permute-start | bytes 294920 | tf_op jit(solution)/shard_map/heads/ppermute | solution.py:33
  5.8 11.5 %collective-permute-start.1 = (bf16[64,768]{1,0:T(8,128)(2,1)}, bf16[64,768]{1,0:T(8,128)(2,1)S(1)}, u32[]{:S(2)}, u32[]{:S(2)}) collective-permute-start(bf16[64,768]{1,0:T(8,128)(2,1)} %get-tuple-element.29), channel_id=1, source_target_pairs={{0,128},{1,129},{2,130},{3,131},{4,132},{5,133},{6,134},{7,135},{8... | collective-permute-start | bytes 294920 | tf_op jit(solution)/shard_map/heads/ppermute | solution.py:33
  10.9 10.3 %copy-start.1 = (bf16[1,64,512]{2,1,0:T(8,128)(2,1)S(1)}, bf16[1,64,512]{2,1,0:T(8,128)(2,1)}, u32[]{:S(2)}) copy-start(bf16[1,64,512]{2,1,0:T(8,128)(2,1)} %param.6) | copy-start | bytes 196612
  10.9 10.3 %copy-start.2 = (bf16[1,64,512]{2,1,0:T(8,128)(2,1)S(1)}, bf16[1,64,512]{2,1,0:T(8,128)(2,1)}, u32[]{:S(2)}) copy-start(bf16[1,64,512]{2,1,0:T(8,128)(2,1)} %param.7) | copy-start | bytes 196612
  10.9 10.3 %collective-permute-start.2 = (bf16[64,768]{1,0:T(8,128)(2,1)}, bf16[64,768]{1,0:T(8,128)(2,1)S(1)}, u32[]{:S(2)}, u32[]{:S(2)}) collective-permute-start(bf16[64,768]{1,0:T(8,128)(2,1)} %get-tuple-element.30), channel_id=1, source_target_pairs={{0,192},{1,193},{2,194},{3,195},{4,196},{5,197},{6,198},{7,199},{8... | collective-permute-start | bytes 294920 | tf_op jit(solution)/shard_map/heads/ppermute | solution.py:33
  21.3 6.1 %collective-permute-start.3 = (bf16[256,256]{1,0:T(8,128)(2,1)S(1)}, bf16[256,256]{1,0:T(8,128)(2,1)S(1)}, u32[]{:S(2)}, u32[]{:S(2)}) collective-permute-start(bf16[256,256]{1,0:T(8,128)(2,1)S(1)} %get-tuple-element.34), channel_id=1, source_target_pairs={{0,12},{1,13},{2,14},{3,15},{4,0},{5,1},{6,2},{7,3},{8,4},{9,5},{1... | collective-permute-start | bytes 393224 | tf_op jit(solution)/shard_map/kv_first/ppermute | solution.py:33
  24.1 5.6 %collective-permute-start.4 = (bf16[256,256]{1,0:T(8,128)(2,1)S(1)}, bf16[256,256]{1,0:T(8,128)(2,1)S(1)}, u32[]{:S(2)}, u32[]{:S(2)}) collective-permute-start(bf16[256,256]{1,0:T(8,128)(2,1)S(1)} %get-tuple-element.34), channel_id=1, source_target_pairs={{0,8},{1,9},{2,10},{3,11},{4,12},{5,13},{6,14},{7,15},{8,0},{9,1},... | collective-permute-start | bytes 393224 | tf_op jit(solution)/shard_map/kv_first/ppermute | solution.py:33
  24.5 6.7 %collective-permute-start.8 = (bf16[256,256]{1,0:T(8,128)(2,1)S(1)}, bf16[256,256]{1,0:T(8,128)(2,1)S(1)}, u32[]{:S(2)}, u32[]{:S(2)}) collective-permute-start(bf16[256,256]{1,0:T(8,128)(2,1)S(1)} %get-tuple-element.34), channel_id=1, source_target_pairs={{0,4},{1,5},{2,6},{3,7},{4,8},{5,9},{6,10},{7,11},{8,12},{9,13},{1... | collective-permute-start | bytes 393224 | tf_op jit(solution)/shard_map/kv_first/ppermute | solution.py:33
  25.2 9.6 %collective-permute-start.6 = (bf16[256,512]{1,0:T(8,128)(2,1)S(1)}, bf16[256,512]{1,0:T(8,128)(2,1)S(1)}, u32[]{:S(2)}, u32[]{:S(2)}) collective-permute-start(bf16[256,512]{1,0:T(8,128)(2,1)S(1)} %get-tuple-element.42.refs_1_), channel_id=1, source_target_pairs={{0,16},{1,17},{2,18},{3,19},{4,20},{5,21},{6,22},{7,23},{8,24},{9,... | collective-permute-start | bytes 786440 | tf_op jit(solution)/shard_map/q_other/ppermute | solution.py:33
  29.7 6.8 %collective-permute-start.5 = (bf16[512,256]{1,0:T(8,128)(2,1)S(1)}, bf16[512,256]{1,0:T(8,128)(2,1)S(1)}, u32[]{:S(2)}, u32[]{:S(2)}) collective-permute-start(bf16[512,256]{1,0:T(8,128)(2,1)S(1)} %constant_dynamic-update-slice_fusion.refs_4_), channel_id=1, source_target_pairs={{0,1},{1,2},{2,3},{3,0},{4,5},{5,6},{6,7},{7,4},{8,9},{9,10},{10,1... | collective-permute-start | bytes 786440 | tf_op jit(solution)/shard_map/kv_second/ppermute | solution.py:33
  31.1 8.2 %collective-permute-start.9 = (bf16[512,256]{1,0:T(8,128)(2,1)S(1)}, bf16[512,256]{1,0:T(8,128)(2,1)S(1)}, u32[]{:S(2)}, u32[]{:S(2)}) collective-permute-start(bf16[512,256]{1,0:T(8,128)(2,1)S(1)} %constant_dynamic-update-slice_fusion.2.refs_3_), channel_id=1, source_target_pairs={{0,1},{1,2},{2,3},{3,0},{4,5},{5,6},{6,7},{7,4},{8,9},{9,10},{10,1... | collective-permute-start | bytes 786440 | tf_op jit(solution)/shard_map/kv_second/ppermute | solution.py:33
  32.1 7.2 %collective-permute-start.11 = (bf16[512,256]{1,0:T(8,128)(2,1)S(1)}, bf16[512,256]{1,0:T(8,128)(2,1)S(1)}, u32[]{:S(2)}, u32[]{:S(2)}) collective-permute-start(bf16[512,256]{1,0:T(8,128)(2,1)S(1)} %constant_dynamic-update-slice_fusion.refs_4_), channel_id=1, source_target_pairs={{0,3},{1,0},{2,1},{3,2},{4,7},{5,4},{6,5},{7,6},{8,11},{9,8},{10,9... | collective-permute-start | bytes 786440 | tf_op jit(solution)/shard_map/kv_second/ppermute | solution.py:33
  33.9 8.1 %collective-permute-start.13 = (bf16[512,256]{1,0:T(8,128)(2,1)S(1)}, bf16[512,256]{1,0:T(8,128)(2,1)S(1)}, u32[]{:S(2)}, u32[]{:S(2)}) collective-permute-start(bf16[512,256]{1,0:T(8,128)(2,1)S(1)} %constant_dynamic-update-slice_fusion.2.refs_3_), channel_id=1, source_target_pairs={{0,3},{1,0},{2,1},{3,2},{4,7},{5,4},{6,5},{7,6},{8,11},{9,8},{10,9... | collective-permute-start | bytes 786440 | tf_op jit(solution)/shard_map/kv_second/ppermute | solution.py:33
  36.5 5.5 %collective-permute-start.7 = (bf16[256,512]{1,0:T(8,128)(2,1)S(1)}, bf16[256,512]{1,0:T(8,128)(2,1)S(1)}, u32[]{:S(2)}, u32[]{:S(2)}) collective-permute-start(bf16[256,512]{1,0:T(8,128)(2,1)S(1)} %collective-permute-done.6.refs_1_), channel_id=1, source_target_pairs={{0,32},{1,33},{2,34},{3,35},{4,36},{5,37},{6,38},{7,39},{8,40},{9,... | collective-permute-start | bytes 786440 | tf_op jit(solution)/shard_map/q_other/ppermute | solution.py:33
  39.3 9.3 %collective-permute-start.10 = (bf16[512,256]{1,0:T(8,128)(2,1)S(1)}, bf16[512,256]{1,0:T(8,128)(2,1)S(1)}, u32[]{:S(2)}, u32[]{:S(2)}) collective-permute-start(bf16[512,256]{1,0:T(8,128)(2,1)S(1)} %collective-permute-done.9.refs_5_), channel_id=1, source_target_pairs={{0,1},{1,2},{2,3},{3,0},{4,5},{5,6},{6,7},{7,4},{8,9},{9,10},{10,1... | collective-permute-start | bytes 786440 | tf_op jit(solution)/shard_map/kv_second/ppermute | solution.py:33
  39.3 9.3 %collective-permute-start.12 = (bf16[512,256]{1,0:T(8,128)(2,1)S(1)}, bf16[512,256]{1,0:T(8,128)(2,1)S(1)}, u32[]{:S(2)}, u32[]{:S(2)}) collective-permute-start(bf16[512,256]{1,0:T(8,128)(2,1)S(1)} %collective-permute-done.11.refs_8_), channel_id=1, source_target_pairs={{0,3},{1,0},{2,1},{3,2},{4,7},{5,4},{6,5},{7,6},{8,11},{9,8},{10,9... | collective-permute-start | bytes 786440 | tf_op jit(solution)/shard_map/kv_second/ppermute | solution.py:33
  53.2 3.8 %collective-permute-start.14 = (bf16[256,640]{1,0:T(8,128)(2,1)S(1)}, bf16[256,640]{1,0:T(8,128)(2,1)S(1)}, u32[]{:S(2)}, u32[]{:S(2)}) collective-permute-start(bf16[256,640]{1,0:T(8,128)(2,1)S(1)} %get-tuple-element.40), channel_id=1, source_target_pairs={{0,32},{1,33},{2,34},{3,35},{4,36},{5,37},{6,38},{7,39},{8,40},{9,... | collective-permute-start | bytes 983048 | tf_op jit(solution)/shard_map/merge_far/ppermute | solution.py:33
  55.8 2.2 %collective-permute-start.15 = (bf16[256,512]{1,0:T(8,128)(2,1)S(1)}, bf16[256,512]{1,0:T(8,128)(2,1)S(1)}, u32[]{:S(2)}, u32[]{:S(2)}) collective-permute-start(bf16[256,512]{1,0:T(8,128)(2,1)S(1)} %get-tuple-element.42.refs_1_), channel_id=1, source_target_pairs={{0,32},{1,33},{2,34},{3,35},{4,36},{5,37},{6,38},{7,39},{8,40},{9,... | collective-permute-start | bytes 786440 | tf_op jit(solution)/shard_map/q_other/ppermute | solution.py:33
  57.7 9.2 %collective-permute-start.16 = (bf16[256,640]{1,0:T(8,128)(2,1)S(1)}, bf16[256,640]{1,0:T(8,128)(2,1)S(1)}, u32[]{:S(2)}, u32[]{:S(2)}) collective-permute-start(bf16[256,640]{1,0:T(8,128)(2,1)S(1)} %merge.2), channel_id=1, source_target_pairs={{0,16},{1,17},{2,18},{3,19},{4,20},{5,21},{6,22},{7,23},{8,24},{9,... | collective-permute-start | bytes 983048 | tf_op jit(solution)/shard_map/merge_far/ppermute | solution.py:33
  66.9 2.5 %collective-permute-start.17 = (bf16[256,640]{1,0:T(8,128)(2,1)S(1)}, bf16[256,640]{1,0:T(8,128)(2,1)S(1)}, u32[]{:S(2)}, u32[]{:S(2)}) collective-permute-start(bf16[256,640]{1,0:T(8,128)(2,1)S(1)} %get-tuple-element.46), channel_id=1, source_target_pairs={{0,32},{1,33},{2,34},{3,35},{4,36},{5,37},{6,38},{7,39},{8,40},{9,... | collective-permute-start | bytes 983048 | tf_op jit(solution)/shard_map/merge_own/ppermute | solution.py:33
  70.5 7.6 %collective-permute-start.18 = (bf16[64,512]{1,0:T(8,128)(2,1)S(1)}, bf16[64,512]{1,0:T(8,128)(2,1)S(1)}, u32[]{:S(2)}, u32[]{:S(2)}) collective-permute-start(bf16[64,512]{1,0:T(8,128)(2,1)S(1)} %get-tuple-element.48), channel_id=1, source_target_pairs={{0,64},{1,65},{2,66},{3,67},{4,68},{5,69},{6,70},{7,71},{8,72},{9,... | collective-permute-start | bytes 196616 | tf_op jit(solution)/shard_map/out_heads/ppermute | solution.py:33
  71.9 9.7 %collective-permute-start.19 = (bf16[64,512]{1,0:T(8,128)(2,1)S(1)}, bf16[64,512]{1,0:T(8,128)(2,1)S(1)}, u32[]{:S(2)}, u32[]{:S(2)}) collective-permute-start(bf16[64,512]{1,0:T(8,128)(2,1)S(1)} %get-tuple-element.49), channel_id=1, source_target_pairs={{0,128},{1,129},{2,130},{3,131},{4,132},{5,133},{6,134},{7,135},{8... | collective-permute-start | bytes 196616 | tf_op jit(solution)/shard_map/out_heads/ppermute | solution.py:33
  75.9 7.7 %collective-permute-start.20 = (bf16[64,512]{1,0:T(8,128)(2,1)S(1)}, bf16[64,512]{1,0:T(8,128)(2,1)S(1)}, u32[]{:S(2)}, u32[]{:S(2)}) collective-permute-start(bf16[64,512]{1,0:T(8,128)(2,1)S(1)} %get-tuple-element.50), channel_id=1, source_target_pairs={{0,192},{1,193},{2,194},{3,195},{4,196},{5,197},{6,198},{7,199},{8... | collective-permute-start | bytes 196616 | tf_op jit(solution)/shard_map/out_heads/ppermute | solution.py:33
